TPU v7x, 128 devices: a whole 4x4x4 slice. The times are simulated.
128 devices in a mesh: fsdp: 16 (over x, z), ctx: 8 (over y, core).
Axes of the slice: x: 4, y: 4, z: 4, core: 2. Of those that a mesh axis runs over, the one named last changes fastest.
Arguments:
- tokens: bfloat16 [16, 1024, 4096], P('fsdp', 'ctx'), may hold values from -6 to 6
- norm_gain: float32 [4096], replicated, may hold values from 0.5 to 1.5
- w_in: bfloat16 [4096, 3, 4096], P(None, None, 'fsdp'), may hold values from -0.09375 to 0.09375
- taps: float32 [3, 3, 4096], P(None, None, 'fsdp'), may hold values from -3 to 3
- decay_rate: float32 [16, 4096], P(None, 'fsdp'), may hold values from 0 to 0.0334, as said below
- residues: float32 [16, 4096], P(None, 'fsdp'), may hold values from -0.12 to 0.12
- skip_gain: float32 [4096], P('fsdp'), may hold values from -4 to 4
- w_out: bfloat16 [4096, 4096], P('fsdp'), may hold values from -0.09375 to 0.09375
Outputs:
- mixed: bfloat16 [16, 1024, 4096], P('fsdp', 'ctx')
Inputs may be any that keep to these rules, and one draw needn't show every extreme that they name: `decay_rate`: positive decay rates of the poles, at most 1/30.
All inputs are finite; a program needn't handle non-finite values.
Results may differ from a plain program's by a relative error of at most 0.024.
Values may be sent and summed in bfloat16 or wider, within the bound.
No kernel may reach another device: no remote copies, remote signals or barrier semaphores. Data moves between devices by JAX's collectives and lax.ppermute only.
A program may use at most 192 MiB of HBM per device.

v0:
```python
import jax
import jax.numpy as jnp
from jax import lax
from jax.sharding import PartitionSpec as P


def from_behind(value, axis, steps):
    count = lax.axis_size(axis)
    first, last = (max(0, -steps), min(count, count - steps))
    return lax.ppermute(value, axis, [(source, source + steps) for source in range(first, last)])


def shards(tokens, norm_gain, w_in, taps, decay_rate, residues, skip_gain, w_out):
    high = lax.Precision.HIGHEST
    values = tokens.astype(jnp.float32)
    inverse_rms = lax.rsqrt(jnp.mean(values * values, axis=-1, keepdims=True) + 1e-06)
    normed = (values * inverse_rms * norm_gain).astype(jnp.bfloat16)
    model_width = w_in.shape[0]
    channels = w_in.shape[2]
    w_flat = w_in.reshape(model_width, 3 * channels)
    features = jnp.einsum(
        "gtd,de->gte",
        lax.all_gather(normed, "fsdp", axis=0, tiled=True),
        w_flat,
        preferred_element_type=jnp.float32,
    ).astype(jnp.bfloat16)
    groups = features.shape[0]
    length = features.shape[1]
    edge_rows = from_behind(features[:, length - 2 :], "ctx", 1)
    extended = jnp.concatenate([edge_rows, features], axis=1).astype(jnp.float32)
    tap_rows = taps.reshape(taps.shape[0], 3 * channels)
    filtered = (
        tap_rows[0] * extended[:, 2:]
        + tap_rows[1] * extended[:, 1:-1]
        + tap_rows[2] * extended[:, :-2]
    )
    query_part = filtered[:, :, :channels]
    product = filtered[:, :, channels : 2 * channels] * filtered[:, :, 2 * channels :]
    offsets = jnp.arange(length, dtype=jnp.float32)
    powers = jnp.exp(-decay_rate[:, None, :] * offsets[None, :, None])
    kernel = jnp.sum(residues[:, None, :] * powers, axis=0)
    positions = jnp.arange(length, dtype=jnp.int32)
    lag_steps = positions[:, None] - positions[None, :]
    toeplitz = jnp.where(
        (lag_steps >= 0)[:, :, None], kernel[jnp.maximum(lag_steps, 0)], jnp.float32(0.0)
    )
    inside = jnp.einsum("tsc,gsc->gtc", toeplitz, product, precision=high)
    end_pow = jnp.exp(-decay_rate[:, None, :] * (length - 1 - offsets)[None, :, None])
    summary = jnp.einsum("nsc,gsc->gnc", end_pow, product, precision=high)
    decay_all = jnp.exp(-decay_rate * length)
    ctx_count = lax.axis_size("ctx")
    incoming = jnp.zeros_like(summary)
    for hop_step in range(ctx_count - 1):
        incoming = from_behind(
            (decay_all * incoming + summary).astype(jnp.bfloat16), "ctx", 1
        ).astype(jnp.float32)
    enter = residues[:, None, :] * jnp.exp(-decay_rate[:, None, :] * (offsets + 1.0)[None, :, None])
    entering = jnp.einsum("ntc,gnc->gtc", enter, incoming, precision=high)
    response = skip_gain * product + inside + entering
    gated = (query_part * response).astype(jnp.bfloat16).reshape(groups * length, channels)
    summed = lax.psum_scatter(
        jnp.dot(gated, w_out, preferred_element_type=jnp.float32).astype(jnp.bfloat16),
        "fsdp",
        scatter_dimension=0,
        tiled=True,
    ).astype(jnp.float32)
    return (values[0] + summed).astype(jnp.bfloat16)[None]


def solution(mesh):
    in_specs = (
        P("fsdp", "ctx", None),
        P(),
        P(None, None, "fsdp"),
        P(None, None, "fsdp"),
        P(None, "fsdp"),
        P(None, "fsdp"),
        P("fsdp"),
        P("fsdp", None),
    )
    out_specs = P("fsdp", "ctx", None)
    return jax.shard_map(shards, mesh=mesh, in_specs=in_specs, out_specs=out_specs, check_vma=False)
```

profile of v0, /device:TPU:6, one launch (start us, length us, event | category | flops | bytes accessed | tf_op | source)
XLA Modules:
  0.0 460.4 jit_solution(5377165375567006929)
XLA Ops:
  6.5 1.7 fusion.8
  8.2 2.5 fusion.10
  10.8 8.8 %copy.61 = bf16[4096,3,256]{0,2,1:T(8,128)(2,1)} copy(bf16[4096,3,256]{2,0,1:T(8,128)(2,1)} %param.10) | data formatting | bytes 12582912 | tf_op args[2]
  19.6 105.0 %all-gather.2.cloned.1.call-done = bf16[16,128,4096]{2,1,0:T(8,128)(2,1)} async-done(((bf16[1,128,4096]{2,1,0:T(8,128)(2,1)}), bf16[16,128,4096]{2,1,0:T(8,128)(2,1)}) %all-gather.2.cloned.1.call-update) | async-done | bytes 16777232 | tf_op jit(solution)/shard_map/all_gather | solution.py:23
  124.7 18.6 %convolution_convert_fusion.1 = bf16[16,128,768]{2,1,0:T(8,128)(2,1)S(1)} fusion(bf16[16,128,4096]{2,1,0:T(8,128)(2,1)} %all-gather.2.cloned.1.call-done, bf16[4096,768,1]{0,1,2:T(8,128)(2,1)} %bitcast.55), kind=kOutput, calls=%fused_computation.15 | convolution fusion | flops 12886474752 | bytes 26214400 | tf_op jit(solution)/shard_map/gtd,de->gte/dot_general | solution.py:21
  143.3 1.6 copy-done.3
  144.9 1.9 collective-permute-start
  147.6 2.6 maximum_convert_fusion
  150.1 1.9 fusion.4
  152.0 2.6 copy-done.1
  154.6 1.6 slice_multiply_fusion.3
  156.2 3.1 copy.67
  159.3 6.5 %fusion.16 = f32[256,16,16]{2,1,0:T(8,128)} fusion(f32[16,128,256]{1,0,2:T(8,128)} %copy.67, f32[128]{0:T(128)S(1)} %iota_subtract_fusion, f32[16,256]{0,1:T(8,128)S(1)} %copy.64), kind=kOutput, calls=%fused_computation.30 | convolution fusion | flops 101187584 | bytes 2376192 | tf_op jit(solution)/shard_map/nsc,gsc->gnc/dot_general | solution.py:49
  165.8 2.5 copy.70
  168.3 4.0 collective-permute-start.1
  173.3 5.2 %collective-permute-start.2 = (bf16[16,16,256]{2,1,0:T(8,128)(2,1)S(1)}, bf16[16,16,256]{2,1,0:T(8,128)(2,1)S(1)}, u32[]{:S(2)}, u32[]{:S(2)}) collective-permute-start(bf16[16,16,256]{2,1,0:T(8,128)(2,1)S(1)} %fusion.26), channel_id=1, source_target_pairs={{0,1},{1,2},{2,3},{3,4},{4,5},{5,6},{6,7},{8,9},{9,10},{10,11},{11... | collective-permute-start | bytes 393224 | tf_op jit(solution)/shard_map/ppermute | solution.py:10
  179.5 5.3 %collective-permute-start.3 = (bf16[16,16,256]{2,1,0:T(8,128)(2,1)S(1)}, bf16[16,16,256]{2,1,0:T(8,128)(2,1)S(1)}, u32[]{:S(2)}, u32[]{:S(2)}) collective-permute-start(bf16[16,16,256]{2,1,0:T(8,128)(2,1)S(1)} %fusion.27), channel_id=1, source_target_pairs={{0,1},{1,2},{2,3},{3,4},{4,5},{5,6},{6,7},{8,9},{9,10},{10,11},{11... | collective-permute-start | bytes 393224 | tf_op jit(solution)/shard_map/ppermute | solution.py:10
  185.8 5.3 %collective-permute-start.4 = (bf16[16,16,256]{2,1,0:T(8,128)(2,1)S(1)}, bf16[16,16,256]{2,1,0:T(8,128)(2,1)S(1)}, u32[]{:S(2)}, u32[]{:S(2)}) collective-permute-start(bf16[16,16,256]{2,1,0:T(8,128)(2,1)S(1)} %fusion.28), channel_id=1, source_target_pairs={{0,1},{1,2},{2,3},{3,4},{4,5},{5,6},{6,7},{8,9},{9,10},{10,11},{11... | collective-permute-start | bytes 393224 | tf_op jit(solution)/shard_map/ppermute | solution.py:10
  192.2 5.3 %collective-permute-start.5 = (bf16[16,16,256]{2,1,0:T(8,128)(2,1)S(1)}, bf16[16,16,256]{2,1,0:T(8,128)(2,1)S(1)}, u32[]{:S(2)}, u32[]{:S(2)}) collective-permute-start(bf16[16,16,256]{2,1,0:T(8,128)(2,1)S(1)} %fusion.29), channel_id=1, source_target_pairs={{0,1},{1,2},{2,3},{3,4},{4,5},{5,6},{6,7},{8,9},{9,10},{10,11},{11... | collective-permute-start | bytes 393224 | tf_op jit(solution)/shard_map/ppermute | solution.py:10
  197.5 1.7 multiply_reduce_fusion
  199.2 4.6 collective-permute-start.6
  203.9 61.7 %gather_fusion = f32[16384,256]{1,0:T(8,128)} fusion(f32[128,256]{1,0:T(8,128)S(1)} %copy.65, s32[16384]{0:T(1024)S(1)} %bitcast_clamp_fusion), kind=kCustom, calls=%fused_computation | custom fusion | bytes 33619968 | tf_op jit(solution)/shard_map/gather | solution.py:45
  265.7 18.0 %copy.66 = f32[128,128,256]{1,0,2:T(8,128)} copy(f32[128,128,256]{2,1,0:T(8,128)} %bitcast.54) | data formatting | bytes 33554432 | tf_op jit(solution)/shard_map/gather | solution.py:45
  283.8 4.6 collective-permute-start.7
  288.3 29.6 %fusion = f32[256,16,128]{2,1,0:T(8,128)} fusion(f32[16,128,256]{1,0,2:T(8,128)} %copy.67, f32[128,128,256]{1,0,2:T(8,128)} %copy.66, pred[128,128]{1,0:T(8,128)(4,1)S(1)} %subtract_compare_fusion), kind=kOutput, calls=%fused_computation.1 | convolution fusion | flops 809500672 | bytes 20987904 | tf_op jit(solution)/shard_map/tsc,gsc->gtc/dot_general | solution.py:47
  317.9 2.9 copy.68
  321.8 3.2 fusion.12
  325.0 2.9 copy.72
  327.9 5.1 %fusion.11 = bf16[16,128,256]{2,1,0:T(8,128)(2,1)S(1)} fusion(f32[16,128,768]{2,1,0:T(8,128)} %copy-done.1, f32[256,16,128]{0,2,1:T(8,128)} %copy.72, f32[256,16,128]{0,2,1:T(8,128)} %copy.68, f32[256]{0:T(256)S(1)} %copy-done.7), kind=kLoop, calls=%fused_computation.23 | loop fusion | flops 3145728 | bytes 11535360 | tf_op jit(solution)/shard_map/convert_element_type | solution.py:60
  333.0 8.1 %convolution_convert_fusion = bf16[2048,4096]{1,0:T(8,128)(2,1)} fusion(bf16[2048,256]{1,0:T(8,128)(2,1)S(1)} %bitcast.56, bf16[256,4096]{1,0:T(8,128)(2,1)S(1)} %copy-done), kind=kOutput, calls=%fused_computation.3 | convolution fusion | flops 4303355904 | bytes 19922944 | tf_op jit(solution)/shard_map/dot_general | solution.py:62
  341.1 110.0 %reduce-scatter.2.cloned.1.call-done = bf16[128,4096]{1,0:T(8,128)(2,1)} async-done(((bf16[2048,4096]{1,0:T(8,128)(2,1)}), bf16[128,4096]{1,0:T(8,128)(2,1)}) %reduce-scatter.2.cloned.1.call-update) | async-done | bytes 1048592 | tf_op jit(solution)/shard_map/reduce_scatter | solution.py:61
  451.1 2.4 fusion.19
  (48 shorter events, 6.0 us)
Async XLA Ops:
  6.5 326.5 %copy-start = (bf16[256,4096]{1,0:T(8,128)(2,1)S(1)}, bf16[256,4096]{1,0:T(8,128)(2,1)}, u32[]{:S(2)}) copy-start(bf16[256,4096]{1,0:T(8,128)(2,1)} %param.15) | copy-start | bytes 6291460
  6.5 118.1 %all-gather.2.cloned.1.call-start = ((), (), s32[]{:S(2)}) async-start(), calls=%async_computation.1 | async-start | bytes 17825792 | tf_op jit(solution)/shard_map/all_gather | solution.py:23
  10.8 8.8 %copy-start.6 = (f32[3,3,256]{2,1,0:T(4,128)S(1)}, f32[3,3,256]{2,1,0:T(4,128)}, u32[]{:S(2)}) copy-start(f32[3,3,256]{2,1,0:T(4,128)} %param.11) | copy-start | bytes 27652
  10.8 8.8 %copy-start.5 = (f32[16,256]{1,0:T(8,128)S(1)}, f32[16,256]{1,0:T(8,128)}, u32[]{:S(2)}) copy-start(f32[16,256]{1,0:T(8,128)} %param.12) | copy-start | bytes 49156
  10.8 440.3 %reduce-scatter.2.cloned.1.call-start = ((), (), s32[]{:S(2)}) async-start(), calls=%async_computation.2 | async-start | bytes 17825792 | tf_op jit(solution)/shard_map/reduce_scatter | solution.py:61
  143.2 1.6 copy-start.3
  144.9 2.6 collective-permute-start
  152.0 2.6 copy-start.1
  165.8 19.1 %copy-start.4 = (f32[16,256]{1,0:T(8,128)S(1)}, f32[16,256]{1,0:T(8,128)}, u32[]{:S(2)}) copy-start(f32[16,256]{1,0:T(8,128)} %param.13) | copy-start | bytes 49156
  168.3 4.9 %collective-permute-start.1 = (bf16[16,16,256]{2,1,0:T(8,128)(2,1)S(1)}, bf16[16,16,256]{2,1,0:T(8,128)(2,1)S(1)}, u32[]{:S(2)}, u32[]{:S(2)}) collective-permute-start(bf16[16,16,256]{2,1,0:T(8,128)(2,1)S(1)} %fusion.25), channel_id=1, source_target_pairs={{0,1},{1,2},{2,3},{3,4},{4,5},{5,6},{6,7},{8,9},{9,10},{10,11},{11... | collective-permute-start | bytes 393224 | tf_op jit(solution)/shard_map/ppermute | solution.py:10
  173.3 6.2 %collective-permute-start.2 = (bf16[16,16,256]{2,1,0:T(8,128)(2,1)S(1)}, bf16[16,16,256]{2,1,0:T(8,128)(2,1)S(1)}, u32[]{:S(2)}, u32[]{:S(2)}) collective-permute-start(bf16[16,16,256]{2,1,0:T(8,128)(2,1)S(1)} %fusion.26), channel_id=1, source_target_pairs={{0,1},{1,2},{2,3},{3,4},{4,5},{5,6},{6,7},{8,9},{9,10},{10,11},{11... | collective-permute-start | bytes 393224 | tf_op jit(solution)/shard_map/ppermute | solution.py:10
  179.5 6.3 %collective-permute-start.3 = (bf16[16,16,256]{2,1,0:T(8,128)(2,1)S(1)}, bf16[16,16,256]{2,1,0:T(8,128)(2,1)S(1)}, u32[]{:S(2)}, u32[]{:S(2)}) collective-permute-start(bf16[16,16,256]{2,1,0:T(8,128)(2,1)S(1)} %fusion.27), channel_id=1, source_target_pairs={{0,1},{1,2},{2,3},{3,4},{4,5},{5,6},{6,7},{8,9},{9,10},{10,11},{11... | collective-permute-start | bytes 393224 | tf_op jit(solution)/shard_map/ppermute | solution.py:10
  185.8 6.3 %collective-permute-start.4 = (bf16[16,16,256]{2,1,0:T(8,128)(2,1)S(1)}, bf16[16,16,256]{2,1,0:T(8,128)(2,1)S(1)}, u32[]{:S(2)}, u32[]{:S(2)}) collective-permute-start(bf16[16,16,256]{2,1,0:T(8,128)(2,1)S(1)} %fusion.28), channel_id=1, source_target_pairs={{0,1},{1,2},{2,3},{3,4},{4,5},{5,6},{6,7},{8,9},{9,10},{10,11},{11... | collective-permute-start | bytes 393224 | tf_op jit(solution)/shard_map/ppermute | solution.py:10
  192.2 7.0 %collective-permute-start.5 = (bf16[16,16,256]{2,1,0:T(8,128)(2,1)S(1)}, bf16[16,16,256]{2,1,0:T(8,128)(2,1)S(1)}, u32[]{:S(2)}, u32[]{:S(2)}) collective-permute-start(bf16[16,16,256]{2,1,0:T(8,128)(2,1)S(1)} %fusion.29), channel_id=1, source_target_pairs={{0,1},{1,2},{2,3},{3,4},{4,5},{5,6},{6,7},{8,9},{9,10},{10,11},{11... | collective-permute-start | bytes 393224 | tf_op jit(solution)/shard_map/ppermute | solution.py:10
  199.2 84.5 %collective-permute-start.6 = (bf16[16,16,256]{2,1,0:T(8,128)(2,1)S(1)}, bf16[16,16,256]{2,1,0:T(8,128)(2,1)S(1)}, u32[]{:S(2)}, u32[]{:S(2)}) collective-permute-start(bf16[16,16,256]{2,1,0:T(8,128)(2,1)S(1)} %fusion.30), channel_id=1, source_target_pairs={{0,1},{1,2},{2,3},{3,4},{4,5},{5,6},{6,7},{8,9},{9,10},{10,11},{11... | collective-permute-start | bytes 393224 | tf_op jit(solution)/shard_map/ppermute | solution.py:10
  283.8 37.1 %collective-permute-start.7 = (bf16[16,16,256]{2,1,0:T(8,128)(2,1)S(1)}, bf16[16,16,256]{2,1,0:T(8,128)(2,1)S(1)}, u32[]{:S(2)}, u32[]{:S(2)}) collective-permute-start(bf16[16,16,256]{2,1,0:T(8,128)(2,1)S(1)} %fusion.31), channel_id=1, source_target_pairs={{0,1},{1,2},{2,3},{3,4},{4,5},{5,6},{6,7},{8,9},{9,10},{10,11},{11... | collective-permute-start | bytes 393224 | tf_op jit(solution)/shard_map/ppermute | solution.py:10
  325.0 2.9 copy-start.7
  341.1 110.0 %copy-start.2 = (bf16[1,128,4096]{2,1,0:T(8,128)(2,1)S(1)}, bf16[1,128,4096]{2,1,0:T(8,128)(2,1)}, u32[]{:S(2)}) copy-start(bf16[1,128,4096]{2,1,0:T(8,128)(2,1)} %param.8) | copy-start | bytes 3145732
Sparse Core Ops, SparseCore 0:
  10.9 113.7 all-gather.1
  341.3 109.7 reduce-scatter.1
where the time goes:
time: 462 us; the launch traced here: 460 us
  waiting for transfers between devices  219 us (47%)
  local copies, waits for them, and re-layouts  106 us (23%)
  matrix products  65.9 us (14%)
  starting transfers between devices  36.3 us (8%)
  other arithmetic  19.7 us (4%)
  between operations  13.7 us (3%)
    reduce_scatter x1, waiting for transfers between devices, shards(): lax.psum_scatter(jnp.dot(gated, w_out, preferred_element_type=jnp.float32...  110 us
    all_gather x1, waiting for transfers between devices, shards(): lax.all_gather(normed, 'fsdp', axis=0, tiled=True)  105 us
    gather x2, local copies, waits for them, and re-layouts, shards(): kernel[jnp.maximum(lag_steps, 0)]  79.8 us
    ppermute x8, starting transfers between devices, from_behind(): lax.ppermute(value, axis, [(source, source + steps) for source in range(f...  36.2 us
    dot_general x1, matrix products, shards(): inside = jnp.einsum('tsc,gsc->gtc', toeplitz, product, precision=high)  29.6 us
    dot_general x1, matrix products, shards(): jnp.einsum('gtd,de->gte', lax.all_gather(normed, 'fsdp', axis=0, tiled=Tr...  18.6 us
    unnamed x18, local copies, waits for them, and re-layouts  13.1 us
  transfers between devices with their start and end apart: 10, of which 7 were waited for; matrix products, arithmetic and copies ran while one was open for 27% of the time, Pallas kernels for 0%

commit v1 on v0

v1 whole, which is shorter than its diff:
```python
import jax
import jax.numpy as jnp
from jax import lax
from jax.experimental import pallas as pl
from jax.experimental.pallas import tpu as pltpu
from jax.sharding import Mesh, PartitionSpec as P

F32 = jnp.float32
BF16 = jnp.bfloat16
OFFSETS = (0, 1, 3, 2)
CHUNK = 16
EDGE = 8


def from_ahead(value, axis, steps):
    count = lax.axis_size(axis)
    return lax.ppermute(value, axis, [(i, (i - steps) % count) for i in range(count)])


def from_behind(value, axis, steps):
    count = lax.axis_size(axis)
    return lax.ppermute(value, axis, [(i, i + steps) for i in range(count - steps)])


def compiler_params():
    return pltpu.CompilerParams(vmem_limit_bytes=44 * 1024 * 1024)


def project(x_ref, w_ref, scratch, seqs, length):
    pieces, depth, width = w_ref.shape
    total = jnp.dot(x_ref[:, :depth], w_ref[0], preferred_element_type=F32)
    for k in range(1, pieces):
        total += jnp.dot(x_ref[:, k * depth : (k + 1) * depth], w_ref[k], preferred_element_type=F32)
    total = total.astype(BF16).astype(F32)
    rows = seqs * length
    for lane in range(width // 128):
        cols = slice(lane * 128, (lane + 1) * 128)
        for s in range(seqs):
            scratch[lane, s, EDGE : EDGE + length, :] = total[s * length : (s + 1) * length, cols]
            scratch[lane, s, EDGE - 2 : EDGE, :] = total[rows + 2 * s : rows + 2 * s + 2, cols]


def wide(row):
    return jnp.broadcast_to(row, (8, 128))


def kv_kernel(order, x_ref, w_ref, taps_ref, kern_ref, pole_ref, jump_ref, y_ref, e_ref, t_ref, fk, fv):
    seqs = fk.shape[1]
    length = fk.shape[2] - EDGE
    project(x_ref, w_ref.at[0, :, 0], fk, seqs, length)
    project(x_ref, w_ref.at[0, :, 1], fv, seqs, length)
    first_row = lax.broadcasted_iota(jnp.int32, (8, 128), 0)

    def each(i, carry):
        lane, s = i // seqs, i % seqs
        tap = lambda j, stream: wide(taps_ref[0, lane, pl.ds(3 * j + stream, 1), :])
        kt = [tap(j, 1) for j in range(3)]
        vt = [tap(j, 2) for j in range(3)]
        kx = [fk[lane, s, pl.ds(EDGE + t, 8, stride=CHUNK), :] for t in range(-2, CHUNK)]
        vx = [fv[lane, s, pl.ds(EDGE + t, 8, stride=CHUNK), :] for t in range(-2, CHUNK)]
        xs = []
        for t in range(CHUNK):
            k = kt[0] * kx[t + 2] + kt[1] * kx[t + 1] + kt[2] * kx[t]
            v = vt[0] * vx[t + 2] + vt[1] * vx[t + 1] + vt[2] * vx[t]
            xs.append(k * v)
        kern = [wide(kern_ref[0, lane, pl.ds(d, 1), :]) for d in range(CHUNK)]
        for t in range(CHUNK):
            y = kern[0] * xs[t]
            for d in range(1, t + 1):
                y += kern[d] * xs[t - d]
            y_ref[0, lane, s, t] = y
        for n in range(16):
            pole = wide(pole_ref[0, lane, pl.ds(n, 1), :])
            state = xs[0]
            for t in range(1, CHUNK):
                state = pole * state + xs[t]
            for j, step in enumerate((1, 2, 4)):
                jump = wide(jump_ref[0, lane, j, pl.ds(n, 1), :])
                moved = jnp.where(first_row >= step, pltpu.roll(state, step, 0), 0.0)
                state = state + jump * moved
            e_ref[0, lane, s, n] = jnp.where(first_row >= 1, pltpu.roll(state, 1, 0), 0.0)
            t_ref[0, lane, s, pl.ds(n, 1), :] = state[7:8, :]
        return carry

    lax.fori_loop(0, seqs * fk.shape[0], each, 0)


def enter_kernel(y_ref, e_ref, in_ref, pole_ref, res_ref, ahead_ref, out_ref):
    lanes, seqs = y_ref.shape[1], y_ref.shape[2]

    def each(i, carry):
        lane, s = i // seqs, i % seqs
        poles, states = [], []
        for n in range(16):
            pole = wide(pole_ref[0, lane, pl.ds(n, 1), :])
            incoming = wide(in_ref[0, lane, s, pl.ds(n, 1), :])
            state = e_ref[0, lane, s, n] + ahead_ref[0, lane, n] * incoming
            poles.append(pole)
            states.append(wide(res_ref[0, lane, pl.ds(n, 1), :]) * pole * state)
        for t in range(CHUNK):
            total = y_ref[0, lane, s, t]
            for n in range(16):
                total += states[n]
            out_ref[0, lane, s, t] = total
            states = [pole * state for pole, state in zip(poles, states)]
        return carry

    lax.fori_loop(0, seqs * lanes, each, 0)


def q_kernel(order, x_ref, w_ref, taps_ref, y_ref, out_ref, fq, gated):
    lanes, seqs = fq.shape[:2]
    length = fq.shape[2] - EDGE
    project(x_ref, w_ref.at[0], fq, seqs, length)

    def each(i, carry):
        lane, s = i // seqs, i % seqs
        qt = [wide(taps_ref[0, lane, pl.ds(3 * j, 1), :]) for j in range(3)]
        qx = [fq[lane, s, pl.ds(EDGE + t, 8, stride=CHUNK), :] for t in range(-2, CHUNK)]
        for t in range(CHUNK):
            q = qt[0] * qx[t + 2] + qt[1] * qx[t + 1] + qt[2] * qx[t]
            gated[lane, s, pl.ds(t, 8, stride=CHUNK), :] = q * y_ref[0, lane, s, t]
        return carry

    lax.fori_loop(0, seqs * lanes, each, 0)
    for lane in range(lanes):
        for s in range(seqs):
            out_ref[0, s, :, lane * 128 : (lane + 1) * 128] = gated[lane, s].astype(BF16)


def out_kernel(order, g_ref, w_ref, *out_refs):
    blocks, seqs = g_ref.shape[:2]
    for s in range(seqs):
        total = jnp.dot(g_ref[0, s], w_ref[order[0]], preferred_element_type=F32)
        for r in range(1, blocks):
            total += jnp.dot(g_ref[r, s], w_ref[order[r]], preferred_element_type=F32)
        out_refs[s][...] = total.astype(BF16)


def shards(tokens, norm_gain, w_in, taps, decay_rate, residues, skip_gain, w_out):
    z = lax.axis_index("z")
    part = lax.axis_index("y") * 2 + lax.axis_index("c")
    order = jnp.stack([(z + step) % 4 for step in OFFSETS]).astype(jnp.int32)
    width, _, channels = w_in.shape
    length = tokens.shape[1]
    blocks = seqs = len(OFFSETS)
    lanes = channels // 128

    with jax.named_scope("weights"):
        w_streams = w_in.transpose(1, 0, 2)
        depth = width // 8
        kv_share = lax.dynamic_slice(w_streams, (1, part * depth, 0), (2, depth, channels))
        q_share = lax.dynamic_slice(w_streams, (0, part * depth, 0), (1, depth, channels))[0]
        out_share = lax.dynamic_slice(w_out, (part * (channels // 8), 0), (channels // 8, width))
        plane = ("z", "y", "c")
        w_kv = lax.all_gather(kv_share, plane, axis=0).reshape(blocks, 8, 2, depth, channels)
        q_share, w_kv = lax.optimization_barrier((q_share, w_kv))
        w_q = lax.all_gather(q_share, plane, axis=0).reshape(blocks, 8, depth, channels)
        out_share, w_q = lax.optimization_barrier((out_share, w_q))
        w_o = lax.all_gather(out_share, plane, axis=0).reshape(blocks, channels, width)

    with jax.named_scope("norm"):
        values = tokens[0].astype(F32)
        inverse_rms = lax.rsqrt(jnp.mean(values * values, axis=-1, keepdims=True) + 1e-06)
        normed = (values * inverse_rms * norm_gain).astype(BF16)

    with jax.named_scope("gather_tokens"):
        last = normed[length - 2 :]
        edges = []
        for step in OFFSETS:
            pairs = [
                (((x * 4 + y) * 2 + c), (((x - step) % 4 * 4) + (y * 2 + c + 1) // 2) * 2 + (c + 1) % 2)
                for x in range(4)
                for y in range(4)
                for c in range(2)
                if y * 2 + c < 7
            ]
            edges.append(lax.ppermute(last, ("x", "y", "c"), pairs))
        rows = [normed] + [from_ahead(normed, "x", step) for step in OFFSETS[1:]]
        tail = jnp.zeros((16 - 2 * seqs, width), BF16)
        x_all = jnp.concatenate(rows + edges + [tail], axis=0)

    with jax.named_scope("params"):
        packed = jnp.concatenate(
            [taps.reshape(9, channels), decay_rate, residues, skip_gain[None], jnp.zeros((6, channels), F32)], axis=0
        )
        packed = jnp.stack([packed] + [from_ahead(packed, "z", step) for step in OFFSETS[1:]])
        packed = packed.reshape(blocks, 48, lanes, 128).transpose(0, 2, 1, 3)
        taps_all, decay, res = packed[:, :, :9], packed[:, :, 9:25], packed[:, :, 25:41]
        lags = jnp.arange(CHUNK, dtype=F32)
        kern = jnp.sum(res[:, :, None] * jnp.exp(-decay[:, :, None] * lags[:, None, None]), axis=3)
        kern = kern.at[:, :, 0].add(packed[:, :, 41])
        pole = jnp.exp(-decay)
        jumps = jnp.exp(-decay[:, :, None] * jnp.array([CHUNK, 2 * CHUNK, 4 * CHUNK], F32)[:, None, None])
        ahead = jnp.exp(-decay[:, :, :, None] * (CHUNK * jnp.arange(8, dtype=F32))[:, None])

    def blocked(shape, index=None):
        index = index or (lambda r, order: (r,))
        return pl.BlockSpec((1,) + shape, lambda r, *o: index(r, *o) + (0,) * len(shape))

    whole_x = pl.BlockSpec(x_all.shape, lambda r, *o: (0, 0))
    by_order = lambda r, order: (order[r],)
    same = lambda r, *o: (r,)
    scratch = pltpu.VMEM((lanes, seqs, EDGE + length, 128), F32)
    by_chunk = (lanes, seqs, CHUNK, 8, 128)
    with jax.named_scope("keys_values"):
        y, e, ends = pl.pallas_call(
            kv_kernel,
            grid_spec=pltpu.PrefetchScalarGridSpec(
                num_scalar_prefetch=1,
                grid=(blocks,),
                in_specs=[
                    whole_x,
                    blocked(w_kv.shape[1:], by_order),
                    blocked(taps_all.shape[1:], same),
                    blocked(kern.shape[1:], same),
                    blocked(pole.shape[1:], same),
                    blocked(jumps.shape[1:], same),
                ],
                out_specs=[blocked(by_chunk, same), blocked(by_chunk, same), blocked((lanes, seqs, 16, 128), same)],
                scratch_shapes=[scratch, scratch],
            ),
            out_shape=[
                jax.ShapeDtypeStruct((blocks,) + by_chunk, F32),
                jax.ShapeDtypeStruct((blocks,) + by_chunk, F32),
                jax.ShapeDtypeStruct((blocks, lanes, seqs, 16, 128), F32),
            ],
            compiler_params=compiler_params(),
            name="keys_values",
        )(order, x_all, w_kv, taps_all, kern, pole, jumps)

    with jax.named_scope("states"):
        core = lax.axis_index("c")
        span = jnp.exp(-decay * length)[:, :, None]
        sent = ends.astype(BF16)
        other = lax.ppermute(sent, "c", [(0, 1), (1, 0)]).astype(F32)
        sent = sent.astype(F32)
        front, back = jnp.where(core == 0, sent, other), jnp.where(core == 0, other, sent)
        chip = (span * front + back).astype(BF16)
        hops = [from_behind(chip, "y", step).astype(F32) for step in (1, 2, 3)]
        square = span * span
        incoming = hops[0] + square * (hops[1] + square * hops[2])
        incoming = jnp.where(core == 0, incoming, span * incoming + front)

    with jax.named_scope("entering"):
        response = pl.pallas_call(
            enter_kernel,
            grid=(blocks,),
            in_specs=[
                blocked(by_chunk, same),
                blocked(by_chunk, same),
                blocked(incoming.shape[1:], same),
                blocked(pole.shape[1:], same),
                blocked(res.shape[1:], same),
                blocked(ahead.shape[1:], same),
            ],
            out_specs=blocked(by_chunk, same),
            out_shape=jax.ShapeDtypeStruct((blocks,) + by_chunk, F32),
            compiler_params=compiler_params(),
            name="entering",
        )(y, e, incoming, pole, res, ahead)

    with jax.named_scope("query_gate"):
        gated = pl.pallas_call(
            q_kernel,
            grid_spec=pltpu.PrefetchScalarGridSpec(
                num_scalar_prefetch=1,
                grid=(blocks,),
                in_specs=[
                    whole_x,
                    blocked(w_q.shape[1:], by_order),
                    blocked(taps_all.shape[1:], same),
                    blocked(by_chunk, same),
                ],
                out_specs=blocked((seqs, length, channels), same),
                scratch_shapes=[scratch, pltpu.VMEM((lanes, seqs, length, 128), F32)],
            ),
            out_shape=jax.ShapeDtypeStruct((blocks, seqs, length, channels), BF16),
            compiler_params=compiler_params(),
            name="query_gate",
        )(order, x_all, w_q, taps_all, response)

    with jax.named_scope("project_out"):
        cols = 512
        partial = pl.pallas_call(
            out_kernel,
            grid_spec=pltpu.PrefetchScalarGridSpec(
                num_scalar_prefetch=1,
                grid=(width // cols,),
                in_specs=[
                    pl.BlockSpec(gated.shape, lambda i, order: (0, 0, 0, 0)),
                    pl.BlockSpec((blocks, channels, cols), lambda i, order: (0, 0, i)),
                ],
                out_specs=[pl.BlockSpec((length, cols), lambda i, order: (0, i))] * seqs,
            ),
            out_shape=[jax.ShapeDtypeStruct((length, width), BF16)] * seqs,
            compiler_params=compiler_params(),
            name="project_out",
        )(order, gated, w_o)

    with jax.named_scope("sum_parts"):
        total = values + partial[0].astype(F32)
        for s, step in enumerate(OFFSETS):
            if step:
                total += from_ahead(partial[s], "x", -step).astype(F32)
        return total.astype(BF16)[None]


def solution(mesh):
    fine = Mesh(mesh.devices.reshape(4, 4, 4, 2), ("x", "z", "y", "c"))
    fsdp, ctx = ("x", "z"), ("y", "c")
    in_specs = (
        P(fsdp, ctx, None),
        P(),
        P(None, None, fsdp),
        P(None, None, fsdp),
        P(None, fsdp),
        P(None, fsdp),
        P(fsdp),
        P(fsdp, None),
    )
    return jax.shard_map(shards, mesh=fine, in_specs=in_specs, out_specs=P(fsdp, ctx, None), check_vma=False)
```

time: 462 us -> 332 us (0.72)
  local copies, waits for them, and re-layouts: 106 us -> 26 us
  matrix products: 65.9 us -> 0 us
  Pallas kernels: 0 us -> 40.2 us
  other arithmetic: 19.7 us -> 3.31 us
  waiting for transfers between devices: 219 us -> 212 us
    reduce_scatter x1 -> x0, waiting for transfers between devices: 110 us -> none  [shards(): lax.psum_scatter(jnp.dot(gated, w_out, preferred_element_type=jnp.float32...]
    gather x2 -> x0, local copies, waits for them, and re-layouts: 79.8 us -> none  [shards(): kernel[jnp.maximum(lag_steps, 0)]]
    ppermute x8 -> x17, waiting for transfers between devices: 4.24 us -> 83.5 us  [the longest x9 45.6 us: from_ahead(): lax.ppermute(value, axis, [(i, (i - steps) % count) for i in range(count)])]
    dot_general x5 -> x0, matrix products: 65.9 us -> none  [the longest x1 29.6 us: shards(): inside = jnp.einsum('tsc,gsc->gtc', toeplitz, product, precision=high)]
    pallas_call x0 -> x4, Pallas kernels: none -> 40.2 us  [the longest x1 18.6 us: shards(): pl.pallas_call(kv_kernel, grid_spec=pltpu.PrefetchScalarGridSpec(num_scal...]
    all_gather x1 -> x3, waiting for transfers between devices: 105 us -> 128 us  [the longest x1 74.2 us: shards(): lax.all_gather(kv_share, plane, axis=0)]
    concatenate x0 -> x9, local copies, waits for them, and re-layouts: none -> 17.8 us  [the longest x1 17.2 us: shards(): x_all = jnp.concatenate(rows + edges + [tail], axis=0)]
    convert_element_type x10 -> x3, other arithmetic: 10.4 us -> 0.4 us  [the longest x1 0.32 us: shards(): normed = (values * inverse_rms * norm_gain).astype(BF16)]
  transfers between devices with their start and end apart: 10 -> 20, of which waited for: 7 -> 10; matrix products, arithmetic and copies ran while one was open for 27% -> 7% of each run, Pallas kernels for 0% -> 9%
where the time goes in v1:
time: 332 us; the launch traced here: 330 us
  waiting for transfers between devices  212 us (64%)
  Pallas kernels  40.2 us (12%)
  starting transfers between devices  35.4 us (11%)
  local copies, waits for them, and re-layouts  26 us (8%)
  between operations  13.6 us (4%)
    all_gather x1, waiting for transfers between devices, shards(): lax.all_gather(kv_share, plane, axis=0)  74.2 us
    all_gather x1, waiting for transfers between devices, shards(): lax.all_gather(q_share, plane, axis=0).reshape(blocks, 8, depth, channels)  53.9 us
    ppermute x9, waiting for transfers between devices, from_ahead(): lax.ppermute(value, axis, [(i, (i - steps) % count) for i in range(count)])  45.6 us
    ppermute x4, waiting for transfers between devices, shards(): edges.append(lax.ppermute(last, ('x', 'y', 'c'), pairs))  34.1 us
    pallas_call x1, Pallas kernels, shards(): pl.pallas_call(kv_kernel, grid_spec=pltpu.PrefetchScalarGridSpec(num_scal...  18.6 us
    concatenate x1, local copies, waits for them, and re-layouts, shards(): x_all = jnp.concatenate(rows + edges + [tail], axis=0)  17.2 us
    ppermute x9, starting transfers between devices, from_ahead(): lax.ppermute(value, axis, [(i, (i - steps) % count) for i in range(count)])  11 us
    ppermute x4, starting transfers between devices, shards(): edges.append(lax.ppermute(last, ('x', 'y', 'c'), pairs))  9.56 us
  transfers between devices with their start and end apart: 20, of which 10 were waited for; matrix products, arithmetic and copies ran while one was open for 7% of the time, Pallas kernels for 9%

profile of v1, /device:TPU:6, one launch (start us, length us, event | category | flops | bytes accessed | tf_op | source)
XLA Modules:
  0.0 330.1 jit_solution(15265689551702802328)
XLA Ops:
  6.6 2.0 dynamic-slice_bitcast_fusion
  8.7 1.7 dynamic-slice_bitcast_fusion.1
  10.4 74.2 %all-gather.7.cloned.1.call-done = bf16[64,512,256]{2,1,0:T(8,128)(2,1)} async-done(((bf16[2,512,256]{2,1,0:T(8,128)(2,1)}), bf16[64,512,256]{2,1,0:T(8,128)(2,1)}) %all-gather.7.cloned.1.call-update) | async-done | bytes 16777232 | tf_op jit(solution)/shard_map/weights/all_gather | solution.py:156
  85.4 53.9 %all-gather.9.cloned.1.call-done = bf16[16384,256]{1,0:T(8,128)(2,1)} async-done(((bf16[512,256]{1,0:T(8,128)(2,1)}), bf16[16384,256]{1,0:T(8,128)(2,1)}) %all-gather.9.cloned.1.call-update) | async-done | bytes 8388624 | tf_op jit(solution)/shard_map/weights/all_gather | solution.py:158
  139.7 2.6 collective-permute-start.7
  142.3 2.2 collective-permute-start.9
  145.2 0.9 collective-permute-start
  146.1 2.4 collective-permute-start.1
  149.3 1.3 collective-permute-start.3
  150.7 3.0 collective-permute-start.4
  154.2 4.0 %collective-permute-start.5 = (bf16[2,4096]{1,0:T(2,128)(2,1)S(1)}, bf16[2,4096]{1,0:T(2,128)(2,1)S(1)}, u32[]{:S(2)}, u32[]{:S(2)}) collective-permute-start(bf16[2,4096]{1,0:T(2,128)(2,1)S(1)} %slice.48), channel_id=1, source_target_pairs={{0,33},{1,34},{2,35},{3,36},{4,37},{5,38},{6,39},{32,65},{33,66},{... | collective-permute-start | bytes 49160 | tf_op jit(solution)/shard_map/gather_tokens/ppermute | solution.py:178
  158.2 32.8 %collective-permute-done.4 = bf16[2,4096]{1,0:T(2,128)(2,1)S(1)} collective-permute-done((bf16[2,4096]{1,0:T(2,128)(2,1)S(1)}, bf16[2,4096]{1,0:T(2,128)(2,1)S(1)}, u32[]{:S(2)}, u32[]{:S(2)}) %collective-permute-start.4) | collective-permute-done | bytes 16416 | tf_op jit(solution)/shard_map/gather_tokens/ppermute | solution.py:178
  191.0 1.3 collective-permute-start.6
  192.3 0.8 collective-permute-done.5
  193.7 17.2 %concatenate.20.x_ref = bf16[528,4096]{1,0:T(8,128)(2,1)} concatenate(bf16[128,4096]{1,0:T(8,128)(2,1)S(1)} %fusion.2, bf16[128,4096]{1,0:T(8,128)(2,1)S(1)} %collective-permute-done, bf16[128,4096]{1,0:T(8,128)(2,1)} %collective-permute-done.1, bf16[128,4096]{1,0:T(8,128)(2,1)} %collective-permute-done.2, bf16[2,4096]{1,0:T(2,128)(2,1)S(1)} %collective-permute-done.3, ...), dimensions={0} | concatenate | bytes 8650752 | tf_op jit(solution)/shard_map/gather_tokens/concatenate | solution.py:181
  210.9 2.2 copy-done.2
  213.1 18.6 %keys_values.1 = (f32[4,2,4,16,8,128]{5,4,3,2,1,0:T(8,128)S(1)}, f32[4,2,4,16,8,128]{5,4,3,2,1,0:T(8,128)S(1)}, f32[4,2,4,16,128]{4,3,2,1,0:T(8,128)S(1)}) custom-call(s32[4]{0:T(128)S(1)} %pad_add_fusion.order, bf16[528,4096]{1,0:T(8,128)(2,1)S(1)} %copy-done.2, bf16[4,8,2,512,256]{4,3,2,1,0:T(8,128)(2,1)} %bitcast.22, ...), custom_call_target="tpu_custom_call" | custom-call | tf_op jit(solution)/shard_map/keys_values/keys_values/pallas_call | solution.py:207
  231.7 1.3 copy-done.4
  233.1 6.7 %collective-permute-start.10 = (bf16[4,2,4,16,128]{4,3,2,1,0:T(8,128)(2,1)S(1)}, bf16[4,2,4,16,128]{4,3,2,1,0:T(8,128)(2,1)S(1)}, u32[]{:S(2)}, u32[]{:S(2)}) collective-permute-start(bf16[4,2,4,16,128]{4,3,2,1,0:T(8,128)(2,1)S(1)} %convert_element_type.48), channel_id=1, source_target_pairs={{0,1},{1,0},{2,3},{3,2},{4,5},{5,4},{6,7},{7,6},{8,9},{9,8},{10,11... | collective-permute-start | bytes 393224 | tf_op jit(solution)/shard_map/states/ppermute | solution.py:236
  239.8 1.0 collective-permute-done.10
  240.8 2.3 collective-permute-start.11
  243.1 4.5 %collective-permute-start.12 = (bf16[4,2,4,16,128]{4,3,2,1,0:T(8,128)(2,1)S(1)}, bf16[4,2,4,16,128]{4,3,2,1,0:T(8,128)(2,1)S(1)}, u32[]{:S(2)}, u32[]{:S(2)}) collective-permute-start(bf16[4,2,4,16,128]{4,3,2,1,0:T(8,128)(2,1)S(1)} %fusion.9), channel_id=1, source_target_pairs={{0,4},{2,6},{1,5},{3,7},{8,12},{10,14},{9,13},{11,15},{16,20},{18,... | collective-permute-start | bytes 393224 | tf_op jit(solution)/shard_map/states/ppermute | solution.py:22
  247.6 1.3 collective-permute-start.13
  249.1 1.5 collective-permute-done.12
  250.6 1.3 collective-permute-done.13
  252.0 3.0 entering.1.y_ref
  255.1 9.1 %query_gate.1.g_ref = bf16[4,4,128,256]{3,2,1,0:T(8,128)(2,1)S(1)} custom-call(s32[4]{0:T(128)S(1)} %pad_add_fusion.order, bf16[528,4096]{1,0:T(8,128)(2,1)S(1)} %copy-done.3, bf16[4,8,512,256]{3,2,1,0:T(8,128)(2,1)} %bitcast.23, f32[4,2,9,128]{3,2,1,0:T(8,128)S(1)} %slice.49.taps_ref, f32[4,2,4,16,8,128]{5,4,3,2,1,0:T(8,128)S(1)} %entering.1.y_ref), custom_call_target="tpu_custom_call" | custom-call | tf_op jit(solution)/shard_map/query_gate/query_gate/pallas_call | solution.py:264
  264.2 9.5 %project_out.1 = (bf16[128,4096]{1,0:T(8,128)(2,1)S(1)}, bf16[128,4096]{1,0:T(8,128)(2,1)S(1)}, bf16[128,4096]{1,0:T(8,128)(2,1)S(1)}, bf16[128,4096]{1,0:T(8,128)(2,1)S(1)}) custom-call(s32[4]{0:T(128)S(1)} %pad_add_fusion.order, bf16[4,4,128,256]{3,2,1,0:T(8,128)(2,1)S(1)} %query_gate.1.g_ref, bf16[4,256,4096]{2,1,0:T(8,128)(2,1)} %bitcast.24), custom_call_target="tpu_custom_call" | custom-call | tf_op jit(solution)/shard_map/project_out/project_out/pallas_call | solution.py:285
  274.1 1.6 collective-permute-start.15
  276.2 23.6 %collective-permute-done.14 = bf16[128,4096]{1,0:T(8,128)(2,1)S(1)} collective-permute-done((bf16[128,4096]{1,0:T(8,128)(2,1)S(1)}, bf16[128,4096]{1,0:T(8,128)(2,1)S(1)}, u32[]{:S(2)}, u32[]{:S(2)}) %collective-permute-start.14) | collective-permute-done | bytes 1048608 | tf_op jit(solution)/shard_map/sum_parts/ppermute | solution.py:17
  299.8 22.0 %collective-permute-done.15 = bf16[128,4096]{1,0:T(8,128)(2,1)S(1)} collective-permute-done((bf16[128,4096]{1,0:T(8,128)(2,1)S(1)}, bf16[128,4096]{1,0:T(8,128)(2,1)S(1)}, u32[]{:S(2)}, u32[]{:S(2)}) %collective-permute-start.15) | collective-permute-done | bytes 1048608 | tf_op jit(solution)/shard_map/sum_parts/ppermute | solution.py:17
  321.8 1.8 fusion.7
  (83 shorter events, 5.0 us)
Async XLA Ops:
  6.5 78.2 %copy-start = (bf16[256,4096]{1,0:T(8,128)(2,1)S(1)}, bf16[256,4096]{1,0:T(8,128)(2,1)}, u32[]{:S(2)}) copy-start(bf16[256,4096]{1,0:T(8,128)(2,1)} %param.18) | copy-start | bytes 6291460
  6.5 132.8 %copy-start.10 = (f32[3,3,256]{2,1,0:T(4,128)S(1)}, f32[3,3,256]{2,1,0:T(4,128)}, u32[]{:S(2)}) copy-start(f32[3,3,256]{2,1,0:T(4,128)} %param.14) | copy-start | bytes 27652
  6.5 132.9 %copy-start.12 = (f32[256]{0:T(256)S(1)}, f32[256]{0:T(256)}, u32[]{:S(2)}) copy-start(f32[256]{0:T(256)} %param.17) | copy-start | bytes 3076
  6.5 132.9 %copy-start.8 = (f32[16,256]{1,0:T(8,128)S(1)}, f32[16,256]{1,0:T(8,128)}, u32[]{:S(2)}) copy-start(f32[16,256]{1,0:T(8,128)} %param.15) | copy-start | bytes 49156
  6.5 132.9 %copy-start.9 = (f32[16,256]{1,0:T(8,128)S(1)}, f32[16,256]{1,0:T(8,128)}, u32[]{:S(2)}) copy-start(f32[16,256]{1,0:T(8,128)} %param.16) | copy-start | bytes 49156
  6.5 138.0 %copy-start.6 = (bf16[1,128,4096]{2,1,0:T(8,128)(2,1)S(1)}, bf16[1,128,4096]{2,1,0:T(8,128)(2,1)}, u32[]{:S(2)}) copy-start(bf16[1,128,4096]{2,1,0:T(8,128)(2,1)} %param.11) | copy-start | bytes 3145732
  6.6 78.0 %all-gather.7.cloned.1.call-start = ((), (), s32[]{:S(2)}) async-start(), calls=%async_computation | async-start | bytes 17301504 | tf_op jit(solution)/shard_map/weights/all_gather | solution.py:156
  6.6 138.3 %copy-start.11 = (f32[4096]{0:T(1024)S(1)}, f32[4096]{0:T(1024)}, u32[]{:S(2)}) copy-start(f32[4096]{0:T(1024)} %param.12) | copy-start | bytes 49156
  8.7 130.7 %all-gather.9.cloned.1.call-start = ((), (), s32[]{:S(2)}) async-start(), calls=%async_computation.1 | async-start | bytes 8650752 | tf_op jit(solution)/shard_map/weights/all_gather | solution.py:158
  84.6 179.5 %all-gather.11.cloned.1.call-start = ((), (), s32[]{:S(2)}) async-start(), calls=%async_computation.2 | async-start | bytes 8650752 | tf_op jit(solution)/shard_map/weights/all_gather | solution.py:160
  139.7 8.8 %collective-permute-start.7 = (f32[48,256]{1,0:T(8,128)S(1)}, f32[48,256]{1,0:T(8,128)S(1)}, u32[]{:S(2)}, u32[]{:S(2)}) collective-permute-start(f32[48,256]{1,0:T(8,128)S(1)} %concatenate.26), channel_id=1, source_target_pairs={{0,24},{8,0},{16,8},{24,16},{1,25},{9,1},{17,9},{25,17},{2,26},{10... | collective-permute-start | bytes 147464 | tf_op jit(solution)/shard_map/params/ppermute | solution.py:17
  142.3 7.0 %collective-permute-start.8 = (f32[48,256]{1,0:T(8,128)S(1)}, f32[48,256]{1,0:T(8,128)S(1)}, u32[]{:S(2)}, u32[]{:S(2)}) collective-permute-start(f32[48,256]{1,0:T(8,128)S(1)} %concatenate.26), channel_id=1, source_target_pairs={{0,8},{8,16},{16,24},{24,0},{1,9},{9,17},{17,25},{25,1},{2,10},{10... | collective-permute-start | bytes 147464 | tf_op jit(solution)/shard_map/params/ppermute | solution.py:17
  142.3 8.3 %collective-permute-start.9 = (f32[48,256]{1,0:T(8,128)S(1)}, f32[48,256]{1,0:T(8,128)S(1)}, u32[]{:S(2)}, u32[]{:S(2)}) collective-permute-start(f32[48,256]{1,0:T(8,128)S(1)} %concatenate.26), channel_id=1, source_target_pairs={{0,16},{8,24},{16,0},{24,8},{1,17},{9,25},{17,1},{25,9},{2,18},{10... | collective-permute-start | bytes 147464 | tf_op jit(solution)/shard_map/params/ppermute | solution.py:17
  144.9 8.9 %copy-start.13 = (f32[3]{0:T(128)S(1)}, f32[3]{0:T(128)}, u32[]{:S(2)}) copy-start(f32[3]{0:T(128)} %constant.92.clone) | copy-start | bytes 40
  145.2 48.5 %collective-permute-start = (bf16[128,4096]{1,0:T(8,128)(2,1)S(1)}, bf16[128,4096]{1,0:T(8,128)(2,1)S(1)}, u32[]{:S(2)}, u32[]{:S(2)}) collective-permute-start(bf16[128,4096]{1,0:T(8,128)(2,1)S(1)} %fusion.2), channel_id=1, source_target_pairs={{0,96},{32,0},{64,32},{96,64},{1,97},{33,1},{65,33},{97,65},{2,98}... | collective-permute-start | bytes 3145736 | tf_op jit(solution)/shard_map/gather_tokens/ppermute | solution.py:17
  146.1 47.5 %collective-permute-start.1 = (bf16[128,4096]{1,0:T(8,128)(2,1)S(1)}, bf16[128,4096]{1,0:T(8,128)(2,1)}, u32[]{:S(2)}, u32[]{:S(2)}) collective-permute-start(bf16[128,4096]{1,0:T(8,128)(2,1)S(1)} %fusion.2), channel_id=1, source_target_pairs={{0,32},{32,64},{64,96},{96,0},{1,33},{33,65},{65,97},{97,1},{2,34}... | collective-permute-start | bytes 3145736 | tf_op jit(solution)/shard_map/gather_tokens/ppermute | solution.py:17
  148.5 45.1 %collective-permute-start.2 = (bf16[128,4096]{1,0:T(8,128)(2,1)S(1)}, bf16[128,4096]{1,0:T(8,128)(2,1)}, u32[]{:S(2)}, u32[]{:S(2)}) collective-permute-start(bf16[128,4096]{1,0:T(8,128)(2,1)S(1)} %fusion.2), channel_id=1, source_target_pairs={{0,64},{32,96},{64,0},{96,32},{1,65},{33,97},{65,1},{97,33},{2,66}... | collective-permute-start | bytes 3145736 | tf_op jit(solution)/shard_map/gather_tokens/ppermute | solution.py:17
  149.3 4.9 %collective-permute-start.3 = (bf16[2,4096]{1,0:T(2,128)(2,1)S(1)}, bf16[2,4096]{1,0:T(2,128)(2,1)S(1)}, u32[]{:S(2)}, u32[]{:S(2)}) collective-permute-start(bf16[2,4096]{1,0:T(2,128)(2,1)S(1)} %slice.48), channel_id=1, source_target_pairs={{0,1},{1,2},{2,3},{3,4},{4,5},{5,6},{6,7},{32,33},{33,34},{34,35},... | collective-permute-start | bytes 49160 | tf_op jit(solution)/shard_map/gather_tokens/ppermute | solution.py:178
  150.7 40.3 %collective-permute-start.4 = (bf16[2,4096]{1,0:T(2,128)(2,1)S(1)}, bf16[2,4096]{1,0:T(2,128)(2,1)S(1)}, u32[]{:S(2)}, u32[]{:S(2)}) collective-permute-start(bf16[2,4096]{1,0:T(2,128)(2,1)S(1)} %slice.48), channel_id=1, source_target_pairs={{0,97},{1,98},{2,99},{3,100},{4,101},{5,102},{6,103},{32,1},{33,2}... | collective-permute-start | bytes 49160 | tf_op jit(solution)/shard_map/gather_tokens/ppermute | solution.py:178
  154.2 38.9 %collective-permute-start.5 = (bf16[2,4096]{1,0:T(2,128)(2,1)S(1)}, bf16[2,4096]{1,0:T(2,128)(2,1)S(1)}, u32[]{:S(2)}, u32[]{:S(2)}) collective-permute-start(bf16[2,4096]{1,0:T(2,128)(2,1)S(1)} %slice.48), channel_id=1, source_target_pairs={{0,33},{1,34},{2,35},{3,36},{4,37},{5,38},{6,39},{32,65},{33,66},{... | collective-permute-start | bytes 49160 | tf_op jit(solution)/shard_map/gather_tokens/ppermute | solution.py:178
  191.0 2.7 collective-permute-start.6
  210.9 2.2 copy-start.2
  233.1 7.7 %collective-permute-start.10 = (bf16[4,2,4,16,128]{4,3,2,1,0:T(8,128)(2,1)S(1)}, bf16[4,2,4,16,128]{4,3,2,1,0:T(8,128)(2,1)S(1)}, u32[]{:S(2)}, u32[]{:S(2)}) collective-permute-start(bf16[4,2,4,16,128]{4,3,2,1,0:T(8,128)(2,1)S(1)} %convert_element_type.48), channel_id=1, source_target_pairs={{0,1},{1,0},{2,3},{3,2},{4,5},{5,4},{6,7},{7,6},{8,9},{9,8},{10,11... | collective-permute-start | bytes 393224 | tf_op jit(solution)/shard_map/states/ppermute | solution.py:236
  239.8 12.2 %copy-start.5 = (f32[4,2,4,16,8,128]{5,4,3,2,1,0:T(8,128)S(1)}, f32[4,2,4,16,8,128]{5,4,3,2,1,0:T(8,128)}, u32[]{:S(2)}) copy-start(f32[4,2,4,16,8,128]{5,4,3,2,1,0:T(8,128)} %copy-done.4) | copy-start | bytes 6291460
  240.8 8.2 %collective-permute-start.11 = (bf16[4,2,4,16,128]{4,3,2,1,0:T(8,128)(2,1)S(1)}, bf16[4,2,4,16,128]{4,3,2,1,0:T(8,128)(2,1)S(1)}, u32[]{:S(2)}, u32[]{:S(2)}) collective-permute-start(bf16[4,2,4,16,128]{4,3,2,1,0:T(8,128)(2,1)S(1)} %fusion.9), channel_id=1, source_target_pairs={{0,2},{2,4},{4,6},{1,3},{3,5},{5,7},{8,10},{10,12},{12,14},{9,11},... | collective-permute-start | bytes 393224 | tf_op jit(solution)/shard_map/states/ppermute | solution.py:22
  243.1 7.4 %collective-permute-start.12 = (bf16[4,2,4,16,128]{4,3,2,1,0:T(8,128)(2,1)S(1)}, bf16[4,2,4,16,128]{4,3,2,1,0:T(8,128)(2,1)S(1)}, u32[]{:S(2)}, u32[]{:S(2)}) collective-permute-start(bf16[4,2,4,16,128]{4,3,2,1,0:T(8,128)(2,1)S(1)} %fusion.9), channel_id=1, source_target_pairs={{0,4},{2,6},{1,5},{3,7},{8,12},{10,14},{9,13},{11,15},{16,20},{18,... | collective-permute-start | bytes 393224 | tf_op jit(solution)/shard_map/states/ppermute | solution.py:22
  247.6 4.3 %collective-permute-start.13 = (bf16[4,2,4,16,128]{4,3,2,1,0:T(8,128)(2,1)S(1)}, bf16[4,2,4,16,128]{4,3,2,1,0:T(8,128)(2,1)S(1)}, u32[]{:S(2)}, u32[]{:S(2)}) collective-permute-start(bf16[4,2,4,16,128]{4,3,2,1,0:T(8,128)(2,1)S(1)} %fusion.9), channel_id=1, source_target_pairs={{0,6},{1,7},{8,14},{9,15},{16,22},{17,23},{24,30},{25,31},{32,38},... | collective-permute-start | bytes 393224 | tf_op jit(solution)/shard_map/states/ppermute | solution.py:22
  252.0 3.0 copy-start.3
  264.2 57.6 %copy-start.7 = (bf16[1,128,4096]{2,1,0:T(8,128)(2,1)S(1)}, bf16[1,128,4096]{2,1,0:T(8,128)(2,1)}, u32[]{:S(2)}) copy-start(bf16[1,128,4096]{2,1,0:T(8,128)(2,1)} %param.11) | copy-start | bytes 3145732
  273.6 26.2 %collective-permute-start.14 = (bf16[128,4096]{1,0:T(8,128)(2,1)S(1)}, bf16[128,4096]{1,0:T(8,128)(2,1)S(1)}, u32[]{:S(2)}, u32[]{:S(2)}) collective-permute-start(bf16[128,4096]{1,0:T(8,128)(2,1)S(1)} %get-tuple-element.36), channel_id=1, source_target_pairs={{0,32},{32,64},{64,96},{96,0},{1,33},{33,65},{65,97},{97,1},{2,34}... | collective-permute-start | bytes 3145736 | tf_op jit(solution)/shard_map/sum_parts/ppermute | solution.py:17
  274.1 47.7 %collective-permute-start.15 = (bf16[128,4096]{1,0:T(8,128)(2,1)S(1)}, bf16[128,4096]{1,0:T(8,128)(2,1)S(1)}, u32[]{:S(2)}, u32[]{:S(2)}) collective-permute-start(bf16[128,4096]{1,0:T(8,128)(2,1)S(1)} %get-tuple-element.37), channel_id=1, source_target_pairs={{0,96},{32,0},{64,32},{96,64},{1,97},{33,1},{65,33},{97,65},{2,98}... | collective-permute-start | bytes 3145736 | tf_op jit(solution)/shard_map/sum_parts/ppermute | solution.py:17
  275.7 46.0 %collective-permute-start.16 = (bf16[128,4096]{1,0:T(8,128)(2,1)S(1)}, bf16[128,4096]{1,0:T(8,128)(2,1)S(1)}, u32[]{:S(2)}, u32[]{:S(2)}) collective-permute-start(bf16[128,4096]{1,0:T(8,128)(2,1)S(1)} %get-tuple-element.38), channel_id=1, source_target_pairs={{0,64},{32,96},{64,0},{96,32},{1,65},{33,97},{65,1},{97,33},{2,66}... | collective-permute-start | bytes 3145736 | tf_op jit(solution)/shard_map/sum_parts/ppermute | solution.py:17
  (2 other events, 3.2 us)
Sparse Core Ops, SparseCore 0:
  9.7 74.9 all-gather.6
  86.9 52.4 all-gather.8
  141.6 52.5 all-gather.10

commit v2 on v1

--- a/solution.py
+++ b/solution.py
@@ -26,29 +26,74 @@
     return pltpu.CompilerParams(vmem_limit_bytes=44 * 1024 * 1024)
 
 
-def project(x_ref, w_ref, scratch, seqs, length):
-    pieces, depth, width = w_ref.shape
-    total = jnp.dot(x_ref[:, :depth], w_ref[0], preferred_element_type=F32)
-    for k in range(1, pieces):
-        total += jnp.dot(x_ref[:, k * depth : (k + 1) * depth], w_ref[k], preferred_element_type=F32)
-    total = total.astype(BF16).astype(F32)
+def load_rows(row_refs, x, sems):
+    copies, first = [], 0
+    for i, ref in enumerate(row_refs):
+        copies.append(pltpu.make_async_copy(ref, x.at[pl.ds(first, ref.shape[0])], sems.at[i]))
+        first += ref.shape[0]
+    for copy in copies:
+        copy.start()
+    for copy in copies:
+        copy.wait()
+
+
+def dot(a, b):
+    return jnp.dot(a, b, preferred_element_type=F32)
+
+
+def from_pieces(quarter, x, own_ref, piece_refs, out):
+    depth = piece_refs[0].shape[1]
+    block = pl.program_id(0)
+
+    @pl.when(block == 0)
+    def _():
+        out[...] = dot(x[...], own_ref[...])
+
+    @pl.when(block > 0)
+    def _():
+        total = None
+        for i, ref in enumerate(piece_refs):
+            part = dot(x[:, pl.ds(pl.multiple_of(quarter[i] * depth, depth), depth)], ref[0])
+            total = part if total is None else total + part
+        out[...] = total
+
+
+def lay_out(total, scratch, seqs, length):
     rows = seqs * length
-    for lane in range(width // 128):
+    for lane in range(scratch.shape[0]):
         cols = slice(lane * 128, (lane + 1) * 128)
         for s in range(seqs):
             scratch[lane, s, EDGE : EDGE + length, :] = total[s * length : (s + 1) * length, cols]
             scratch[lane, s, EDGE - 2 : EDGE, :] = total[rows + 2 * s : rows + 2 * s + 2, cols]
 
 
+def k_kernel(quarter, own_ref, p0, p1, p2, p3, r0, r1, r2, r3, r4, out_ref, x, total, sems):
+    @pl.when(pl.program_id(0) == 0)
+    def _():
+        load_rows((r0, r1, r2, r3, r4), x, sems)
+
+    from_pieces(quarter, x, own_ref, (p0, p1, p2, p3), total)
+    out_ref[0] = total[...].astype(BF16)
+
+
 def wide(row):
     return jnp.broadcast_to(row, (8, 128))
 
 
-def kv_kernel(order, x_ref, w_ref, taps_ref, kern_ref, pole_ref, jump_ref, y_ref, e_ref, t_ref, fk, fv):
+def v_kernel(
+    quarter, own_ref, p0, p1, p2, p3, r0, r1, r2, r3, r4, k_ref, taps_ref, kern_ref, pole_ref, jump_ref,
+    y_ref, e_ref, t_ref, x, total, sems, fk, fv,
+):
     seqs = fk.shape[1]
     length = fk.shape[2] - EDGE
-    project(x_ref, w_ref.at[0, :, 0], fk, seqs, length)
-    project(x_ref, w_ref.at[0, :, 1], fv, seqs, length)
+
+    @pl.when(pl.program_id(0) == 0)
+    def _():
+        load_rows((r0, r1, r2, r3, r4), x, sems)
+
+    from_pieces(quarter, x, own_ref, (p0, p1, p2, p3), total)
+    lay_out(k_ref[0].astype(F32), fk, seqs, length)
+    lay_out(total[...].astype(BF16).astype(F32), fv, seqs, length)
     first_row = lax.broadcasted_iota(jnp.int32, (8, 128), 0)
 
     def each(i, carry):
@@ -108,10 +153,19 @@
     lax.fori_loop(0, seqs * lanes, each, 0)
 
 
-def q_kernel(order, x_ref, w_ref, taps_ref, y_ref, out_ref, fq, gated):
+def q_kernel(order, w_ref, r0, r1, r2, r3, r4, taps_ref, y_ref, out_ref, x, sems, fq, gated):
     lanes, seqs = fq.shape[:2]
     length = fq.shape[2] - EDGE
-    project(x_ref, w_ref.at[0], fq, seqs, length)
+    _, pieces, depth, _ = w_ref.shape
+
+    @pl.when(pl.program_id(0) == 0)
+    def _():
+        load_rows((r0, r1, r2, r3, r4), x, sems)
+
+    total = dot(x[:, :depth], w_ref[0, 0])
+    for k in range(1, pieces):
+        total += dot(x[:, k * depth : (k + 1) * depth], w_ref[0, k])
+    lay_out(total.astype(BF16).astype(F32), fq, seqs, length)
 
     def each(i, carry):
         lane, s = i // seqs, i % seqs
@@ -129,12 +183,16 @@
 
 
 def out_kernel(order, g_ref, w_ref, *out_refs):
-    blocks, seqs = g_ref.shape[:2]
+    blocks, seqs, length, channels = g_ref.shape
+    total = [None] * 2
+    for r in range(blocks):
+        rows = g_ref[r].reshape(seqs * length, channels)
+        for half in range(2):
+            part = dot(rows, w_ref[order[r], 0, half * channels : (half + 1) * channels, :])
+            total[half] = part if r == 0 else total[half] + part
     for s in range(seqs):
-        total = jnp.dot(g_ref[0, s], w_ref[order[0]], preferred_element_type=F32)
-        for r in range(1, blocks):
-            total += jnp.dot(g_ref[r, s], w_ref[order[r]], preferred_element_type=F32)
-        out_refs[s][...] = total.astype(BF16)
+        for half in range(2):
+            out_refs[s][:, half * 256 : (half + 1) * 256] = total[half][s * length : (s + 1) * length].astype(BF16)
 
 
 def shards(tokens, norm_gain, w_in, taps, decay_rate, residues, skip_gain, w_out):
@@ -146,18 +204,13 @@
     blocks = seqs = len(OFFSETS)
     lanes = channels // 128
 
-    with jax.named_scope("weights"):
+    with jax.named_scope("background_weights"):
         w_streams = w_in.transpose(1, 0, 2)
         depth = width // 8
-        kv_share = lax.dynamic_slice(w_streams, (1, part * depth, 0), (2, depth, channels))
         q_share = lax.dynamic_slice(w_streams, (0, part * depth, 0), (1, depth, channels))[0]
-        out_share = lax.dynamic_slice(w_out, (part * (channels // 8), 0), (channels // 8, width))
-        plane = ("z", "y", "c")
-        w_kv = lax.all_gather(kv_share, plane, axis=0).reshape(blocks, 8, 2, depth, channels)
-        q_share, w_kv = lax.optimization_barrier((q_share, w_kv))
-        w_q = lax.all_gather(q_share, plane, axis=0).reshape(blocks, 8, depth, channels)
-        out_share, w_q = lax.optimization_barrier((out_share, w_q))
-        w_o = lax.all_gather(out_share, plane, axis=0).reshape(blocks, channels, width)
+        out_share = [lax.dynamic_slice(w_out, (0, part * depth + half * 256), (channels, 256)) for half in range(2)]
+        w_qo = lax.all_gather(jnp.concatenate([q_share] + out_share, axis=0), ("z", "y", "c"), axis=0)
+        w_qo = w_qo.reshape(blocks, 8, 2 * depth, channels)
 
     with jax.named_scope("norm"):
         values = tokens[0].astype(F32)
@@ -177,8 +230,21 @@
             ]
             edges.append(lax.ppermute(last, ("x", "y", "c"), pairs))
         rows = [normed] + [from_ahead(normed, "x", step) for step in OFFSETS[1:]]
-        tail = jnp.zeros((16 - 2 * seqs, width), BF16)
-        x_all = jnp.concatenate(rows + edges + [tail], axis=0)
+        rows.append(jnp.concatenate(edges + [jnp.zeros((16 - 2 * seqs, width), BF16)], axis=0))
+
+    with jax.named_scope("gather_kv_weights"):
+        parity, core = lax.axis_index("y") % 2, lax.axis_index("c")
+        own_quarter = 2 * parity + core
+        quarter = jnp.stack([own_quarter, own_quarter ^ 2, own_quarter ^ 1, own_quarter ^ 3]).astype(jnp.int32)
+        pieces = []
+        for stream, way in ((1, 1), (2, -1)):
+            share = lax.dynamic_slice(w_streams, (stream, own_quarter * (width // 4), 0), (1, width // 4, channels))[0]
+            ahead = from_ahead(share, "z", 1)
+            behind = from_ahead(share, "z", -1)
+            far = from_ahead(behind if way == 1 else ahead, "z", -way)
+            along_z = jnp.stack([ahead, behind, far])
+            along_y = jnp.stack([from_ahead(ahead, "y", 1), from_ahead(behind, "y", -1), from_ahead(far, "y", -way)])
+            pieces.append([along_z, along_y, from_ahead(along_z, "c", 1), from_ahead(along_y, "c", 1)])
 
     with jax.named_scope("params"):
         packed = jnp.concatenate(
@@ -198,27 +264,46 @@
         index = index or (lambda r, order: (r,))
         return pl.BlockSpec((1,) + shape, lambda r, *o: index(r, *o) + (0,) * len(shape))
 
-    whole_x = pl.BlockSpec(x_all.shape, lambda r, *o: (0, 0))
     by_order = lambda r, order: (order[r],)
     same = lambda r, *o: (r,)
     scratch = pltpu.VMEM((lanes, seqs, EDGE + length, 128), F32)
     by_chunk = (lanes, seqs, CHUNK, 8, 128)
-    with jax.named_scope("keys_values"):
-        y, e, ends = pl.pallas_call(
-            kv_kernel,
+    high = seqs * length + 16
+    in_place = [pl.BlockSpec(memory_space=pl.ANY)] * len(rows)
+    x_scratch, row_sems = pltpu.VMEM((high, width), BF16), pltpu.SemaphoreType.DMA((len(rows),))
+    weight_specs = [pl.BlockSpec((width, channels), lambda r, *o: (0, 0))]
+    weight_specs += [blocked((width // 4, channels), lambda r, *o: (jnp.maximum(r - 1, 0),))] * 4
+    with jax.named_scope("keys"):
+        keys = pl.pallas_call(
+            k_kernel,
             grid_spec=pltpu.PrefetchScalarGridSpec(
                 num_scalar_prefetch=1,
                 grid=(blocks,),
-                in_specs=[
-                    whole_x,
-                    blocked(w_kv.shape[1:], by_order),
+                in_specs=weight_specs + in_place,
+                out_specs=blocked((high, channels), same),
+                scratch_shapes=[x_scratch, pltpu.VMEM((high, channels), F32), row_sems],
+            ),
+            out_shape=jax.ShapeDtypeStruct((blocks, high, channels), BF16),
+            compiler_params=compiler_params(),
+            name="keys",
+        )(quarter, w_streams[1], *pieces[0], *rows)
+    with jax.named_scope("values_filter"):
+        y, e, ends = pl.pallas_call(
+            v_kernel,
+            grid_spec=pltpu.PrefetchScalarGridSpec(
+                num_scalar_prefetch=1,
+                grid=(blocks,),
+                in_specs=weight_specs
+                + in_place
+                + [
+                    blocked((high, channels), same),
                     blocked(taps_all.shape[1:], same),
                     blocked(kern.shape[1:], same),
                     blocked(pole.shape[1:], same),
                     blocked(jumps.shape[1:], same),
                 ],
                 out_specs=[blocked(by_chunk, same), blocked(by_chunk, same), blocked((lanes, seqs, 16, 128), same)],
-                scratch_shapes=[scratch, scratch],
+                scratch_shapes=[x_scratch, pltpu.VMEM((high, channels), F32), row_sems, scratch, scratch],
             ),
             out_shape=[
                 jax.ShapeDtypeStruct((blocks,) + by_chunk, F32),
@@ -226,11 +311,10 @@
                 jax.ShapeDtypeStruct((blocks, lanes, seqs, 16, 128), F32),
             ],
             compiler_params=compiler_params(),
-            name="keys_values",
-        )(order, x_all, w_kv, taps_all, kern, pole, jumps)
+            name="values_filter",
+        )(quarter, w_streams[2], *pieces[1], *rows, keys, taps_all, kern, pole, jumps)
 
     with jax.named_scope("states"):
-        core = lax.axis_index("c")
         span = jnp.exp(-decay * length)[:, :, None]
         sent = ends.astype(BF16)
         other = lax.ppermute(sent, "c", [(0, 1), (1, 0)]).astype(F32)
@@ -266,19 +350,16 @@
             grid_spec=pltpu.PrefetchScalarGridSpec(
                 num_scalar_prefetch=1,
                 grid=(blocks,),
-                in_specs=[
-                    whole_x,
-                    blocked(w_q.shape[1:], by_order),
-                    blocked(taps_all.shape[1:], same),
-                    blocked(by_chunk, same),
-                ],
+                in_specs=[blocked((8, depth, channels), by_order)]
+                + in_place
+                + [blocked(taps_all.shape[1:], same), blocked(by_chunk, same)],
                 out_specs=blocked((seqs, length, channels), same),
-                scratch_shapes=[scratch, pltpu.VMEM((lanes, seqs, length, 128), F32)],
+                scratch_shapes=[x_scratch, row_sems, scratch, pltpu.VMEM((lanes, seqs, length, 128), F32)],
             ),
             out_shape=jax.ShapeDtypeStruct((blocks, seqs, length, channels), BF16),
             compiler_params=compiler_params(),
             name="query_gate",
-        )(order, x_all, w_q, taps_all, response)
+        )(order, w_qo, *rows, taps_all, response)
 
     with jax.named_scope("project_out"):
         cols = 512
@@ -289,14 +370,14 @@
                 grid=(width // cols,),
                 in_specs=[
                     pl.BlockSpec(gated.shape, lambda i, order: (0, 0, 0, 0)),
-                    pl.BlockSpec((blocks, channels, cols), lambda i, order: (0, 0, i)),
+                    pl.BlockSpec((blocks, 1, depth, channels), lambda i, order: (0, i, 1, 0)),
                 ],
                 out_specs=[pl.BlockSpec((length, cols), lambda i, order: (0, i))] * seqs,
             ),
             out_shape=[jax.ShapeDtypeStruct((length, width), BF16)] * seqs,
             compiler_params=compiler_params(),
             name="project_out",
-        )(order, gated, w_o)
+        )(order, gated, w_qo)
 
     with jax.named_scope("sum_parts"):
         total = values + partial[0].astype(F32)

time: 332 us -> 292 us (0.88)
  waiting for transfers between devices: 212 us -> 130 us
  starting transfers between devices: 35.4 us -> 60.8 us
  other arithmetic: 3.31 us -> 18.8 us
  Pallas kernels: 40.2 us -> 50.1 us
  local copies, waits for them, and re-layouts: 26 us -> 16.6 us
    all_gather x3 -> x1, waiting for transfers between devices: 128 us -> 0.01 us  [shards(): lax.all_gather(jnp.concatenate([q_share] + out_share, axis=0), ('z', 'y',...]
    ppermute x9 -> x25, waiting for transfers between devices: 45.6 us -> 126 us  [from_ahead(): lax.ppermute(value, axis, [(i, (i - steps) % count) for i in range(count)])]
    ppermute x4, waiting for transfers between devices: 34.1 us -> 0.83 us  [shards(): edges.append(lax.ppermute(last, ('x', 'y', 'c'), pairs))]
    ppermute x9 -> x25, starting transfers between devices: 11 us -> 40.3 us  [from_ahead(): lax.ppermute(value, axis, [(i, (i - steps) % count) for i in range(count)])]
    concatenate x1, local copies, waits for them, and re-layouts: 17.2 us -> 0.11 us  [shards(): jnp.concatenate(edges + [jnp.zeros((16 - 2 * seqs, width), BF16)], axis=0)]
    another operation x0 -> x5, other arithmetic: none -> 10.6 us  [the longest x2 5.39 us: shards(): along_z = jnp.stack([ahead, behind, far])]
    pallas_call x1 -> x2, Pallas kernels: 18.6 us -> 27 us  [the longest x1 17.1 us: shards(): pl.pallas_call(v_kernel, grid_spec=pltpu.PrefetchScalarGridSpec(num_scala...]
    ppermute x1, starting transfers between devices: 6.7 us -> 0.01 us  [shards(): other = lax.ppermute(sent, 'c', [(0, 1), (1, 0)]).astype(F32)]
  transfers between devices with their start and end apart: 20 -> 34, of which waited for: 10 -> 14; matrix products, arithmetic and copies ran while one was open for 7% -> 9% of each run, Pallas kernels for 9% -> 10%
where the time goes in v2:
time: 292 us; the launch traced here: 291 us
  waiting for transfers between devices  130 us (45%)
  starting transfers between devices  60.8 us (21%)
  Pallas kernels  50.1 us (17%)
  other arithmetic  18.8 us (6%)
  local copies, waits for them, and re-layouts  16.6 us (6%)
  between operations  14 us (5%)
    ppermute x25, waiting for transfers between devices, from_ahead(): lax.ppermute(value, axis, [(i, (i - steps) % count) for i in range(count)])  126 us
    ppermute x25, starting transfers between devices, from_ahead(): lax.ppermute(value, axis, [(i, (i - steps) % count) for i in range(count)])  40.3 us
    pallas_call x1, Pallas kernels, shards(): pl.pallas_call(v_kernel, grid_spec=pltpu.PrefetchScalarGridSpec(num_scala...  17.1 us
    ppermute x4, starting transfers between devices, shards(): edges.append(lax.ppermute(last, ('x', 'y', 'c'), pairs))  12.3 us
    pallas_call x1, Pallas kernels, shards(): pl.pallas_call(q_kernel, grid_spec=pltpu.PrefetchScalarGridSpec(num_scala...  10.7 us
    pallas_call x1, Pallas kernels, shards(): pl.pallas_call(k_kernel, grid_spec=pltpu.PrefetchScalarGridSpec(num_scala...  9.86 us
    pallas_call x1, Pallas kernels, shards(): pl.pallas_call(out_kernel, grid_spec=pltpu.PrefetchScalarGridSpec(num_sca...  9.46 us
    ppermute x3, starting transfers between devices, from_behind(): lax.ppermute(value, axis, [(i, i + steps) for i in range(count - steps)])  8.29 us
  transfers between devices with their start and end apart: 34, of which 14 were waited for; matrix products, arithmetic and copies ran while one was open for 9% of the time, Pallas kernels for 10%

profile of v2, /device:TPU:6, one launch (start us, length us, event | category | flops | bytes accessed | tf_op | source)
XLA Modules:
  0.0 290.7 jit_solution(14249432547977008108)
XLA Ops:
  12.8 2.2 collective-permute-start.18
  17.3 11.4 %collective-permute-done.19 = bf16[1024,256]{1,0:T(8,128)(2,1)S(1)} collective-permute-done((bf16[1024,256]{1,0:T(8,128)(2,1)S(1)}, bf16[1024,256]{1,0:T(8,128)(2,1)S(1)}, u32[]{:S(2)}, u32[]{:S(2)}) %collective-permute-start.19) | collective-permute-done | bytes 524320 | tf_op jit(solution)/shard_map/gather_kv_weights/ppermute | solution.py:17
  32.0 4.7 %collective-permute-start.4 = (bf16[2,4096]{1,0:T(2,128)(2,1)S(1)}, bf16[2,4096]{1,0:T(2,128)(2,1)S(1)}, u32[]{:S(2)}, u32[]{:S(2)}) collective-permute-start(bf16[2,4096]{1,0:T(2,128)(2,1)S(1)} %slice.56), channel_id=1, source_target_pairs={{0,97},{1,98},{2,99},{3,100},{4,101},{5,102},{6,103},{32,1},{33,2}... | collective-permute-start | bytes 49160 | tf_op jit(solution)/shard_map/gather_tokens/ppermute | solution.py:231
  36.8 3.5 %collective-permute-start.21 = (bf16[1024,256]{1,0:T(8,128)(2,1)S(1)}, bf16[1024,256]{1,0:T(8,128)(2,1)S(1)}, u32[]{:S(2)}, u32[]{:S(2)}) collective-permute-start(bf16[1024,256]{1,0:T(8,128)(2,1)S(1)} %collective-permute-done.18), channel_id=1, source_target_pairs={{0,6},{2,0},{4,2},{6,4},{1,7},{3,1},{5,3},{7,5},{8,14},{10,8},{12,... | collective-permute-start | bytes 1572872 | tf_op jit(solution)/shard_map/gather_kv_weights/ppermute | solution.py:17
  40.3 3.5 %collective-permute-start.22 = (bf16[1024,256]{1,0:T(8,128)(2,1)S(1)}, bf16[1024,256]{1,0:T(8,128)(2,1)S(1)}, u32[]{:S(2)}, u32[]{:S(2)}) collective-permute-start(bf16[1024,256]{1,0:T(8,128)(2,1)S(1)} %collective-permute-done.19), channel_id=1, source_target_pairs={{0,2},{2,4},{4,6},{6,0},{1,3},{3,5},{5,7},{7,1},{8,10},{10,12},{12... | collective-permute-start | bytes 1572872 | tf_op jit(solution)/shard_map/gather_kv_weights/ppermute | solution.py:17
  43.8 2.2 collective-permute-done.10
  46.0 3.5 %collective-permute-start.12 = (bf16[1024,256]{1,0:T(8,128)(2,1)S(1)}, bf16[1024,256]{1,0:T(8,128)(2,1)}, u32[]{:S(2)}, u32[]{:S(2)}) collective-permute-start(bf16[1024,256]{1,0:T(8,128)(2,1)S(1)} %collective-permute-done.10), channel_id=1, source_target_pairs={{0,24},{8,0},{16,8},{24,16},{1,25},{9,1},{17,9},{25,17},{2,26},{10... | collective-permute-start | bytes 1572872 | tf_op jit(solution)/shard_map/gather_kv_weights/ppermute | solution.py:17
  50.4 11.0 %collective-permute-done.20 = bf16[1024,256]{1,0:T(8,128)(2,1)} collective-permute-done((bf16[1024,256]{1,0:T(8,128)(2,1)S(1)}, bf16[1024,256]{1,0:T(8,128)(2,1)}, u32[]{:S(2)}, u32[]{:S(2)}) %collective-permute-start.20) | collective-permute-done | bytes 524320 | tf_op jit(solution)/shard_map/gather_kv_weights/ppermute | solution.py:17
  65.0 5.2 %collective-permute-done.12 = bf16[1024,256]{1,0:T(8,128)(2,1)} collective-permute-done((bf16[1024,256]{1,0:T(8,128)(2,1)S(1)}, bf16[1024,256]{1,0:T(8,128)(2,1)}, u32[]{:S(2)}, u32[]{:S(2)}) %collective-permute-start.12) | collective-permute-done | bytes 524320 | tf_op jit(solution)/shard_map/gather_kv_weights/ppermute | solution.py:17
  70.3 3.3 %collective-permute-start.15 = (bf16[1024,256]{1,0:T(8,128)(2,1)}, bf16[1024,256]{1,0:T(8,128)(2,1)}, u32[]{:S(2)}, u32[]{:S(2)}) collective-permute-start(bf16[1024,256]{1,0:T(8,128)(2,1)} %collective-permute-done.12), channel_id=1, source_target_pairs={{0,6},{2,0},{4,2},{6,4},{1,7},{3,1},{5,3},{7,5},{8,14},{10,8},{12,... | collective-permute-start | bytes 1572872 | tf_op jit(solution)/shard_map/gather_kv_weights/ppermute | solution.py:17
  73.9 2.8 pad_maximum_fusion.2.p0
  76.7 2.6 pad_maximum_fusion.p0
  79.3 9.6 %collective-permute-done.23 = bf16[1024,256]{1,0:T(8,128)(2,1)} collective-permute-done((bf16[1024,256]{1,0:T(8,128)(2,1)}, bf16[1024,256]{1,0:T(8,128)(2,1)}, u32[]{:S(2)}, u32[]{:S(2)}) %collective-permute-start.23) | collective-permute-done | bytes 524320 | tf_op jit(solution)/shard_map/gather_kv_weights/ppermute | solution.py:17
  90.2 2.4 pad_maximum_fusion.3.p1
  92.6 5.0 %collective-permute-start.6 = (bf16[2,4096]{1,0:T(2,128)(2,1)S(1)}, bf16[2,4096]{1,0:T(2,128)(2,1)S(1)}, u32[]{:S(2)}, u32[]{:S(2)}) collective-permute-start(bf16[2,4096]{1,0:T(2,128)(2,1)S(1)} %slice.56), channel_id=1, source_target_pairs={{0,65},{1,66},{2,67},{3,68},{4,69},{5,70},{6,71},{32,97},{33,98},{... | collective-permute-start | bytes 49160 | tf_op jit(solution)/shard_map/gather_tokens/ppermute | solution.py:231
  97.6 3.2 %collective-permute-start.7 = (f32[48,256]{1,0:T(8,128)S(1)}, f32[48,256]{1,0:T(8,128)S(1)}, u32[]{:S(2)}, u32[]{:S(2)}) collective-permute-start(f32[48,256]{1,0:T(8,128)S(1)} %concatenate.30), channel_id=1, source_target_pairs={{0,24},{8,0},{16,8},{24,16},{1,25},{9,1},{17,9},{25,17},{2,26},{10... | collective-permute-start | bytes 147464 | tf_op jit(solution)/shard_map/params/ppermute | solution.py:17
  100.8 9.5 %collective-permute-done.14 = bf16[1024,256]{1,0:T(8,128)(2,1)} collective-permute-done((bf16[1024,256]{1,0:T(8,128)(2,1)S(1)}, bf16[1024,256]{1,0:T(8,128)(2,1)}, u32[]{:S(2)}, u32[]{:S(2)}) %collective-permute-start.14) | collective-permute-done | bytes 524320 | tf_op jit(solution)/shard_map/gather_kv_weights/ppermute | solution.py:17
  110.5 4.0 %collective-permute-start.9 = (f32[48,256]{1,0:T(8,128)S(1)}, f32[48,256]{1,0:T(8,128)S(1)}, u32[]{:S(2)}, u32[]{:S(2)}) collective-permute-start(f32[48,256]{1,0:T(8,128)S(1)} %concatenate.30), channel_id=1, source_target_pairs={{0,16},{8,24},{16,0},{24,8},{1,17},{9,25},{17,1},{25,9},{2,18},{10... | collective-permute-start | bytes 147464 | tf_op jit(solution)/shard_map/params/ppermute | solution.py:17
  114.5 2.7 pad_maximum_fusion.1.p1
  118.7 4.5 %slice_bitcast_fusion = (bf16[4096,256]{1,0:T(8,128)(2,1)}, bf16[4096,256]{1,0:T(8,128)(2,1)}) fusion(bf16[3,4096,256]{2,1,0:T(8,128)(2,1)} %bitcast.45), kind=kLoop, calls=%fused_computation.10 | loop fusion | bytes 8388608 | tf_op jit(solution)/shard_map/keys/squeeze | solution.py:289
  123.6 16.6 %collective-permute-done.1.r2 = bf16[128,4096]{1,0:T(8,128)(2,1)S(1)} collective-permute-done((bf16[128,4096]{1,0:T(8,128)(2,1)S(1)}, bf16[128,4096]{1,0:T(8,128)(2,1)S(1)}, u32[]{:S(2)}, u32[]{:S(2)}) %collective-permute-start.1) | collective-permute-done | bytes 1048608 | tf_op jit(solution)/shard_map/gather_tokens/ppermute | solution.py:17
  144.4 14.8 %collective-permute-done.2.r3 = bf16[128,4096]{1,0:T(8,128)(2,1)} collective-permute-done((bf16[128,4096]{1,0:T(8,128)(2,1)S(1)}, bf16[128,4096]{1,0:T(8,128)(2,1)}, u32[]{:S(2)}, u32[]{:S(2)}) %collective-permute-start.2) | collective-permute-done | bytes 1048608 | tf_op jit(solution)/shard_map/gather_tokens/ppermute | solution.py:17
  159.2 9.9 %keys.1.k_ref = bf16[4,528,256]{2,1,0:T(8,128)(2,1)S(1)} custom-call(s32[4]{0:T(128)S(1)} %pad_add_fusion.1.quarter, bf16[4096,256]{1,0:T(8,128)(2,1)} %get-tuple-element.33.own_ref, bf16[3,1024,256]{2,1,0:T(8,128)(2,1)} %pad_maximum_fusion.2.p0, bf16[3,1024,256]{2,1,0:T(8,128)(2,1)} %pad_maximum_fusion.3.p1, ...), custom_call_target="tpu_custom_call" | custom-call | tf_op jit(solution)/shard_map/keys/keys/pallas_call | solution.py:277
  170.0 17.1 %values_filter.1 = (f32[4,2,4,16,8,128]{5,4,3,2,1,0:T(8,128)}, f32[4,2,4,16,8,128]{5,4,3,2,1,0:T(8,128)}, f32[4,2,4,16,128]{4,3,2,1,0:T(8,128)S(1)}) custom-call(s32[4]{0:T(128)S(1)} %pad_add_fusion.1.quarter, bf16[4096,256]{1,0:T(8,128)(2,1)} %get-tuple-element.34.own_ref, bf16[3,1024,256]{2,1,0:T(8,128)(2,1)} %pad_maximum_fusion.p0, ...), custom_call_target="tpu_custom_call" | custom-call | tf_op jit(solution)/shard_map/values_filter/values_filter/pallas_call | solution.py:291
  190.4 2.3 collective-permute-start.27
  192.8 4.7 %collective-permute-start.28 = (bf16[4,2,4,16,128]{4,3,2,1,0:T(8,128)(2,1)S(1)}, bf16[4,2,4,16,128]{4,3,2,1,0:T(8,128)(2,1)S(1)}, u32[]{:S(2)}, u32[]{:S(2)}) collective-permute-start(bf16[4,2,4,16,128]{4,3,2,1,0:T(8,128)(2,1)S(1)} %fusion.9), channel_id=1, source_target_pairs={{0,4},{2,6},{1,5},{3,7},{8,12},{10,14},{9,13},{11,15},{16,20},{18,... | collective-permute-start | bytes 393224 | tf_op jit(solution)/shard_map/states/ppermute | solution.py:22
  204.2 3.0 %entering.1.y_ref = f32[4,2,4,16,8,128]{5,4,3,2,1,0:T(8,128)S(1)} custom-call(f32[4,2,4,16,8,128]{5,4,3,2,1,0:T(8,128)S(1)} %copy-done.2, f32[4,2,4,16,8,128]{5,4,3,2,1,0:T(8,128)S(1)} %copy-done.3, f32[4,2,4,16,128]{4,3,2,1,0:T(8,128)S(1)} %add_select_fusion.in_ref, f32[4,2,16,128]{3,2,1,0:T(8,128)S(1)} %copy-done.5, f32[4,2,16,128]{3,2,1,0:T(8,128)S(1)} %copy-done.9, ...), custom_call_target="tpu_custom_call" | custom-call | tf_op jit(solution)/shard_map/entering/entering/pallas_call | solution.py:330
  210.1 10.7 %query_gate.1.g_ref = bf16[4,4,128,256]{3,2,1,0:T(8,128)(2,1)S(1)} custom-call(s32[4]{0:T(128)S(1)} %pad_add_fusion.order, bf16[4,8,1024,256]{3,2,1,0:T(8,128)(2,1)} %bitcast.43, bf16[128,4096]{1,0:T(8,128)(2,1)S(1)} %fusion.2.r0, bf16[128,4096]{1,0:T(8,128)(2,1)S(1)} %collective-permute-done.r1, bf16[128,4096]{1,0:T(8,128)(2,1)S(1)} %collective-permute-done.1.r2, ...), custom_call_target="tpu_custom_call" | custom-call | tf_op jit(solution)/shard_map/query_gate/query_gate/pallas_call | solution.py:348
  220.8 9.5 %project_out.1 = (bf16[128,4096]{1,0:T(8,128)(2,1)S(1)}, bf16[128,4096]{1,0:T(8,128)(2,1)S(1)}, bf16[128,4096]{1,0:T(8,128)(2,1)S(1)}, bf16[128,4096]{1,0:T(8,128)(2,1)S(1)}) custom-call(s32[4]{0:T(128)S(1)} %pad_add_fusion.order, bf16[4,4,128,256]{3,2,1,0:T(8,128)(2,1)S(1)} %query_gate.1.g_ref, bf16[4,8,1024,256]{3,2,1,0:T(8,128)(2,1)} %bitcast.44), custom_call_target="tpu_custom_call" | custom-call | tf_op jit(solution)/shard_map/project_out/project_out/pallas_call | solution.py:366
  230.3 4.3 %collective-permute-start.30 = (bf16[128,4096]{1,0:T(8,128)(2,1)S(1)}, bf16[128,4096]{1,0:T(8,128)(2,1)S(1)}, u32[]{:S(2)}, u32[]{:S(2)}) collective-permute-start(bf16[128,4096]{1,0:T(8,128)(2,1)S(1)} %get-tuple-element.28), channel_id=1, source_target_pairs={{0,32},{32,64},{64,96},{96,0},{1,33},{33,65},{65,97},{97,1},{2,34}... | collective-permute-start | bytes 3145736 | tf_op jit(solution)/shard_map/sum_parts/ppermute | solution.py:17
  236.2 42.5 %collective-permute-done.30 = bf16[128,4096]{1,0:T(8,128)(2,1)S(1)} collective-permute-done((bf16[128,4096]{1,0:T(8,128)(2,1)S(1)}, bf16[128,4096]{1,0:T(8,128)(2,1)S(1)}, u32[]{:S(2)}, u32[]{:S(2)}) %collective-permute-start.30) | collective-permute-done | bytes 1048608 | tf_op jit(solution)/shard_map/sum_parts/ppermute | solution.py:17
  278.7 3.4 %collective-permute-done.31 = bf16[128,4096]{1,0:T(8,128)(2,1)S(1)} collective-permute-done((bf16[128,4096]{1,0:T(8,128)(2,1)S(1)}, bf16[128,4096]{1,0:T(8,128)(2,1)S(1)}, u32[]{:S(2)}, u32[]{:S(2)}) %collective-permute-start.31) | collective-permute-done | bytes 1048608 | tf_op jit(solution)/shard_map/sum_parts/ppermute | solution.py:17
  (147 shorter events, 41.1 us)
Async XLA Ops:
  6.5 202.0 %all-gather.3.cloned.1.call-start = ((), (), s32[]{:S(2)}) async-start(), calls=%async_computation | async-start | bytes 17301504 | tf_op jit(solution)/shard_map/background_weights/all_gather | solution.py:212
  10.8 18.0 %collective-permute-start.19 = (bf16[1024,256]{1,0:T(8,128)(2,1)S(1)}, bf16[1024,256]{1,0:T(8,128)(2,1)S(1)}, u32[]{:S(2)}, u32[]{:S(2)}) collective-permute-start(bf16[1024,256]{1,0:T(8,128)(2,1)S(1)} %get-tuple-element.31), channel_id=1, source_target_pairs={{0,8},{8,16},{16,24},{24,0},{1,9},{9,17},{17,25},{25,1},{2,10},{10... | collective-permute-start | bytes 1572872 | tf_op jit(solution)/shard_map/gather_kv_weights/ppermute | solution.py:17
  12.8 24.0 %collective-permute-start.18 = (bf16[1024,256]{1,0:T(8,128)(2,1)S(1)}, bf16[1024,256]{1,0:T(8,128)(2,1)S(1)}, u32[]{:S(2)}, u32[]{:S(2)}) collective-permute-start(bf16[1024,256]{1,0:T(8,128)(2,1)S(1)} %get-tuple-element.31), channel_id=1, source_target_pairs={{0,24},{8,0},{16,8},{24,16},{1,25},{9,1},{17,9},{25,17},{2,26},{10... | collective-permute-start | bytes 1572872 | tf_op jit(solution)/shard_map/gather_kv_weights/ppermute | solution.py:17
  15.0 31.0 %collective-permute-start.10 = (bf16[1024,256]{1,0:T(8,128)(2,1)S(1)}, bf16[1024,256]{1,0:T(8,128)(2,1)S(1)}, u32[]{:S(2)}, u32[]{:S(2)}) collective-permute-start(bf16[1024,256]{1,0:T(8,128)(2,1)S(1)} %get-tuple-element.32), channel_id=1, source_target_pairs={{0,24},{8,0},{16,8},{24,16},{1,25},{9,1},{17,9},{25,17},{2,26},{10... | collective-permute-start | bytes 1572872 | tf_op jit(solution)/shard_map/gather_kv_weights/ppermute | solution.py:17
  16.9 32.6 %collective-permute-start.11 = (bf16[1024,256]{1,0:T(8,128)(2,1)S(1)}, bf16[1024,256]{1,0:T(8,128)(2,1)S(1)}, u32[]{:S(2)}, u32[]{:S(2)}) collective-permute-start(bf16[1024,256]{1,0:T(8,128)(2,1)S(1)} %get-tuple-element.32), channel_id=1, source_target_pairs={{0,8},{8,16},{16,24},{24,0},{1,9},{9,17},{17,25},{25,1},{2,10},{10... | collective-permute-start | bytes 1572872 | tf_op jit(solution)/shard_map/gather_kv_weights/ppermute | solution.py:17
  28.8 32.6 %collective-permute-start.20 = (bf16[1024,256]{1,0:T(8,128)(2,1)S(1)}, bf16[1024,256]{1,0:T(8,128)(2,1)}, u32[]{:S(2)}, u32[]{:S(2)}) collective-permute-start(bf16[1024,256]{1,0:T(8,128)(2,1)S(1)} %collective-permute-done.19), channel_id=1, source_target_pairs={{0,8},{8,16},{16,24},{24,0},{1,9},{9,17},{17,25},{25,1},{2,10},{10... | collective-permute-start | bytes 1572872 | tf_op jit(solution)/shard_map/gather_kv_weights/ppermute | solution.py:17
  32.0 8.2 %collective-permute-start.4 = (bf16[2,4096]{1,0:T(2,128)(2,1)S(1)}, bf16[2,4096]{1,0:T(2,128)(2,1)S(1)}, u32[]{:S(2)}, u32[]{:S(2)}) collective-permute-start(bf16[2,4096]{1,0:T(2,128)(2,1)S(1)} %slice.56), channel_id=1, source_target_pairs={{0,97},{1,98},{2,99},{3,100},{4,101},{5,102},{6,103},{32,1},{33,2}... | collective-permute-start | bytes 49160 | tf_op jit(solution)/shard_map/gather_tokens/ppermute | solution.py:231
  36.8 26.2 %collective-permute-start.21 = (bf16[1024,256]{1,0:T(8,128)(2,1)S(1)}, bf16[1024,256]{1,0:T(8,128)(2,1)S(1)}, u32[]{:S(2)}, u32[]{:S(2)}) collective-permute-start(bf16[1024,256]{1,0:T(8,128)(2,1)S(1)} %collective-permute-done.18), channel_id=1, source_target_pairs={{0,6},{2,0},{4,2},{6,4},{1,7},{3,1},{5,3},{7,5},{8,14},{10,8},{12,... | collective-permute-start | bytes 1572872 | tf_op jit(solution)/shard_map/gather_kv_weights/ppermute | solution.py:17
  40.3 24.4 %collective-permute-start.22 = (bf16[1024,256]{1,0:T(8,128)(2,1)S(1)}, bf16[1024,256]{1,0:T(8,128)(2,1)S(1)}, u32[]{:S(2)}, u32[]{:S(2)}) collective-permute-start(bf16[1024,256]{1,0:T(8,128)(2,1)S(1)} %collective-permute-done.19), channel_id=1, source_target_pairs={{0,2},{2,4},{4,6},{6,0},{1,3},{3,5},{5,7},{7,1},{8,10},{10,12},{12... | collective-permute-start | bytes 1572872 | tf_op jit(solution)/shard_map/gather_kv_weights/ppermute | solution.py:17
  46.0 24.2 %collective-permute-start.12 = (bf16[1024,256]{1,0:T(8,128)(2,1)S(1)}, bf16[1024,256]{1,0:T(8,128)(2,1)}, u32[]{:S(2)}, u32[]{:S(2)}) collective-permute-start(bf16[1024,256]{1,0:T(8,128)(2,1)S(1)} %collective-permute-done.10), channel_id=1, source_target_pairs={{0,24},{8,0},{16,8},{24,16},{1,25},{9,1},{17,9},{25,17},{2,26},{10... | collective-permute-start | bytes 1572872 | tf_op jit(solution)/shard_map/gather_kv_weights/ppermute | solution.py:17
  49.5 68.8 %collective-permute-start = (bf16[128,4096]{1,0:T(8,128)(2,1)S(1)}, bf16[128,4096]{1,0:T(8,128)(2,1)S(1)}, u32[]{:S(2)}, u32[]{:S(2)}) collective-permute-start(bf16[128,4096]{1,0:T(8,128)(2,1)S(1)} %fusion.2.r0), channel_id=1, source_target_pairs={{0,96},{32,0},{64,32},{96,64},{1,97},{33,1},{65,33},{97,65},{2,98}... | collective-permute-start | bytes 3145736 | tf_op jit(solution)/shard_map/gather_tokens/ppermute | solution.py:17
  61.3 27.6 %collective-permute-start.23 = (bf16[1024,256]{1,0:T(8,128)(2,1)}, bf16[1024,256]{1,0:T(8,128)(2,1)}, u32[]{:S(2)}, u32[]{:S(2)}) collective-permute-start(bf16[1024,256]{1,0:T(8,128)(2,1)} %collective-permute-done.20), channel_id=1, source_target_pairs={{0,2},{2,4},{4,6},{6,0},{1,3},{3,5},{5,7},{7,1},{8,10},{10,12},{12... | collective-permute-start | bytes 1572872 | tf_op jit(solution)/shard_map/gather_kv_weights/ppermute | solution.py:17
  63.0 34.6 %collective-permute-start.13 = (bf16[1024,256]{1,0:T(8,128)(2,1)S(1)}, bf16[1024,256]{1,0:T(8,128)(2,1)}, u32[]{:S(2)}, u32[]{:S(2)}) collective-permute-start(bf16[1024,256]{1,0:T(8,128)(2,1)S(1)} %collective-permute-done.10), channel_id=1, source_target_pairs={{0,6},{2,0},{4,2},{6,4},{1,7},{3,1},{5,3},{7,5},{8,14},{10,8},{12,... | collective-permute-start | bytes 1572872 | tf_op jit(solution)/shard_map/gather_kv_weights/ppermute | solution.py:17
  64.7 45.6 %collective-permute-start.14 = (bf16[1024,256]{1,0:T(8,128)(2,1)S(1)}, bf16[1024,256]{1,0:T(8,128)(2,1)}, u32[]{:S(2)}, u32[]{:S(2)}) collective-permute-start(bf16[1024,256]{1,0:T(8,128)(2,1)S(1)} %collective-permute-done.11), channel_id=1, source_target_pairs={{0,2},{2,4},{4,6},{6,0},{1,3},{3,5},{5,7},{7,1},{8,10},{10,12},{12... | collective-permute-start | bytes 1572872 | tf_op jit(solution)/shard_map/gather_kv_weights/ppermute | solution.py:17
  70.3 40.3 %collective-permute-start.15 = (bf16[1024,256]{1,0:T(8,128)(2,1)}, bf16[1024,256]{1,0:T(8,128)(2,1)}, u32[]{:S(2)}, u32[]{:S(2)}) collective-permute-start(bf16[1024,256]{1,0:T(8,128)(2,1)} %collective-permute-done.12), channel_id=1, source_target_pairs={{0,6},{2,0},{4,2},{6,4},{1,7},{3,1},{5,3},{7,5},{8,14},{10,8},{12,... | collective-permute-start | bytes 1572872 | tf_op jit(solution)/shard_map/gather_kv_weights/ppermute | solution.py:17
  88.9 3.7 %collective-permute-start.5 = (bf16[2,4096]{1,0:T(2,128)(2,1)S(1)}, bf16[2,4096]{1,0:T(2,128)(2,1)S(1)}, u32[]{:S(2)}, u32[]{:S(2)}) collective-permute-start(bf16[2,4096]{1,0:T(2,128)(2,1)S(1)} %slice.56), channel_id=1, source_target_pairs={{0,33},{1,34},{2,35},{3,36},{4,37},{5,38},{6,39},{32,65},{33,66},{... | collective-permute-start | bytes 49160 | tf_op jit(solution)/shard_map/gather_tokens/ppermute | solution.py:231
  92.6 24.6 %collective-permute-start.6 = (bf16[2,4096]{1,0:T(2,128)(2,1)S(1)}, bf16[2,4096]{1,0:T(2,128)(2,1)S(1)}, u32[]{:S(2)}, u32[]{:S(2)}) collective-permute-start(bf16[2,4096]{1,0:T(2,128)(2,1)S(1)} %slice.56), channel_id=1, source_target_pairs={{0,65},{1,66},{2,67},{3,68},{4,69},{5,70},{6,71},{32,97},{33,98},{... | collective-permute-start | bytes 49160 | tf_op jit(solution)/shard_map/gather_tokens/ppermute | solution.py:231
  97.6 20.0 %collective-permute-start.7 = (f32[48,256]{1,0:T(8,128)S(1)}, f32[48,256]{1,0:T(8,128)S(1)}, u32[]{:S(2)}, u32[]{:S(2)}) collective-permute-start(f32[48,256]{1,0:T(8,128)S(1)} %concatenate.30), channel_id=1, source_target_pairs={{0,24},{8,0},{16,8},{24,16},{1,25},{9,1},{17,9},{25,17},{2,26},{10... | collective-permute-start | bytes 147464 | tf_op jit(solution)/shard_map/params/ppermute | solution.py:17
  110.4 7.3 %collective-permute-start.8 = (f32[48,256]{1,0:T(8,128)S(1)}, f32[48,256]{1,0:T(8,128)S(1)}, u32[]{:S(2)}, u32[]{:S(2)}) collective-permute-start(f32[48,256]{1,0:T(8,128)S(1)} %concatenate.30), channel_id=1, source_target_pairs={{0,8},{8,16},{16,24},{24,0},{1,9},{9,17},{17,25},{25,1},{2,10},{10... | collective-permute-start | bytes 147464 | tf_op jit(solution)/shard_map/params/ppermute | solution.py:17
  110.5 7.7 %collective-permute-start.9 = (f32[48,256]{1,0:T(8,128)S(1)}, f32[48,256]{1,0:T(8,128)S(1)}, u32[]{:S(2)}, u32[]{:S(2)}) collective-permute-start(f32[48,256]{1,0:T(8,128)S(1)} %concatenate.30), channel_id=1, source_target_pairs={{0,16},{8,24},{16,0},{24,8},{1,17},{9,25},{17,1},{25,9},{2,18},{10... | collective-permute-start | bytes 147464 | tf_op jit(solution)/shard_map/params/ppermute | solution.py:17
  117.2 22.9 %collective-permute-start.1 = (bf16[128,4096]{1,0:T(8,128)(2,1)S(1)}, bf16[128,4096]{1,0:T(8,128)(2,1)S(1)}, u32[]{:S(2)}, u32[]{:S(2)}) collective-permute-start(bf16[128,4096]{1,0:T(8,128)(2,1)S(1)} %fusion.2.r0), channel_id=1, source_target_pairs={{0,32},{32,64},{64,96},{96,0},{1,33},{33,65},{65,97},{97,1},{2,34}... | collective-permute-start | bytes 3145736 | tf_op jit(solution)/shard_map/gather_tokens/ppermute | solution.py:17
  117.7 41.5 %collective-permute-start.24 = (bf16[3,1024,256]{2,1,0:T(8,128)(2,1)}, bf16[3,1024,256]{2,1,0:T(8,128)(2,1)}, u32[]{:S(2)}, u32[]{:S(2)}) collective-permute-start(bf16[3,1024,256]{2,1,0:T(8,128)(2,1)} %pad_maximum_fusion.2.p0), channel_id=1, source_target_pairs={{0,1},{1,0},{2,3},{3,2},{4,5},{5,4},{6,7},{7,6},{8,9},{9,8},{10,11... | collective-permute-start | bytes 4718600 | tf_op jit(solution)/shard_map/gather_kv_weights/ppermute | solution.py:17
  117.7 51.4 %collective-permute-start.16 = (bf16[3,1024,256]{2,1,0:T(8,128)(2,1)}, bf16[3,1024,256]{2,1,0:T(8,128)(2,1)}, u32[]{:S(2)}, u32[]{:S(2)}) collective-permute-start(bf16[3,1024,256]{2,1,0:T(8,128)(2,1)} %pad_maximum_fusion.p0), channel_id=1, source_target_pairs={{0,1},{1,0},{2,3},{3,2},{4,5},{5,4},{6,7},{7,6},{8,9},{9,8},{10,11... | collective-permute-start | bytes 4718600 | tf_op jit(solution)/shard_map/gather_kv_weights/ppermute | solution.py:17
  118.2 41.0 %collective-permute-start.25 = (bf16[3,1024,256]{2,1,0:T(8,128)(2,1)}, bf16[3,1024,256]{2,1,0:T(8,128)(2,1)}, u32[]{:S(2)}, u32[]{:S(2)}) collective-permute-start(bf16[3,1024,256]{2,1,0:T(8,128)(2,1)} %pad_maximum_fusion.3.p1), channel_id=1, source_target_pairs={{0,1},{1,0},{2,3},{3,2},{4,5},{5,4},{6,7},{7,6},{8,9},{9,8},{10,11... | collective-permute-start | bytes 4718600 | tf_op jit(solution)/shard_map/gather_kv_weights/ppermute | solution.py:17
  118.3 50.8 %collective-permute-start.17 = (bf16[3,1024,256]{2,1,0:T(8,128)(2,1)}, bf16[3,1024,256]{2,1,0:T(8,128)(2,1)}, u32[]{:S(2)}, u32[]{:S(2)}) collective-permute-start(bf16[3,1024,256]{2,1,0:T(8,128)(2,1)} %pad_maximum_fusion.1.p1), channel_id=1, source_target_pairs={{0,1},{1,0},{2,3},{3,2},{4,5},{5,4},{6,7},{7,6},{8,9},{9,8},{10,11... | collective-permute-start | bytes 4718600 | tf_op jit(solution)/shard_map/gather_kv_weights/ppermute | solution.py:17
  140.2 19.0 %collective-permute-start.2 = (bf16[128,4096]{1,0:T(8,128)(2,1)S(1)}, bf16[128,4096]{1,0:T(8,128)(2,1)}, u32[]{:S(2)}, u32[]{:S(2)}) collective-permute-start(bf16[128,4096]{1,0:T(8,128)(2,1)S(1)} %fusion.2.r0), channel_id=1, source_target_pairs={{0,64},{32,96},{64,0},{96,32},{1,65},{33,97},{65,1},{97,33},{2,66}... | collective-permute-start | bytes 3145736 | tf_op jit(solution)/shard_map/gather_tokens/ppermute | solution.py:17
  190.4 9.3 %collective-permute-start.27 = (bf16[4,2,4,16,128]{4,3,2,1,0:T(8,128)(2,1)S(1)}, bf16[4,2,4,16,128]{4,3,2,1,0:T(8,128)(2,1)S(1)}, u32[]{:S(2)}, u32[]{:S(2)}) collective-permute-start(bf16[4,2,4,16,128]{4,3,2,1,0:T(8,128)(2,1)S(1)} %fusion.9), channel_id=1, source_target_pairs={{0,2},{2,4},{4,6},{1,3},{3,5},{5,7},{8,10},{10,12},{12,14},{9,11},... | collective-permute-start | bytes 393224 | tf_op jit(solution)/shard_map/states/ppermute | solution.py:22
  192.8 7.4 %collective-permute-start.28 = (bf16[4,2,4,16,128]{4,3,2,1,0:T(8,128)(2,1)S(1)}, bf16[4,2,4,16,128]{4,3,2,1,0:T(8,128)(2,1)S(1)}, u32[]{:S(2)}, u32[]{:S(2)}) collective-permute-start(bf16[4,2,4,16,128]{4,3,2,1,0:T(8,128)(2,1)S(1)} %fusion.9), channel_id=1, source_target_pairs={{0,4},{2,6},{1,5},{3,7},{8,12},{10,14},{9,13},{11,15},{16,20},{18,... | collective-permute-start | bytes 393224 | tf_op jit(solution)/shard_map/states/ppermute | solution.py:22
  197.4 4.1 %collective-permute-start.29 = (bf16[4,2,4,16,128]{4,3,2,1,0:T(8,128)(2,1)S(1)}, bf16[4,2,4,16,128]{4,3,2,1,0:T(8,128)(2,1)S(1)}, u32[]{:S(2)}, u32[]{:S(2)}) collective-permute-start(bf16[4,2,4,16,128]{4,3,2,1,0:T(8,128)(2,1)S(1)} %fusion.9), channel_id=1, source_target_pairs={{0,6},{1,7},{8,14},{9,15},{16,22},{17,23},{24,30},{25,31},{32,38},... | collective-permute-start | bytes 393224 | tf_op jit(solution)/shard_map/states/ppermute | solution.py:22
  230.3 48.4 %collective-permute-start.30 = (bf16[128,4096]{1,0:T(8,128)(2,1)S(1)}, bf16[128,4096]{1,0:T(8,128)(2,1)S(1)}, u32[]{:S(2)}, u32[]{:S(2)}) collective-permute-start(bf16[128,4096]{1,0:T(8,128)(2,1)S(1)} %get-tuple-element.28), channel_id=1, source_target_pairs={{0,32},{32,64},{64,96},{96,0},{1,33},{33,65},{65,97},{97,1},{2,34}... | collective-permute-start | bytes 3145736 | tf_op jit(solution)/shard_map/sum_parts/ppermute | solution.py:17
  234.6 47.5 %collective-permute-start.31 = (bf16[128,4096]{1,0:T(8,128)(2,1)S(1)}, bf16[128,4096]{1,0:T(8,128)(2,1)S(1)}, u32[]{:S(2)}, u32[]{:S(2)}) collective-permute-start(bf16[128,4096]{1,0:T(8,128)(2,1)S(1)} %get-tuple-element.29), channel_id=1, source_target_pairs={{0,96},{32,0},{64,32},{96,64},{1,97},{33,1},{65,33},{97,65},{2,98}... | collective-permute-start | bytes 3145736 | tf_op jit(solution)/shard_map/sum_parts/ppermute | solution.py:17
  234.6 47.5 %collective-permute-start.32 = (bf16[128,4096]{1,0:T(8,128)(2,1)S(1)}, bf16[128,4096]{1,0:T(8,128)(2,1)S(1)}, u32[]{:S(2)}, u32[]{:S(2)}) collective-permute-start(bf16[128,4096]{1,0:T(8,128)(2,1)S(1)} %get-tuple-element.30), channel_id=1, source_target_pairs={{0,64},{32,96},{64,0},{96,32},{1,65},{33,97},{65,1},{97,33},{2,66}... | collective-permute-start | bytes 3145736 | tf_op jit(solution)/shard_map/sum_parts/ppermute | solution.py:17
  (31 other events, 642.0 us)
Sparse Core Ops, SparseCore 0:
  9.6 104.5 all-gather.2

commit v3 on v0

v3 whole, which is shorter than its diff:
```python
import functools

import jax
import jax.numpy as jnp
from jax import lax
from jax.experimental import pallas as pl
from jax.experimental.pallas import tpu as pltpu
from jax.sharding import Mesh, PartitionSpec as P

F32 = jnp.float32
BF16 = jnp.bfloat16
OFFSETS = (0, 1, 3, 2)
CHUNK = 16
HEAD = 16
QUERY, KEY, VALUE = 0, 1, 2


def from_ahead(value, axis, steps):
    count = lax.axis_size(axis)
    return lax.ppermute(value, axis, [(i, (i - steps) % count) for i in range(count)])


def from_behind(value, axis, steps):
    count = lax.axis_size(axis)
    return lax.ppermute(value, axis, [(i, i + steps) for i in range(count - steps)])


def gather_along(value, axis):
    return [value] + [from_ahead(value, axis, step) for step in OFFSETS[1:]]


def compiler_params():
    return pltpu.CompilerParams(vmem_limit_bytes=60 * 1024 * 1024)


def norm_kernel(edge_ref, tokens_ref, gain_ref, out_ref, natural):
    def normed(rows):
        values = rows.astype(F32)
        inverse_rms = lax.rsqrt(jnp.mean(values * values, axis=-1, keepdims=True) + 1e-06)
        return values * inverse_rms * gain_ref[...]

    out_ref[:HEAD] = normed(edge_ref[...]).astype(BF16)
    values = normed(tokens_ref[0])
    for lane in range(natural.shape[0]):
        cols = slice(lane * 128, (lane + 1) * 128)
        natural[lane] = values[:, cols]
        for t in range(0, CHUNK, 2):
            pair = [natural[lane, pl.ds(t + i, 8, stride=CHUNK), :] for i in range(2)]
            out_ref[HEAD + 8 * t : HEAD + 8 * t + 16, cols] = jnp.concatenate(pair, axis=0).astype(BF16)


def pack_kernel(taps_ref, decay_ref, res_ref, skip_ref, out_ref):
    out_ref[...] = jnp.zeros_like(out_ref)
    for j in range(3):
        out_ref[3 * j : 3 * j + 3] = taps_ref[j]
    out_ref[16:32] = decay_ref[...]
    out_ref[32:48] = res_ref[...]
    out_ref[9:10] = skip_ref[...]


def coefficient_kernel(p0, p1, p2, p3, taps_ref, kern_ref, pole_ref, jump_ref, res_ref, reach_ref, span_ref):
    chunk_of = lax.broadcasted_iota(jnp.int32, (8, 128), 0).astype(F32) * CHUNK
    for r, packed in enumerate((p0, p1, p2, p3)):
        for lane in range(2):
            cols = slice(lane * 128, (lane + 1) * 128)
            decay, res = packed[16:32, cols], packed[32:48, cols]
            taps_ref[r, lane] = packed[0:16, cols]
            pole_ref[r, lane] = jnp.exp(-decay)
            res_ref[r, lane] = res
            span_ref[r, lane] = jnp.exp(-decay * (8 * CHUNK))
            for j in range(3):
                jump_ref[r, lane, j] = jnp.exp(-decay * (CHUNK << j))
            for d in range(CHUNK):
                row = jnp.sum(res * jnp.exp(-decay * d), axis=0, keepdims=True)
                kern_ref[r, lane, d : d + 1] = row + packed[9:10, cols] if d == 0 else row
            for n in range(16):
                reach_ref[r, lane, n] = jnp.exp(-wide(decay[n : n + 1]) * chunk_of)


def copy(source, target, sem):
    pltpu.make_async_copy(source, target, sem).start()


def wait_for(ref, sem):
    pltpu.make_async_copy(ref, ref, sem).wait()


def start_rows(row_refs, x, sem):
    high = row_refs[0].shape[0]
    for i, ref in enumerate(row_refs):
        copy(ref, x.at[pl.ds(i * high, high)], sem)


def start_weights(order, w_ref, stream, block, w, sem):
    if len(w_ref.shape) == 3:
        copy(w_ref.at[stream], w, sem)
    else:
        depth = w_ref.shape[3]
        for part in range(8):
            copy(w_ref.at[order[block], part, stream], w.at[pl.ds(part * depth, depth)], sem)


def dot(a, b):
    return jnp.dot(a, b, preferred_element_type=F32)


def project(x, w, scratch):
    total = dot(x[...], w[...]).astype(BF16).astype(F32)
    lanes, seqs = scratch.shape[:2]
    first_row = lax.broadcasted_iota(jnp.int32, (8, 128), 0) == 0
    for lane in range(lanes):
        cols = slice(lane * 128, (lane + 1) * 128)
        for s in range(seqs):
            first = s * (HEAD + 8 * CHUNK) + HEAD
            edge = total[first - 8 : first, cols]
            for back in (1, 2):
                last = total[first + 8 * (CHUNK - back) : first + 8 * (CHUNK - back) + 8, cols]
                scratch[lane, s, 2 - back] = jnp.where(first_row, pltpu.roll(edge, back, 0), pltpu.roll(last, 1, 0))
            scratch[lane, s, 2:] = total[first : first + 8 * CHUNK, cols].reshape(CHUNK, 8, 128)


def both(first, second):
    return jnp.concatenate([first, second], axis=0).astype(BF16)


def halves(pair):
    pair = pair.astype(F32)
    return pair[:8], pair[8:]


def wide(row):
    return jnp.broadcast_to(row, (8, 128))


def each_unit(scratch, body):
    lanes, seqs = scratch.shape[:2]

    def step(i, carry):
        body(i // seqs, i % seqs)
        return carry

    lax.fori_loop(0, lanes * seqs, step, 0)


def kv_kernel(first, seqs, order, w_ref, *refs):
    row_refs, refs = refs[:seqs], refs[seqs:]
    taps_ref, kern_ref, pole_ref, jump_ref, y_out, e_out, t_ref, x, w, fk, fv, ys, es, row_sem, w_sems, out_sems = refs
    blocks = w.shape[0]
    for block in range(blocks):
        for i, stream in enumerate((KEY, VALUE)):
            start_weights(order, w_ref, stream, block + first, w.at[block, i], w_sems.at[block])
        if block == 0:
            start_rows(row_refs, x, row_sem)
    first_row = lax.broadcasted_iota(jnp.int32, (8, 128), 0)
    wait_for(x, row_sem)

    def each_block(block, carry):
        wait_for(w.at[block], w_sems.at[block])
        project(x, w.at[block, 0], fk)
        project(x, w.at[block, 1], fv)
        c = block + first

        def unit(lane, s):
            tap = lambda j, stream: wide(taps_ref[c, lane, pl.ds(3 * j + stream, 1), :])
            kt = [tap(j, KEY) for j in range(3)]
            vt = [tap(j, VALUE) for j in range(3)]
            kx = [fk[lane, s, t] for t in range(CHUNK + 2)]
            vx = [fv[lane, s, t] for t in range(CHUNK + 2)]
            xs = []
            for t in range(CHUNK):
                k = kt[0] * kx[t + 2] + kt[1] * kx[t + 1] + kt[2] * kx[t]
                v = vt[0] * vx[t + 2] + vt[1] * vx[t + 1] + vt[2] * vx[t]
                xs.append(k * v)
            kern = [wide(kern_ref[c, lane, pl.ds(d, 1), :]) for d in range(CHUNK)]
            for t in range(0, CHUNK, 2):
                pair = []
                for u in (t, t + 1):
                    y = kern[0] * xs[u]
                    for d in range(1, u + 1):
                        y += kern[d] * xs[u - d]
                    pair.append(y)
                ys[block, lane, s, t // 2] = both(*pair)
            for n in range(0, 16, 2):
                pair = []
                for m in (n, n + 1):
                    pole = wide(pole_ref[c, lane, pl.ds(m, 1), :])
                    state = xs[0]
                    for t in range(1, CHUNK):
                        state = pole * state + xs[t]
                    for j, step in enumerate((1, 2, 4)):
                        jump = wide(jump_ref[c, lane, j, pl.ds(m, 1), :])
                        moved = jnp.where(first_row >= step, pltpu.roll(state, step, 0), 0.0)
                        state = state + jump * moved
                    pair.append(jnp.where(first_row >= 1, pltpu.roll(state, 1, 0), 0.0))
                    t_ref[block, lane, s, pl.ds(m, 1), :] = state[7:8, :]
                es[block, lane, s, n // 2] = both(*pair)

        each_unit(fk, unit)
        copy(ys.at[block], y_out.at[block], out_sems.at[0])
        copy(es.at[block], e_out.at[block], out_sems.at[1])
        return carry

    lax.fori_loop(0, blocks, each_block, 0)
    wait_for(ys, out_sems.at[0])
    wait_for(es, out_sems.at[1])


def q_kernel(first, seqs, order, w_ref, *refs):
    row_refs, refs = refs[:seqs], refs[seqs:]
    taps_ref, q_out, x, w, fq, qs, row_sem, w_sems, out_sem = refs
    blocks = w.shape[0]
    for block in range(blocks):
        start_weights(order, w_ref, QUERY, block + first, w.at[block], w_sems.at[block])
        if block == 0:
            start_rows(row_refs, x, row_sem)
    wait_for(x, row_sem)

    def each_block(block, carry):
        wait_for(w.at[block], w_sems.at[block])
        project(x, w.at[block], fq)

        def unit(lane, s):
            qt = [wide(taps_ref[block + first, lane, pl.ds(3 * j + QUERY, 1), :]) for j in range(3)]
            qx = [fq[lane, s, t] for t in range(CHUNK + 2)]
            q = [qt[0] * qx[t + 2] + qt[1] * qx[t + 1] + qt[2] * qx[t] for t in range(CHUNK)]
            for t in range(0, CHUNK, 2):
                qs[block, lane, s, t // 2] = both(q[t], q[t + 1])

        each_unit(fq, unit)
        copy(qs.at[block], q_out.at[block], out_sem)
        return carry

    lax.fori_loop(0, blocks, each_block, 0)
    wait_for(qs, out_sem)


def gate_kernel(y_ref, e_ref, q_ref, in_ref, pole_ref, res_ref, reach_ref, out_ref, gated):
    def unit(s, carry):
        poles, states = [], []
        for n in range(0, 16, 2):
            for m, state in zip((n, n + 1), halves(e_ref[0, 0, s, n // 2])):
                pole = wide(pole_ref[0, 0, pl.ds(m, 1), :])
                state = state + reach_ref[0, 0, m] * wide(in_ref[0, 0, s, pl.ds(m, 1), :])
                poles.append(pole)
                states.append(wide(res_ref[0, 0, pl.ds(m, 1), :]) * pole * state)
        for t in range(0, CHUNK, 2):
            for u, y, q in zip((t, t + 1), halves(y_ref[0, 0, s, t // 2]), halves(q_ref[0, 0, s, t // 2])):
                total = y
                for n in range(16):
                    total += states[n]
                gated[s, pl.ds(u, 8, stride=CHUNK), :] = total * q
                states = [pole * state for pole, state in zip(poles, states)]
        return carry

    lax.fori_loop(0, gated.shape[0], unit, 0)
    out_ref[0] = gated[...].astype(BF16)


def out_kernel(seqs, order, own_ref, others_ref, w_ref, *refs):
    outs, (w, rows, sums, row_sem, w_sems, out_sems) = refs[: 2 * len(seqs)], refs[2 * len(seqs) :]
    length, channels = own_ref.shape[2:]
    tiles = w.shape[0]
    for r in range(4):
        cols = pl.ds(pl.multiple_of(order[r] * channels, channels), channels)
        for i, s in enumerate(seqs):
            source = own_ref.at[0, s] if r == 0 else others_ref.at[r - 1, s]
            copy(source, rows.at[pl.ds(i * length, length), cols], row_sem)
    for t in range(tiles):
        copy(w_ref.at[:, t // 2, pl.ds(t % 2 * channels, channels)], w.at[t], w_sems.at[t])
    wait_for(rows, row_sem)
    for half in range(2):

        def each_tile(i, carry, half=half):
            t = half * (tiles // 2) + i
            wait_for(w.at[t], w_sems.at[t])
            total = dot(rows[...], w[t].reshape(rows.shape[1], channels)).astype(BF16)
            for s in range(len(seqs)):
                there = pl.ds(pl.multiple_of(i * channels, channels), channels)
                sums[half, s, :, there] = total[s * length : (s + 1) * length]
            return carry

        lax.fori_loop(0, tiles // 2, each_tile, 0)
        for s in range(len(seqs)):
            copy(sums.at[half, s], outs[2 * s + half], out_sems.at[half])
    for half in range(2):
        wait_for(sums.at[half], out_sems.at[half])


def carry_states(ends, span):
    core = lax.axis_index("c")
    span = span[:, :, None]
    sent = ends.astype(BF16)
    other = from_ahead(sent, "c", 1).astype(F32)
    sent = sent.astype(F32)
    front, back = jnp.where(core == 0, sent, other), jnp.where(core == 0, other, sent)
    chip = (span * front + back).astype(BF16)
    hops = [from_behind(chip, "y", step).astype(F32) for step in (1, 2, 3)]
    square = span * span
    incoming = hops[0] + square * (hops[1] + square * hops[2])
    return jnp.where(core == 0, incoming, span * incoming + front)


IN_PLACE = pl.BlockSpec(memory_space=pl.ANY)
IN_VMEM = pl.BlockSpec(memory_space=pltpu.VMEM)
IN_SMEM = pl.BlockSpec(memory_space=pltpu.SMEM)
DMA = pltpu.SemaphoreType.DMA


def keys_values(order, w, rows, first, blocks, coefficients, name):
    seqs, (high, width) = len(rows), rows[0].shape
    lanes = coefficients[0].shape[1]
    by_chunk = (blocks, lanes, seqs, CHUNK // 2, 16, 128)
    features = pltpu.VMEM((lanes, seqs, CHUNK + 2, 8, 128), F32)
    return pl.pallas_call(
        functools.partial(kv_kernel, first, seqs),
        in_specs=[IN_SMEM] + [IN_PLACE] * (1 + seqs) + [IN_VMEM] * 4,
        out_specs=[IN_PLACE, IN_PLACE, IN_VMEM],
        scratch_shapes=[
            pltpu.VMEM((seqs * high, width), BF16),
            pltpu.VMEM((blocks, 2, width, lanes * 128), BF16),
            features,
            features,
            pltpu.VMEM(by_chunk, BF16),
            pltpu.VMEM(by_chunk, BF16),
            DMA,
            DMA((blocks,)),
            DMA((2,)),
        ],
        out_shape=[
            jax.ShapeDtypeStruct(by_chunk, BF16),
            jax.ShapeDtypeStruct(by_chunk, BF16),
            jax.ShapeDtypeStruct((blocks, lanes, seqs, 16, 128), F32),
        ],
        compiler_params=compiler_params(),
        name=name,
    )(order, w, *rows, *coefficients)


def queries(order, w, rows, first, blocks, taps, name):
    seqs, (high, width) = len(rows), rows[0].shape
    lanes = taps.shape[1]
    by_chunk = (blocks, lanes, seqs, CHUNK // 2, 16, 128)
    return pl.pallas_call(
        functools.partial(q_kernel, first, seqs),
        in_specs=[IN_SMEM] + [IN_PLACE] * (1 + seqs) + [IN_VMEM],
        out_specs=IN_PLACE,
        scratch_shapes=[
            pltpu.VMEM((seqs * high, width), BF16),
            pltpu.VMEM((blocks, width, lanes * 128), BF16),
            pltpu.VMEM((lanes, seqs, CHUNK + 2, 8, 128), F32),
            pltpu.VMEM(by_chunk, BF16),
            DMA,
            DMA((blocks,)),
            DMA,
        ],
        out_shape=jax.ShapeDtypeStruct(by_chunk, BF16),
        compiler_params=compiler_params(),
        name=name,
    )(order, w, *rows, taps)


def gate(y, e, query, first, coefficients, name):
    blocks, lanes, seqs = y.shape[:3]
    length = CHUNK * 8
    at = lambda a, first: pl.BlockSpec((1, 1) + a.shape[2:], lambda r, lane: (r + first, lane) + (0,) * (a.ndim - 2))
    return pl.pallas_call(
        gate_kernel,
        grid=(blocks, lanes),
        in_specs=[at(a, 0) for a in (y, e, query)] + [at(a, first) for a in coefficients],
        out_specs=pl.BlockSpec((1, seqs, length, 128), lambda r, lane: (r, 0, 0, lane)),
        scratch_shapes=[pltpu.VMEM((seqs, length, 128), F32)],
        out_shape=jax.ShapeDtypeStruct((blocks, seqs, length, lanes * 128), BF16),
        compiler_params=compiler_params(),
        name=name,
    )(y, e, query, *coefficients)


def project_out(order, seqs, own, others, w, name):
    length, channels = own.shape[2:]
    blocks, half = w.shape[0], w.shape[1] * channels
    return pl.pallas_call(
        functools.partial(out_kernel, seqs),
        in_specs=[IN_SMEM] + [IN_PLACE] * 3,
        out_specs=[IN_PLACE] * (2 * len(seqs)),
        scratch_shapes=[
            pltpu.VMEM((2 * w.shape[1], blocks, channels, channels), BF16),
            pltpu.VMEM((len(seqs) * length, blocks * channels), BF16),
            pltpu.VMEM((2, len(seqs), length, half), BF16),
            DMA,
            DMA((2 * w.shape[1],)),
            DMA((2,)),
        ],
        out_shape=[jax.ShapeDtypeStruct((length, half), BF16)] * (2 * len(seqs)),
        compiler_params=compiler_params(),
        name=name,
    )(order, own, others, w)


def shards(tokens, norm_gain, w_in, taps, decay_rate, residues, skip_gain, w_out):
    z, core = lax.axis_index("z"), lax.axis_index("c")
    part = lax.axis_index("y") * 2 + core
    width, _, channels = w_in.shape
    length = tokens.shape[1]
    blocks = seqs = len(OFFSETS)
    lanes = channels // 128
    depth = width // 8

    w_streams = w_in.transpose(1, 0, 2)
    with jax.named_scope("gather_in_weights"):
        share = lax.dynamic_slice(w_streams, (0, part * depth, 0), (3, depth, channels))
        w_all = lax.all_gather(share, ("z", "y", "c"), axis=0).reshape(blocks, 8, 3, depth, channels)

    with jax.named_scope("norm"):
        pairs = [(i, i + 1) for i in range(7)]
        edge = lax.ppermute(tokens[0, length - HEAD :], ("y", "c"), pairs)
        normed = pl.pallas_call(
            norm_kernel,
            out_shape=jax.ShapeDtypeStruct((HEAD + length, width), BF16),
            scratch_shapes=[pltpu.VMEM((width // 128, length, 128), F32)],
            compiler_params=compiler_params(),
            name="norm",
        )(edge, tokens, norm_gain[None])

    with jax.named_scope("gather_tokens"):
        rows = gather_along(normed, "x")

    with jax.named_scope("gather_out_weights"):
        w_out, normed = lax.optimization_barrier((w_out, normed))
        out_share = [
            lax.dynamic_slice(w_out, (0, (part * 2 + i) * channels), (channels, channels)) for i in range(2)
        ]
        w_o = lax.all_gather(jnp.concatenate(out_share, axis=0), ("z", "y", "c"), axis=0)
        w_o = w_o.reshape(blocks, 8, 2 * channels, channels)

    with jax.named_scope("coefficients"):
        packed = pl.pallas_call(
            pack_kernel, out_shape=jax.ShapeDtypeStruct((48, channels), F32), name="pack"
        )(taps, decay_rate, residues, skip_gain[None])
        per_pole = jax.ShapeDtypeStruct((blocks, lanes, 16, 128), F32)
        taps_all, kern, pole, jumps, res, reach, span = pl.pallas_call(
            coefficient_kernel,
            out_shape=[
                per_pole,
                per_pole,
                per_pole,
                jax.ShapeDtypeStruct((blocks, lanes, 3, 16, 128), F32),
                per_pole,
                jax.ShapeDtypeStruct((blocks, lanes, 16, 8, 128), F32),
                per_pole,
            ],
            compiler_params=compiler_params(),
            name="coefficients",
        )(*gather_along(packed, "z"))

    order = jnp.stack([(z + step) % 4 for step in OFFSETS]).astype(jnp.int32)
    coefficients = (taps_all, kern, pole, jumps)

    y0, e0, ends0 = keys_values(order, w_streams, rows, 0, 1, coefficients, "own_keys_values")
    query0 = queries(order, w_streams, rows, 0, 1, taps_all, "own_queries")
    y0, e0, ends0, query0, w_all = lax.optimization_barrier((y0, e0, ends0, query0, w_all))

    y, e, ends = keys_values(order, w_all, rows, 1, 3, coefficients, "keys_values")
    with jax.named_scope("states"):
        incoming = carry_states(jnp.concatenate([ends0, ends], axis=0), span)
    query = queries(order, w_all, rows, 1, 3, taps_all, "queries")
    coefficients = (incoming, pole, res, reach)
    own_gated = gate(y0, e0, query0, 0, coefficients, "own_gate")
    gated = gate(y, e, query, 1, coefficients, "gate")

    far, far_b = project_out(order, (3,), own_gated, gated, w_o, "project_far")
    far, far_b, gated = lax.optimization_barrier((far, far_b, gated))
    own, own_b, near, near_b, back, back_b = project_out(order, (0, 1, 2), own_gated, gated, w_o, "project_out")

    with jax.named_scope("sum_parts"):
        passing, passing_b = from_ahead(far, "x", -1), from_ahead(far_b, "x", 1)
        direct_b, direct = from_ahead(near_b, "x", -1), from_ahead(back, "x", 1)
        added = (near.astype(F32) + passing.astype(F32)).astype(BF16)
        added_b = (back_b.astype(F32) + passing_b.astype(F32)).astype(BF16)
        added, added_b = from_ahead(added, "x", -1), from_ahead(added_b, "x", 1)
        others = jnp.concatenate(
            [added.astype(F32) + direct.astype(F32), added_b.astype(F32) + direct_b.astype(F32)], axis=1
        )
        own = jnp.concatenate([own, own_b], axis=1)
        return (tokens[0].astype(F32) + own.astype(F32) + others).astype(BF16)[None]


def solution(mesh):
    fine = Mesh(mesh.devices.reshape(4, 4, 4, 2), ("x", "z", "y", "c"))
    fsdp, ctx = ("x", "z"), ("y", "c")
    in_specs = (
        P(fsdp, ctx, None),
        P(),
        P(None, None, fsdp),
        P(None, None, fsdp),
        P(None, fsdp),
        P(None, fsdp),
        P(fsdp),
        P(fsdp, None),
    )
    return jax.shard_map(shards, mesh=fine, in_specs=in_specs, out_specs=P(fsdp, ctx, None), check_vma=False)
```

time: 462 us -> 221 us (0.48)
  waiting for transfers between devices: 219 us -> 80.7 us
  local copies, waits for them, and re-layouts: 106 us -> 6.29 us
  Pallas kernels: 0 us -> 83.4 us
  matrix products: 65.9 us -> 0 us
  other arithmetic: 19.7 us -> 7.08 us
  starting transfers between devices: 36.3 us -> 29.4 us
    reduce_scatter x1 -> x0, waiting for transfers between devices: 110 us -> none  [shards(): lax.psum_scatter(jnp.dot(gated, w_out, preferred_element_type=jnp.float32...]
    pallas_call x0 -> x11, Pallas kernels: none -> 83.4 us  [the longest x2 31 us: keys_values(): pl.pallas_call(functools.partial(kv_kernel, first, seqs), in_specs=[IN_SM...]
    all_gather x1 -> x2, waiting for transfers between devices: 105 us -> 21.6 us  [the longest x1 18.6 us: shards(): lax.all_gather(share, ('z', 'y', 'c'), axis=0)]
    gather x2 -> x0, local copies, waits for them, and re-layouts: 79.8 us -> none  [shards(): kernel[jnp.maximum(lag_steps, 0)]]
    dot_general x5 -> x0, matrix products: 65.9 us -> none  [the longest x1 29.6 us: shards(): inside = jnp.einsum('tsc,gsc->gtc', toeplitz, product, precision=high)]
    ppermute x8 -> x17, waiting for transfers between devices: 4.24 us -> 59 us  [the longest x13 58.1 us: from_ahead(): lax.ppermute(value, axis, [(i, (i - steps) % count) for i in range(count)])]
    unnamed x18 -> x20, local copies, waits for them, and re-layouts: 13.1 us -> 2.32 us
    dot_general x3 -> x0, local copies, waits for them, and re-layouts: 8.33 us -> none  [the longest x1 2.93 us: shards(): entering = jnp.einsum('ntc,gnc->gtc', enter, incoming, precision=high)]
  transfers between devices with their start and end apart: 10 -> 19, of which waited for: 7 -> 13; matrix products, arithmetic and copies ran while one was open for 27% -> 3% of each run, Pallas kernels for 0% -> 34%
where the time goes in v3:
time: 221 us
  Pallas kernels  83.4 us (38%)
  waiting for transfers between devices  80.7 us (37%)
  starting transfers between devices  29.4 us (13%)
  between operations  13.7 us (6%)
  other arithmetic  7.08 us (3%)
  local copies, waits for them, and re-layouts  6.29 us (3%)
    ppermute x13, waiting for transfers between devices, from_ahead(): lax.ppermute(value, axis, [(i, (i - steps) % count) for i in range(count)])  58.1 us
    pallas_call x2, Pallas kernels, keys_values(): pl.pallas_call(functools.partial(kv_kernel, first, seqs), in_specs=[IN_SM...  31 us
    pallas_call x2, Pallas kernels, project_out(): pl.pallas_call(functools.partial(out_kernel, seqs), in_specs=[IN_SMEM] +...  20 us
    ppermute x13, starting transfers between devices, from_ahead(): lax.ppermute(value, axis, [(i, (i - steps) % count) for i in range(count)])  18.9 us
    all_gather x1, waiting for transfers between devices, shards(): lax.all_gather(share, ('z', 'y', 'c'), axis=0)  18.6 us
    pallas_call x2, Pallas kernels, queries(): pl.pallas_call(functools.partial(q_kernel, first, seqs), in_specs=[IN_SME...  16.8 us
    ppermute x3, starting transfers between devices, from_behind(): lax.ppermute(value, axis, [(i, i + steps) for i in range(count - steps)])  8.69 us
    pallas_call x2, Pallas kernels, gate(): pl.pallas_call(gate_kernel, grid=(blocks, lanes), in_specs=[at(a, 0) for...  8.56 us
  transfers between devices with their start and end apart: 19, of which 13 were waited for; matrix products, arithmetic and copies ran while one was open for 3% of the time, Pallas kernels for 34%

profile of v3, /device:TPU:6, one launch (start us, length us, event | category | flops | bytes accessed | tf_op | source)
XLA Modules:
  0.0 220.6 jit_solution(888744359191335213)
XLA Ops:
  6.5 2.1 dynamic-slice_bitcast_fusion
  9.6 1.7 collective-permute-start
  13.0 3.6 %norm.1.refs_0_ = bf16[144,4096]{1,0:T(8,128)(2,1)} custom-call(bf16[16,4096]{1,0:T(8,128)(2,1)} %copy-done.7, bf16[1,128,4096]{2,1,0:T(8,128)(2,1)} %tokens_ref.1, f32[1,4096]{1,0:T(1,128)} %bitcast.27), custom_call_target="tpu_custom_call" | custom-call | tf_op jit(solution)/shard_map/norm/norm/pallas_call | solution.py:416
  19.2 2.4 %collective-permute-start.2 = (bf16[144,4096]{1,0:T(8,128)(2,1)}, bf16[144,4096]{1,0:T(8,128)(2,1)S(1)}, u32[]{:S(2)}, u32[]{:S(2)}) collective-permute-start(bf16[144,4096]{1,0:T(8,128)(2,1)} %norm.1.refs_0_), channel_id=1, source_target_pairs={{0,32},{32,64},{64,96},{96,0},{1,33},{33,65},{65,97},{97,1},{2,34}... | collective-permute-start | bytes 3538952 | tf_op jit(solution)/shard_map/gather_tokens/ppermute | solution.py:20
  21.8 1.4 pack.1.p0
  23.2 4.0 %collective-permute-start.4 = (f32[48,256]{1,0:T(8,128)}, f32[48,256]{1,0:T(8,128)}, u32[]{:S(2)}, u32[]{:S(2)}) collective-permute-start(f32[48,256]{1,0:T(8,128)} %pack.1.p0), channel_id=1, source_target_pairs={{0,24},{8,0},{16,8},{24,16},{1,25},{9,1},{17,9},{25,17},{2,26},{10... | collective-permute-start | bytes 147464 | tf_op jit(solution)/shard_map/coefficients/ppermute | solution.py:20
  27.2 2.5 %collective-permute-done.4.p1 = f32[48,256]{1,0:T(8,128)} collective-permute-done((f32[48,256]{1,0:T(8,128)}, f32[48,256]{1,0:T(8,128)}, u32[]{:S(2)}, u32[]{:S(2)}) %collective-permute-start.4) | collective-permute-done | bytes 49184 | tf_op jit(solution)/shard_map/coefficients/ppermute | solution.py:20
  29.7 3.0 %collective-permute-start.6 = (f32[48,256]{1,0:T(8,128)}, f32[48,256]{1,0:T(8,128)S(1)}, u32[]{:S(2)}, u32[]{:S(2)}) collective-permute-start(f32[48,256]{1,0:T(8,128)} %pack.1.p0), channel_id=1, source_target_pairs={{0,16},{8,24},{16,0},{24,8},{1,17},{9,25},{17,1},{25,9},{2,18},{10... | collective-permute-start | bytes 147464 | tf_op jit(solution)/shard_map/coefficients/ppermute | solution.py:20
  34.2 2.7 %collective-permute-done.6.p3 = f32[48,256]{1,0:T(8,128)S(1)} collective-permute-done((f32[48,256]{1,0:T(8,128)}, f32[48,256]{1,0:T(8,128)S(1)}, u32[]{:S(2)}, u32[]{:S(2)}) %collective-permute-start.6) | collective-permute-done | bytes 49184 | tf_op jit(solution)/shard_map/coefficients/ppermute | solution.py:20
  37.5 2.1 coefficients.1
  39.6 9.4 %collective-permute-done.1.refs_1_ = bf16[144,4096]{1,0:T(8,128)(2,1)S(1)} collective-permute-done((bf16[144,4096]{1,0:T(8,128)(2,1)}, bf16[144,4096]{1,0:T(8,128)(2,1)S(1)}, u32[]{:S(2)}, u32[]{:S(2)}) %collective-permute-start.1) | collective-permute-done | bytes 1179680 | tf_op jit(solution)/shard_map/gather_tokens/ppermute | solution.py:20
  49.1 20.7 %collective-permute-done.3.refs_3_ = bf16[144,4096]{1,0:T(8,128)(2,1)S(1)} collective-permute-done((bf16[144,4096]{1,0:T(8,128)(2,1)}, bf16[144,4096]{1,0:T(8,128)(2,1)S(1)}, u32[]{:S(2)}, u32[]{:S(2)}) %collective-permute-start.3) | collective-permute-done | bytes 1179680 | tf_op jit(solution)/shard_map/gather_tokens/ppermute | solution.py:20
  70.8 6.3 %own_queries.1.q_ref = bf16[1,2,4,8,16,128]{5,4,3,2,1,0:T(8,128)(2,1)} custom-call(s32[4]{0:T(128)} %pad_add_fusion.order, bf16[3,4096,256]{2,1,0:T(8,128)(2,1)} %bitcast.23, bf16[144,4096]{1,0:T(8,128)(2,1)} %norm.1.refs_0_, bf16[144,4096]{1,0:T(8,128)(2,1)} %copy-done, bf16[144,4096]{1,0:T(8,128)(2,1)} %copy-done.1, bf16[144,4096]{1,0:T(8,128)(2,1)} %copy-done.2, ...), custom_call_target="tpu_custom_call" | custom-call | tf_op jit(solution)/shard_map/own_queries/pallas_call | solution.py:343
  77.0 10.5 %own_keys_values.1 = (bf16[1,2,4,8,16,128]{5,4,3,2,1,0:T(8,128)(2,1)}, bf16[1,2,4,8,16,128]{5,4,3,2,1,0:T(8,128)(2,1)}, f32[1,2,4,16,128]{4,3,2,1,0:T(8,128)}) custom-call(s32[4]{0:T(128)} %pad_add_fusion.order, bf16[3,4096,256]{2,1,0:T(8,128)(2,1)} %bitcast.24, bf16[144,4096]{1,0:T(8,128)(2,1)} %norm.1.refs_0_, bf16[144,4096]{1,0:T(8,128)(2,1)} %copy-done, ...), custom_call_target="tpu_custom_call" | custom-call | tf_op jit(solution)/shard_map/own_keys_values/pallas_call | solution.py:314
  87.6 18.6 %all-gather.5.cloned.1.call-done = bf16[96,512,256]{2,1,0:T(8,128)(2,1)} async-done(((bf16[3,512,256]{2,1,0:T(8,128)(2,1)}), bf16[96,512,256]{2,1,0:T(8,128)(2,1)}) %all-gather.5.cloned.1.call-update) | async-done | bytes 25165840 | tf_op jit(solution)/shard_map/gather_in_weights/all_gather | solution.py:411
  106.2 20.5 %keys_values.1 = (bf16[3,2,4,8,16,128]{5,4,3,2,1,0:T(8,128)(2,1)}, bf16[3,2,4,8,16,128]{5,4,3,2,1,0:T(8,128)(2,1)}, f32[3,2,4,16,128]{4,3,2,1,0:T(8,128)}) custom-call(s32[4]{0:T(128)} %pad_add_fusion.order, bf16[4,8,3,512,256]{4,3,2,1,0:T(8,128)(2,1)} %bitcast.19, bf16[144,4096]{1,0:T(8,128)(2,1)} %norm.1.refs_0_, bf16[144,4096]{1,0:T(8,128)(2,1)} %copy-done, ...), custom_call_target="tpu_custom_call" | custom-call | tf_op jit(solution)/shard_map/keys_values/pallas_call | solution.py:314
  129.2 4.6 %collective-permute-start.10 = (bf16[4,2,4,16,128]{4,3,2,1,0:T(8,128)(2,1)S(1)}, bf16[4,2,4,16,128]{4,3,2,1,0:T(8,128)(2,1)S(1)}, u32[]{:S(2)}, u32[]{:S(2)}) collective-permute-start(bf16[4,2,4,16,128]{4,3,2,1,0:T(8,128)(2,1)S(1)} %fusion.2), channel_id=1, source_target_pairs={{0,6},{1,7},{8,14},{9,15},{16,22},{17,23},{24,30},{25,31},{32,38},... | collective-permute-start | bytes 393224 | tf_op jit(solution)/shard_map/states/ppermute | solution.py:25
  133.8 1.3 collective-permute-start.9
  135.1 2.8 %collective-permute-start.8 = (bf16[4,2,4,16,128]{4,3,2,1,0:T(8,128)(2,1)S(1)}, bf16[4,2,4,16,128]{4,3,2,1,0:T(8,128)(2,1)S(1)}, u32[]{:S(2)}, u32[]{:S(2)}) collective-permute-start(bf16[4,2,4,16,128]{4,3,2,1,0:T(8,128)(2,1)S(1)} %fusion.2), channel_id=1, source_target_pairs={{0,2},{2,4},{4,6},{1,3},{3,5},{5,7},{8,10},{10,12},{12,14},{9,11},... | collective-permute-start | bytes 393224 | tf_op jit(solution)/shard_map/states/ppermute | solution.py:25
  137.9 10.5 %queries.1.q_ref = bf16[3,2,4,8,16,128]{5,4,3,2,1,0:T(8,128)(2,1)} custom-call(s32[4]{0:T(128)} %pad_add_fusion.order, bf16[4,8,3,512,256]{4,3,2,1,0:T(8,128)(2,1)} %bitcast.20, bf16[144,4096]{1,0:T(8,128)(2,1)} %norm.1.refs_0_, bf16[144,4096]{1,0:T(8,128)(2,1)} %copy-done, bf16[144,4096]{1,0:T(8,128)(2,1)} %copy-done.1, bf16[144,4096]{1,0:T(8,128)(2,1)} %copy-done.2, ...), custom_call_target="tpu_custom_call" | custom-call | tf_op jit(solution)/shard_map/queries/pallas_call | solution.py:343
  149.3 2.6 %own_gate.1.own_ref = bf16[1,4,128,256]{3,2,1,0:T(8,128)(2,1)} custom-call(bf16[1,2,4,8,16,128]{5,4,3,2,1,0:T(8,128)(2,1)} %get-tuple-element.42.y_ref, bf16[1,2,4,8,16,128]{5,4,3,2,1,0:T(8,128)(2,1)} %get-tuple-element.43.e_ref, bf16[1,2,4,8,16,128]{5,4,3,2,1,0:T(8,128)(2,1)} %own_queries.1.q_ref, f32[4,2,4,16,128]{4,3,2,1,0:T(8,128)} %add_select_fusion.in_ref, ...), custom_call_target="tpu_custom_call" | custom-call | tf_op jit(solution)/shard_map/own_gate/pallas_call | solution.py:366
  151.9 6.0 %gate.1.others_ref = bf16[3,4,128,256]{3,2,1,0:T(8,128)(2,1)} custom-call(bf16[3,2,4,8,16,128]{5,4,3,2,1,0:T(8,128)(2,1)} %get-tuple-element.51.y_ref, bf16[3,2,4,8,16,128]{5,4,3,2,1,0:T(8,128)(2,1)} %get-tuple-element.52.e_ref, bf16[3,2,4,8,16,128]{5,4,3,2,1,0:T(8,128)(2,1)} %queries.1.q_ref, f32[4,2,4,16,128]{4,3,2,1,0:T(8,128)} %add_select_fusion.in_ref, ...), custom_call_target="tpu_custom_call" | custom-call | tf_op jit(solution)/shard_map/gate/pallas_call | solution.py:366
  157.9 3.0 %all-gather.7.cloned.1.call-done = bf16[16384,256]{1,0:T(8,128)(2,1)} async-done(((bf16[512,256]{1,0:T(8,128)(2,1)}), bf16[16384,256]{1,0:T(8,128)(2,1)}) %all-gather.7.cloned.1.call-update) | async-done | bytes 8388624 | tf_op jit(solution)/shard_map/gather_out_weights/all_gather | solution.py:432
  160.8 8.6 %project_far.1 = (bf16[128,2048]{1,0:T(8,128)(2,1)}, bf16[128,2048]{1,0:T(8,128)(2,1)}) custom-call(s32[4]{0:T(128)} %pad_add_fusion.order, bf16[1,4,128,256]{3,2,1,0:T(8,128)(2,1)} %own_gate.1.own_ref, bf16[3,4,128,256]{3,2,1,0:T(8,128)(2,1)} %gate.1.others_ref, bf16[4,8,512,256]{3,2,1,0:T(8,128)(2,1)} %bitcast.21), custom_call_target="tpu_custom_call" | custom-call | tf_op jit(solution)/shard_map/project_far/pallas_call | solution.py:381
  170.6 2.4 %collective-permute-start.11 = (bf16[128,2048]{1,0:T(8,128)(2,1)}, bf16[128,2048]{1,0:T(8,128)(2,1)S(1)}, u32[]{:S(2)}, u32[]{:S(2)}) collective-permute-start(bf16[128,2048]{1,0:T(8,128)(2,1)} %get-tuple-element.60), channel_id=1, source_target_pairs={{0,32},{32,64},{64,96},{96,0},{1,33},{33,65},{65,97},{97,1},{2,34}... | collective-permute-start | bytes 1572872 | tf_op jit(solution)/shard_map/sum_parts/ppermute | solution.py:20
  173.0 11.3 %project_out.1 = (bf16[128,2048]{1,0:T(8,128)(2,1)}, bf16[128,2048]{1,0:T(8,128)(2,1)}, bf16[128,2048]{1,0:T(8,128)(2,1)}, bf16[128,2048]{1,0:T(8,128)(2,1)}, bf...) custom-call(s32[4]{0:T(128)} %pad_add_fusion.order, bf16[1,4,128,256]{3,2,1,0:T(8,128)(2,1)} %own_gate.1.own_ref, ...), custom_call_target="tpu_custom_call" | custom-call | tf_op jit(solution)/shard_map/project_out/pallas_call | solution.py:381
  186.4 1.2 collective-permute-start.15
  189.0 3.2 %collective-permute-start.12 = (bf16[128,2048]{1,0:T(8,128)(2,1)S(1)}, bf16[128,2048]{1,0:T(8,128)(2,1)S(1)}, u32[]{:S(2)}, u32[]{:S(2)}) collective-permute-start(bf16[128,2048]{1,0:T(8,128)(2,1)S(1)} %add_convert_fusion.1), channel_id=1, source_target_pairs={{0,32},{32,64},{64,96},{96,0},{1,33},{33,65},{65,97},{97,1},{2,34}... | collective-permute-start | bytes 1572872 | tf_op jit(solution)/shard_map/sum_parts/ppermute | solution.py:20
  192.2 7.2 %collective-permute-done.16 = bf16[128,2048]{1,0:T(8,128)(2,1)S(1)} collective-permute-done((bf16[128,2048]{1,0:T(8,128)(2,1)}, bf16[128,2048]{1,0:T(8,128)(2,1)S(1)}, u32[]{:S(2)}, u32[]{:S(2)}) %collective-permute-start.16) | collective-permute-done | bytes 524320 | tf_op jit(solution)/shard_map/sum_parts/ppermute | solution.py:20
  199.4 3.1 %collective-permute-done.15 = bf16[128,2048]{1,0:T(8,128)(2,1)S(1)} collective-permute-done((bf16[128,2048]{1,0:T(8,128)(2,1)S(1)}, bf16[128,2048]{1,0:T(8,128)(2,1)S(1)}, u32[]{:S(2)}, u32[]{:S(2)}) %collective-permute-start.15) | collective-permute-done | bytes 524320 | tf_op jit(solution)/shard_map/sum_parts/ppermute | solution.py:20
  202.7 9.5 %collective-permute-done.13 = bf16[128,2048]{1,0:T(8,128)(2,1)S(1)} collective-permute-done((bf16[128,2048]{1,0:T(8,128)(2,1)}, bf16[128,2048]{1,0:T(8,128)(2,1)S(1)}, u32[]{:S(2)}, u32[]{:S(2)}) %collective-permute-start.13) | collective-permute-done | bytes 524320 | tf_op jit(solution)/shard_map/sum_parts/ppermute | solution.py:20
  212.4 1.3 fusion
  (55 shorter events, 16.6 us)
Async XLA Ops:
  6.5 99.7 %all-gather.5.cloned.1.call-start = ((), (), s32[]{:S(2)}) async-start(), calls=%async_computation | async-start | bytes 25952256 | tf_op jit(solution)/shard_map/gather_in_weights/all_gather | solution.py:411
  8.6 152.2 %all-gather.7.cloned.1.call-start = ((), (), s32[]{:S(2)}) async-start(), calls=%async_computation.1 | async-start | bytes 8650752 | tf_op jit(solution)/shard_map/gather_out_weights/all_gather | solution.py:432
  9.6 2.7 %collective-permute-start = (bf16[16,4096]{1,0:T(8,128)(2,1)S(1)}, bf16[16,4096]{1,0:T(8,128)(2,1)S(1)}, u32[]{:S(2)}, u32[]{:S(2)}) collective-permute-start(bf16[16,4096]{1,0:T(8,128)(2,1)S(1)} %slice_bitcast_fusion), channel_id=1, source_target_pairs={{0,1},{1,2},{2,3},{3,4},{4,5},{5,6},{6,7},{8,9},{9,10},{10,11},{11... | collective-permute-start | bytes 393224 | tf_op jit(solution)/shard_map/norm/ppermute | solution.py:415
  12.3 0.7 copy-start.7
  18.3 30.8 %collective-permute-start.1 = (bf16[144,4096]{1,0:T(8,128)(2,1)}, bf16[144,4096]{1,0:T(8,128)(2,1)S(1)}, u32[]{:S(2)}, u32[]{:S(2)}) collective-permute-start(bf16[144,4096]{1,0:T(8,128)(2,1)} %norm.1.refs_0_), channel_id=1, source_target_pairs={{0,96},{32,0},{64,32},{96,64},{1,97},{33,1},{65,33},{97,65},{2,98}... | collective-permute-start | bytes 3538952 | tf_op jit(solution)/shard_map/gather_tokens/ppermute | solution.py:20
  19.2 29.9 %collective-permute-start.2 = (bf16[144,4096]{1,0:T(8,128)(2,1)}, bf16[144,4096]{1,0:T(8,128)(2,1)S(1)}, u32[]{:S(2)}, u32[]{:S(2)}) collective-permute-start(bf16[144,4096]{1,0:T(8,128)(2,1)} %norm.1.refs_0_), channel_id=1, source_target_pairs={{0,32},{32,64},{64,96},{96,0},{1,33},{33,65},{65,97},{97,1},{2,34}... | collective-permute-start | bytes 3538952 | tf_op jit(solution)/shard_map/gather_tokens/ppermute | solution.py:20
  21.6 48.1 %collective-permute-start.3 = (bf16[144,4096]{1,0:T(8,128)(2,1)}, bf16[144,4096]{1,0:T(8,128)(2,1)S(1)}, u32[]{:S(2)}, u32[]{:S(2)}) collective-permute-start(bf16[144,4096]{1,0:T(8,128)(2,1)} %norm.1.refs_0_), channel_id=1, source_target_pairs={{0,64},{32,96},{64,0},{96,32},{1,65},{33,97},{65,1},{97,33},{2,66}... | collective-permute-start | bytes 3538952 | tf_op jit(solution)/shard_map/gather_tokens/ppermute | solution.py:20
  23.2 6.5 %collective-permute-start.4 = (f32[48,256]{1,0:T(8,128)}, f32[48,256]{1,0:T(8,128)}, u32[]{:S(2)}, u32[]{:S(2)}) collective-permute-start(f32[48,256]{1,0:T(8,128)} %pack.1.p0), channel_id=1, source_target_pairs={{0,24},{8,0},{16,8},{24,16},{1,25},{9,1},{17,9},{25,17},{2,26},{10... | collective-permute-start | bytes 147464 | tf_op jit(solution)/shard_map/coefficients/ppermute | solution.py:20
  27.2 6.9 %collective-permute-start.5 = (f32[48,256]{1,0:T(8,128)}, f32[48,256]{1,0:T(8,128)}, u32[]{:S(2)}, u32[]{:S(2)}) collective-permute-start(f32[48,256]{1,0:T(8,128)} %pack.1.p0), channel_id=1, source_target_pairs={{0,8},{8,16},{16,24},{24,0},{1,9},{9,17},{17,25},{25,1},{2,10},{10... | collective-permute-start | bytes 147464 | tf_op jit(solution)/shard_map/coefficients/ppermute | solution.py:20
  29.7 7.2 %collective-permute-start.6 = (f32[48,256]{1,0:T(8,128)}, f32[48,256]{1,0:T(8,128)S(1)}, u32[]{:S(2)}, u32[]{:S(2)}) collective-permute-start(f32[48,256]{1,0:T(8,128)} %pack.1.p0), channel_id=1, source_target_pairs={{0,16},{8,24},{16,0},{24,8},{1,17},{9,25},{17,1},{25,9},{2,18},{10... | collective-permute-start | bytes 147464 | tf_op jit(solution)/shard_map/coefficients/ppermute | solution.py:20
  36.9 0.6 copy-start.9
  49.1 20.7 %copy-start = (bf16[144,4096]{1,0:T(8,128)(2,1)}, bf16[144,4096]{1,0:T(8,128)(2,1)S(1)}, u32[]{:S(2)}) copy-start(bf16[144,4096]{1,0:T(8,128)(2,1)S(1)} %collective-permute-done.1.refs_1_) | copy-start | bytes 3538948
  49.1 20.7 %copy-start.1 = (bf16[144,4096]{1,0:T(8,128)(2,1)}, bf16[144,4096]{1,0:T(8,128)(2,1)S(1)}, u32[]{:S(2)}) copy-start(bf16[144,4096]{1,0:T(8,128)(2,1)S(1)} %collective-permute-done.2.refs_2_) | copy-start | bytes 3538948
  69.7 1.0 copy-start.2
  106.2 21.5 %copy-start.8 = (f32[1,2,4,16,128]{4,3,2,1,0:T(8,128)S(1)}, f32[1,2,4,16,128]{4,3,2,1,0:T(8,128)}, u32[]{:S(2)}) copy-start(f32[1,2,4,16,128]{4,3,2,1,0:T(8,128)} %get-tuple-element.46) | copy-start | bytes 196612
  106.2 22.9 %copy-start.4 = (f32[4,2,16,128]{3,2,1,0:T(8,128)S(1)}, f32[4,2,16,128]{3,2,1,0:T(8,128)}, u32[]{:S(2)}) copy-start(f32[4,2,16,128]{3,2,1,0:T(8,128)} %get-tuple-element.45) | copy-start | bytes 196612
  127.7 1.4 collective-permute-start.7
  129.2 19.2 %collective-permute-start.10 = (bf16[4,2,4,16,128]{4,3,2,1,0:T(8,128)(2,1)S(1)}, bf16[4,2,4,16,128]{4,3,2,1,0:T(8,128)(2,1)S(1)}, u32[]{:S(2)}, u32[]{:S(2)}) collective-permute-start(bf16[4,2,4,16,128]{4,3,2,1,0:T(8,128)(2,1)S(1)} %fusion.2), channel_id=1, source_target_pairs={{0,6},{1,7},{8,14},{9,15},{16,22},{17,23},{24,30},{25,31},{32,38},... | collective-permute-start | bytes 393224 | tf_op jit(solution)/shard_map/states/ppermute | solution.py:25
  133.8 14.6 %collective-permute-start.9 = (bf16[4,2,4,16,128]{4,3,2,1,0:T(8,128)(2,1)S(1)}, bf16[4,2,4,16,128]{4,3,2,1,0:T(8,128)(2,1)S(1)}, u32[]{:S(2)}, u32[]{:S(2)}) collective-permute-start(bf16[4,2,4,16,128]{4,3,2,1,0:T(8,128)(2,1)S(1)} %fusion.2), channel_id=1, source_target_pairs={{0,4},{2,6},{1,5},{3,7},{8,12},{10,14},{9,13},{11,15},{16,20},{18,... | collective-permute-start | bytes 393224 | tf_op jit(solution)/shard_map/states/ppermute | solution.py:25
  135.1 13.3 %collective-permute-start.8 = (bf16[4,2,4,16,128]{4,3,2,1,0:T(8,128)(2,1)S(1)}, bf16[4,2,4,16,128]{4,3,2,1,0:T(8,128)(2,1)S(1)}, u32[]{:S(2)}, u32[]{:S(2)}) collective-permute-start(bf16[4,2,4,16,128]{4,3,2,1,0:T(8,128)(2,1)S(1)} %fusion.2), channel_id=1, source_target_pairs={{0,2},{2,4},{4,6},{1,3},{3,5},{5,7},{8,10},{10,12},{12,14},{9,11},... | collective-permute-start | bytes 393224 | tf_op jit(solution)/shard_map/states/ppermute | solution.py:25
  169.5 15.8 %collective-permute-start.14 = (bf16[128,2048]{1,0:T(8,128)(2,1)}, bf16[128,2048]{1,0:T(8,128)(2,1)S(1)}, u32[]{:S(2)}, u32[]{:S(2)}) collective-permute-start(bf16[128,2048]{1,0:T(8,128)(2,1)} %get-tuple-element.63), channel_id=1, source_target_pairs={{0,96},{32,0},{64,32},{96,64},{1,97},{33,1},{65,33},{97,65},{2,98}... | collective-permute-start | bytes 1572872 | tf_op jit(solution)/shard_map/sum_parts/ppermute | solution.py:20
  170.6 17.2 %collective-permute-start.11 = (bf16[128,2048]{1,0:T(8,128)(2,1)}, bf16[128,2048]{1,0:T(8,128)(2,1)S(1)}, u32[]{:S(2)}, u32[]{:S(2)}) collective-permute-start(bf16[128,2048]{1,0:T(8,128)(2,1)} %get-tuple-element.60), channel_id=1, source_target_pairs={{0,32},{32,64},{64,96},{96,0},{1,33},{33,65},{65,97},{97,1},{2,34}... | collective-permute-start | bytes 1572872 | tf_op jit(solution)/shard_map/sum_parts/ppermute | solution.py:20
  184.3 15.1 %collective-permute-start.16 = (bf16[128,2048]{1,0:T(8,128)(2,1)}, bf16[128,2048]{1,0:T(8,128)(2,1)S(1)}, u32[]{:S(2)}, u32[]{:S(2)}) collective-permute-start(bf16[128,2048]{1,0:T(8,128)(2,1)} %get-tuple-element.64), channel_id=1, source_target_pairs={{0,32},{32,64},{64,96},{96,0},{1,33},{33,65},{65,97},{97,1},{2,34}... | collective-permute-start | bytes 1572872 | tf_op jit(solution)/shard_map/sum_parts/ppermute | solution.py:20
  186.4 16.1 %collective-permute-start.15 = (bf16[128,2048]{1,0:T(8,128)(2,1)S(1)}, bf16[128,2048]{1,0:T(8,128)(2,1)S(1)}, u32[]{:S(2)}, u32[]{:S(2)}) collective-permute-start(bf16[128,2048]{1,0:T(8,128)(2,1)S(1)} %add_convert_fusion), channel_id=1, source_target_pairs={{0,96},{32,0},{64,32},{96,64},{1,97},{33,1},{65,33},{97,65},{2,98}... | collective-permute-start | bytes 1572872 | tf_op jit(solution)/shard_map/sum_parts/ppermute | solution.py:20
  187.7 24.6 %collective-permute-start.13 = (bf16[128,2048]{1,0:T(8,128)(2,1)}, bf16[128,2048]{1,0:T(8,128)(2,1)S(1)}, u32[]{:S(2)}, u32[]{:S(2)}) collective-permute-start(bf16[128,2048]{1,0:T(8,128)(2,1)} %get-tuple-element.61), channel_id=1, source_target_pairs={{0,96},{32,0},{64,32},{96,64},{1,97},{33,1},{65,33},{97,65},{2,98}... | collective-permute-start | bytes 1572872 | tf_op jit(solution)/shard_map/sum_parts/ppermute | solution.py:20
  188.9 23.4 %copy-start.3 = (bf16[1,128,4096]{2,1,0:T(8,128)(2,1)S(1)}, bf16[1,128,4096]{2,1,0:T(8,128)(2,1)}, u32[]{:S(2)}) copy-start(bf16[1,128,4096]{2,1,0:T(8,128)(2,1)} %tokens_ref.1) | copy-start | bytes 3145732
  188.9 23.4 %copy-start.5 = (bf16[128,2048]{1,0:T(8,128)(2,1)S(1)}, bf16[128,2048]{1,0:T(8,128)(2,1)}, u32[]{:S(2)}) copy-start(bf16[128,2048]{1,0:T(8,128)(2,1)} %get-tuple-element.57) | copy-start | bytes 1572868
  188.9 23.4 %copy-start.6 = (bf16[128,2048]{1,0:T(8,128)(2,1)S(1)}, bf16[128,2048]{1,0:T(8,128)(2,1)}, u32[]{:S(2)}) copy-start(bf16[128,2048]{1,0:T(8,128)(2,1)} %get-tuple-element.58) | copy-start | bytes 1572868
  189.0 23.3 %collective-permute-start.12 = (bf16[128,2048]{1,0:T(8,128)(2,1)S(1)}, bf16[128,2048]{1,0:T(8,128)(2,1)S(1)}, u32[]{:S(2)}, u32[]{:S(2)}) collective-permute-start(bf16[128,2048]{1,0:T(8,128)(2,1)S(1)} %add_convert_fusion.1), channel_id=1, source_target_pairs={{0,32},{32,64},{64,96},{96,0},{1,33},{33,65},{65,97},{97,1},{2,34}... | collective-permute-start | bytes 1572872 | tf_op jit(solution)/shard_map/sum_parts/ppermute | solution.py:20
Sparse Core Ops, SparseCore 0:
  9.6 96.5 all-gather.4
  108.5 52.3 all-gather.6

commit v4 on v3

--- a/solution.py
+++ b/solution.py
@@ -259,23 +259,23 @@
 def out_kernel(seqs, order, own_ref, others_ref, w_ref, *refs):
     outs, (w, rows, sums, row_sem, w_sems, out_sems) = refs[: 2 * len(seqs)], refs[2 * len(seqs) :]
     length, channels = own_ref.shape[2:]
-    tiles = w.shape[0]
+    tiles, _, _, cols = w.shape
     for r in range(4):
-        cols = pl.ds(pl.multiple_of(order[r] * channels, channels), channels)
+        block = pl.ds(pl.multiple_of(order[r] * channels, channels), channels)
         for i, s in enumerate(seqs):
             source = own_ref.at[0, s] if r == 0 else others_ref.at[r - 1, s]
-            copy(source, rows.at[pl.ds(i * length, length), cols], row_sem)
+            copy(source, rows.at[pl.ds(i * length, length), block], row_sem)
     for t in range(tiles):
-        copy(w_ref.at[:, t // 2, pl.ds(t % 2 * channels, channels)], w.at[t], w_sems.at[t])
+        copy(w_ref.at[:, :, pl.ds(t * cols, cols)], w.at[t], w_sems.at[t])
     wait_for(rows, row_sem)
     for half in range(2):
 
         def each_tile(i, carry, half=half):
             t = half * (tiles // 2) + i
             wait_for(w.at[t], w_sems.at[t])
-            total = dot(rows[...], w[t].reshape(rows.shape[1], channels)).astype(BF16)
+            total = dot(rows[...], w[t].reshape(rows.shape[1], cols)).astype(BF16)
             for s in range(len(seqs)):
-                there = pl.ds(pl.multiple_of(i * channels, channels), channels)
+                there = pl.ds(pl.multiple_of(i * cols, cols), cols)
                 sums[half, s, :, there] = total[s * length : (s + 1) * length]
             return carry
 
@@ -377,17 +377,19 @@
 
 def project_out(order, seqs, own, others, w, name):
     length, channels = own.shape[2:]
-    blocks, half = w.shape[0], w.shape[1] * channels
+    blocks, half = w.shape[0], w.shape[2] // 2
+    cols = 4 * channels
+    tiles = w.shape[2] // cols
     return pl.pallas_call(
         functools.partial(out_kernel, seqs),
         in_specs=[IN_SMEM] + [IN_PLACE] * 3,
         out_specs=[IN_PLACE] * (2 * len(seqs)),
         scratch_shapes=[
-            pltpu.VMEM((2 * w.shape[1], blocks, channels, channels), BF16),
+            pltpu.VMEM((tiles, blocks, channels, cols), BF16),
             pltpu.VMEM((len(seqs) * length, blocks * channels), BF16),
             pltpu.VMEM((2, len(seqs), length, half), BF16),
             DMA,
-            DMA((2 * w.shape[1],)),
+            DMA((tiles,)),
             DMA((2,)),
         ],
         out_shape=[jax.ShapeDtypeStruct((length, half), BF16)] * (2 * len(seqs)),
@@ -426,11 +428,8 @@
 
     with jax.named_scope("gather_out_weights"):
         w_out, normed = lax.optimization_barrier((w_out, normed))
-        out_share = [
-            lax.dynamic_slice(w_out, (0, (part * 2 + i) * channels), (channels, channels)) for i in range(2)
-        ]
-        w_o = lax.all_gather(jnp.concatenate(out_share, axis=0), ("z", "y", "c"), axis=0)
-        w_o = w_o.reshape(blocks, 8, 2 * channels, channels)
+        out_share = lax.dynamic_slice(w_out, (core * (channels // 2), 0), (channels // 2, width))
+        w_o = lax.all_gather(out_share, ("z", "c"), axis=0).reshape(blocks, channels, width)
 
     with jax.named_scope("coefficients"):
         packed = pl.pallas_call(

time: 221 us -> 216 us (0.977)
  Pallas kernels: 83.4 us -> 78.9 us
    pallas_call x2, Pallas kernels: 20 us -> 15 us  [project_out(): pl.pallas_call(functools.partial(out_kernel, seqs), in_specs=[IN_SMEM] +...]
    all_gather x1, waiting for transfers between devices: 2.97 us -> 0.01 us  [shards(): lax.all_gather(out_share, ('z', 'c'), axis=0)]
    ppermute x13, waiting for transfers between devices: 58.1 us -> 60.6 us  [from_ahead(): lax.ppermute(value, axis, [(i, (i - steps) % count) for i in range(count)])]
  transfers between devices with their start and end apart: 19 -> 19, of which waited for: 13 -> 12; matrix products, arithmetic and copies ran while one was open for 3% -> 3% of each run, Pallas kernels for 34% -> 34%
where the time goes in v4:
time: 216 us; the launch traced here: 215 us
  waiting for transfers between devices  81.1 us (38%)
  Pallas kernels  78.9 us (37%)
  starting transfers between devices  28.1 us (13%)
  between operations  13.7 us (6%)
  local copies, waits for them, and re-layouts  6.67 us (3%)
  other arithmetic  6.38 us (3%)
    ppermute x13, waiting for transfers between devices, from_ahead(): lax.ppermute(value, axis, [(i, (i - steps) % count) for i in range(count)])  60.6 us
    pallas_call x2, Pallas kernels, keys_values(): pl.pallas_call(functools.partial(kv_kernel, first, seqs), in_specs=[IN_SM...  30.9 us
    all_gather x1, waiting for transfers between devices, shards(): lax.all_gather(share, ('z', 'y', 'c'), axis=0)  19.5 us
    ppermute x13, starting transfers between devices, from_ahead(): lax.ppermute(value, axis, [(i, (i - steps) % count) for i in range(count)])  17.5 us
    pallas_call x2, Pallas kernels, queries(): pl.pallas_call(functools.partial(q_kernel, first, seqs), in_specs=[IN_SME...  17.4 us
    pallas_call x2, Pallas kernels, project_out(): pl.pallas_call(functools.partial(out_kernel, seqs), in_specs=[IN_SMEM] +...  15 us
    ppermute x3, starting transfers between devices, from_behind(): lax.ppermute(value, axis, [(i, i + steps) for i in range(count - steps)])  8.87 us
    pallas_call x2, Pallas kernels, gate(): pl.pallas_call(gate_kernel, grid=(blocks, lanes), in_specs=[at(a, 0) for...  8.49 us
  transfers between devices with their start and end apart: 19, of which 12 were waited for; matrix products, arithmetic and copies ran while one was open for 3% of the time, Pallas kernels for 34%

profile of v4, /device:TPU:6, one launch (start us, length us, event | category | flops | bytes accessed | tf_op | source)
XLA Modules:
  0.0 214.8 jit_solution(5135596796045806964)
XLA Ops:
  6.5 2.2 %dynamic-slice_bitcast_fusion = bf16[3,512,256]{2,1,0:T(8,128)(2,1)} fusion(bf16[4096,3,256]{2,0,1:T(8,128)(2,1)} %param.10, s32[]{:T(128)S(6)} %select_n.45), kind=kLoop, calls=%fused_computation.6 | loop fusion | bytes 1572868 | tf_op jit(solution)/shard_map/gather_in_weights/dynamic_slice | solution.py:412
  9.8 1.7 collective-permute-start
  13.1 3.6 %norm.1.refs_0_ = bf16[144,4096]{1,0:T(8,128)(2,1)} custom-call(bf16[16,4096]{1,0:T(8,128)(2,1)} %copy-done.8, bf16[1,128,4096]{2,1,0:T(8,128)(2,1)} %tokens_ref.1, f32[1,4096]{1,0:T(1,128)} %bitcast.27), custom_call_target="tpu_custom_call" | custom-call | tf_op jit(solution)/shard_map/norm/norm/pallas_call | solution.py:418
  19.2 2.4 %collective-permute-start.2 = (bf16[144,4096]{1,0:T(8,128)(2,1)S(1)}, bf16[144,4096]{1,0:T(8,128)(2,1)}, u32[]{:S(2)}, u32[]{:S(2)}) collective-permute-start(bf16[144,4096]{1,0:T(8,128)(2,1)S(1)} %copy-done.2), channel_id=1, source_target_pairs={{0,32},{32,64},{64,96},{96,0},{1,33},{33,65},{65,97},{97,1},{2,34}... | collective-permute-start | bytes 3538952 | tf_op jit(solution)/shard_map/gather_tokens/ppermute | solution.py:20
  21.8 1.4 pack.1.p0
  23.2 4.0 %collective-permute-start.4 = (f32[48,256]{1,0:T(8,128)}, f32[48,256]{1,0:T(8,128)S(1)}, u32[]{:S(2)}, u32[]{:S(2)}) collective-permute-start(f32[48,256]{1,0:T(8,128)} %pack.1.p0), channel_id=1, source_target_pairs={{0,24},{8,0},{16,8},{24,16},{1,25},{9,1},{17,9},{25,17},{2,26},{10... | collective-permute-start | bytes 147464 | tf_op jit(solution)/shard_map/coefficients/ppermute | solution.py:20
  27.2 2.5 %collective-permute-done.4.p1 = f32[48,256]{1,0:T(8,128)S(1)} collective-permute-done((f32[48,256]{1,0:T(8,128)}, f32[48,256]{1,0:T(8,128)S(1)}, u32[]{:S(2)}, u32[]{:S(2)}) %collective-permute-start.4) | collective-permute-done | bytes 49184 | tf_op jit(solution)/shard_map/coefficients/ppermute | solution.py:20
  29.7 2.8 %collective-permute-start.6 = (f32[48,256]{1,0:T(8,128)}, f32[48,256]{1,0:T(8,128)S(1)}, u32[]{:S(2)}, u32[]{:S(2)}) collective-permute-start(f32[48,256]{1,0:T(8,128)} %pack.1.p0), channel_id=1, source_target_pairs={{0,16},{8,24},{16,0},{24,8},{1,17},{9,25},{17,1},{25,9},{2,18},{10... | collective-permute-start | bytes 147464 | tf_op jit(solution)/shard_map/coefficients/ppermute | solution.py:20
  34.0 2.8 %collective-permute-done.6.p3 = f32[48,256]{1,0:T(8,128)S(1)} collective-permute-done((f32[48,256]{1,0:T(8,128)}, f32[48,256]{1,0:T(8,128)S(1)}, u32[]{:S(2)}, u32[]{:S(2)}) %collective-permute-start.6) | collective-permute-done | bytes 49184 | tf_op jit(solution)/shard_map/coefficients/ppermute | solution.py:20
  37.5 2.2 %coefficients.1 = (f32[4,2,16,128]{3,2,1,0:T(8,128)}, f32[4,2,16,128]{3,2,1,0:T(8,128)}, f32[4,2,16,128]{3,2,1,0:T(8,128)}, f32[4,2,3,16,128]{4,3,2,1,0:T(8,128)...) custom-call(f32[48,256]{1,0:T(8,128)} %pack.1.p0, f32[48,256]{1,0:T(8,128)} %copy-done.10, ...), custom_call_target="tpu_custom_call" | custom-call | tf_op jit(solution)/shard_map/coefficients/coefficients/pallas_call | solution.py:439
  39.7 9.2 %collective-permute-done.1.refs_1_ = bf16[144,4096]{1,0:T(8,128)(2,1)S(1)} collective-permute-done((bf16[144,4096]{1,0:T(8,128)(2,1)S(1)}, bf16[144,4096]{1,0:T(8,128)(2,1)S(1)}, u32[]{:S(2)}, u32[]{:S(2)}) %collective-permute-start.1) | collective-permute-done | bytes 1179680 | tf_op jit(solution)/shard_map/gather_tokens/ppermute | solution.py:20
  48.9 20.8 %collective-permute-done.3.refs_3_ = bf16[144,4096]{1,0:T(8,128)(2,1)} collective-permute-done((bf16[144,4096]{1,0:T(8,128)(2,1)S(1)}, bf16[144,4096]{1,0:T(8,128)(2,1)}, u32[]{:S(2)}, u32[]{:S(2)}) %collective-permute-start.3) | collective-permute-done | bytes 1179680 | tf_op jit(solution)/shard_map/gather_tokens/ppermute | solution.py:20
  69.6 6.6 %own_queries.1.q_ref = bf16[1,2,4,8,16,128]{5,4,3,2,1,0:T(8,128)(2,1)} custom-call(s32[4]{0:T(128)} %pad_add_fusion.order, bf16[3,4096,256]{2,1,0:T(8,128)(2,1)} %bitcast.23, bf16[144,4096]{1,0:T(8,128)(2,1)} %norm.1.refs_0_, bf16[144,4096]{1,0:T(8,128)(2,1)} %copy-done.3, bf16[144,4096]{1,0:T(8,128)(2,1)} %collective-permute-done.2.refs_2_, ...), custom_call_target="tpu_custom_call" | custom-call | tf_op jit(solution)/shard_map/own_queries/pallas_call | solution.py:343
  76.2 10.4 %own_keys_values.1 = (bf16[1,2,4,8,16,128]{5,4,3,2,1,0:T(8,128)(2,1)}, bf16[1,2,4,8,16,128]{5,4,3,2,1,0:T(8,128)(2,1)}, f32[1,2,4,16,128]{4,3,2,1,0:T(8,128)}) custom-call(s32[4]{0:T(128)} %pad_add_fusion.order, bf16[3,4096,256]{2,1,0:T(8,128)(2,1)} %bitcast.24, bf16[144,4096]{1,0:T(8,128)(2,1)} %norm.1.refs_0_, bf16[144,4096]{1,0:T(8,128)(2,1)} %copy-done.3, ...), custom_call_target="tpu_custom_call" | custom-call | tf_op jit(solution)/shard_map/own_keys_values/pallas_call | solution.py:314
  86.7 19.5 %all-gather.5.cloned.1.call-done = bf16[96,512,256]{2,1,0:T(8,128)(2,1)} async-done(((bf16[3,512,256]{2,1,0:T(8,128)(2,1)}), bf16[96,512,256]{2,1,0:T(8,128)(2,1)}) %all-gather.5.cloned.1.call-update) | async-done | bytes 25165840 | tf_op jit(solution)/shard_map/gather_in_weights/all_gather | solution.py:413
  106.2 20.5 %keys_values.1 = (bf16[3,2,4,8,16,128]{5,4,3,2,1,0:T(8,128)(2,1)}, bf16[3,2,4,8,16,128]{5,4,3,2,1,0:T(8,128)(2,1)}, f32[3,2,4,16,128]{4,3,2,1,0:T(8,128)}) custom-call(s32[4]{0:T(128)} %pad_add_fusion.order, bf16[4,8,3,512,256]{4,3,2,1,0:T(8,128)(2,1)} %bitcast.19, bf16[144,4096]{1,0:T(8,128)(2,1)} %norm.1.refs_0_, bf16[144,4096]{1,0:T(8,128)(2,1)} %copy-done.3, ...), custom_call_target="tpu_custom_call" | custom-call | tf_op jit(solution)/shard_map/keys_values/pallas_call | solution.py:314
  129.2 4.6 %collective-permute-start.10 = (bf16[4,2,4,16,128]{4,3,2,1,0:T(8,128)(2,1)S(1)}, bf16[4,2,4,16,128]{4,3,2,1,0:T(8,128)(2,1)S(1)}, u32[]{:S(2)}, u32[]{:S(2)}) collective-permute-start(bf16[4,2,4,16,128]{4,3,2,1,0:T(8,128)(2,1)S(1)} %fusion.2), channel_id=1, source_target_pairs={{0,6},{1,7},{8,14},{9,15},{16,22},{17,23},{24,30},{25,31},{32,38},... | collective-permute-start | bytes 393224 | tf_op jit(solution)/shard_map/states/ppermute | solution.py:25
  133.8 1.3 collective-permute-start.9
  135.2 2.9 %collective-permute-start.8 = (bf16[4,2,4,16,128]{4,3,2,1,0:T(8,128)(2,1)S(1)}, bf16[4,2,4,16,128]{4,3,2,1,0:T(8,128)(2,1)S(1)}, u32[]{:S(2)}, u32[]{:S(2)}) collective-permute-start(bf16[4,2,4,16,128]{4,3,2,1,0:T(8,128)(2,1)S(1)} %fusion.2), channel_id=1, source_target_pairs={{0,2},{2,4},{4,6},{1,3},{3,5},{5,7},{8,10},{10,12},{12,14},{9,11},... | collective-permute-start | bytes 393224 | tf_op jit(solution)/shard_map/states/ppermute | solution.py:25
  138.1 10.7 %queries.1.q_ref = bf16[3,2,4,8,16,128]{5,4,3,2,1,0:T(8,128)(2,1)} custom-call(s32[4]{0:T(128)} %pad_add_fusion.order, bf16[4,8,3,512,256]{4,3,2,1,0:T(8,128)(2,1)} %bitcast.20, bf16[144,4096]{1,0:T(8,128)(2,1)} %norm.1.refs_0_, bf16[144,4096]{1,0:T(8,128)(2,1)} %copy-done.3, bf16[144,4096]{1,0:T(8,128)(2,1)} %collective-permute-done.2.refs_2_, ...), custom_call_target="tpu_custom_call" | custom-call | tf_op jit(solution)/shard_map/queries/pallas_call | solution.py:343
  149.7 2.6 %own_gate.1.own_ref = bf16[1,4,128,256]{3,2,1,0:T(8,128)(2,1)} custom-call(bf16[1,2,4,8,16,128]{5,4,3,2,1,0:T(8,128)(2,1)} %get-tuple-element.42.y_ref, bf16[1,2,4,8,16,128]{5,4,3,2,1,0:T(8,128)(2,1)} %get-tuple-element.43.e_ref, bf16[1,2,4,8,16,128]{5,4,3,2,1,0:T(8,128)(2,1)} %own_queries.1.q_ref, f32[4,2,4,16,128]{4,3,2,1,0:T(8,128)} %add_select_fusion.in_ref, ...), custom_call_target="tpu_custom_call" | custom-call | tf_op jit(solution)/shard_map/own_gate/pallas_call | solution.py:366
  152.3 5.9 %gate.1.others_ref = bf16[3,4,128,256]{3,2,1,0:T(8,128)(2,1)} custom-call(bf16[3,2,4,8,16,128]{5,4,3,2,1,0:T(8,128)(2,1)} %get-tuple-element.51.y_ref, bf16[3,2,4,8,16,128]{5,4,3,2,1,0:T(8,128)(2,1)} %get-tuple-element.52.e_ref, bf16[3,2,4,8,16,128]{5,4,3,2,1,0:T(8,128)(2,1)} %queries.1.q_ref, f32[4,2,4,16,128]{4,3,2,1,0:T(8,128)} %add_select_fusion.in_ref, ...), custom_call_target="tpu_custom_call" | custom-call | tf_op jit(solution)/shard_map/gate/pallas_call | solution.py:366
  158.2 6.1 %project_far.1 = (bf16[128,2048]{1,0:T(8,128)(2,1)}, bf16[128,2048]{1,0:T(8,128)(2,1)}) custom-call(s32[4]{0:T(128)} %pad_add_fusion.order, bf16[1,4,128,256]{3,2,1,0:T(8,128)(2,1)} %own_gate.1.own_ref, bf16[3,4,128,256]{3,2,1,0:T(8,128)(2,1)} %gate.1.others_ref, bf16[4,256,4096]{2,1,0:T(8,128)(2,1)} %bitcast.21), custom_call_target="tpu_custom_call" | custom-call | tf_op jit(solution)/shard_map/project_far/pallas_call | solution.py:383
  165.3 2.4 %collective-permute-start.11 = (bf16[128,2048]{1,0:T(8,128)(2,1)}, bf16[128,2048]{1,0:T(8,128)(2,1)S(1)}, u32[]{:S(2)}, u32[]{:S(2)}) collective-permute-start(bf16[128,2048]{1,0:T(8,128)(2,1)} %get-tuple-element.60), channel_id=1, source_target_pairs={{0,32},{32,64},{64,96},{96,0},{1,33},{33,65},{65,97},{97,1},{2,34}... | collective-permute-start | bytes 1572872 | tf_op jit(solution)/shard_map/sum_parts/ppermute | solution.py:20
  167.7 8.9 %project_out.1 = (bf16[128,2048]{1,0:T(8,128)(2,1)}, bf16[128,2048]{1,0:T(8,128)(2,1)}, bf16[128,2048]{1,0:T(8,128)(2,1)}, bf16[128,2048]{1,0:T(8,128)(2,1)}, bf...) custom-call(s32[4]{0:T(128)} %pad_add_fusion.order, bf16[1,4,128,256]{3,2,1,0:T(8,128)(2,1)} %own_gate.1.own_ref, ...), custom_call_target="tpu_custom_call" | custom-call | tf_op jit(solution)/shard_map/project_out/pallas_call | solution.py:383
  176.6 2.8 %collective-permute-done.14 = bf16[128,2048]{1,0:T(8,128)(2,1)S(1)} collective-permute-done((bf16[128,2048]{1,0:T(8,128)(2,1)}, bf16[128,2048]{1,0:T(8,128)(2,1)S(1)}, u32[]{:S(2)}, u32[]{:S(2)}) %collective-permute-start.14) | collective-permute-done | bytes 524320 | tf_op jit(solution)/shard_map/sum_parts/ppermute | solution.py:20
  180.9 1.2 add_convert_fusion.1
  182.1 3.2 %collective-permute-start.12 = (bf16[128,2048]{1,0:T(8,128)(2,1)S(1)}, bf16[128,2048]{1,0:T(8,128)(2,1)S(1)}, u32[]{:S(2)}, u32[]{:S(2)}) collective-permute-start(bf16[128,2048]{1,0:T(8,128)(2,1)S(1)} %add_convert_fusion.1), channel_id=1, source_target_pairs={{0,32},{32,64},{64,96},{96,0},{1,33},{33,65},{65,97},{97,1},{2,34}... | collective-permute-start | bytes 1572872 | tf_op jit(solution)/shard_map/sum_parts/ppermute | solution.py:20
  185.3 6.4 %collective-permute-done.16 = bf16[128,2048]{1,0:T(8,128)(2,1)S(1)} collective-permute-done((bf16[128,2048]{1,0:T(8,128)(2,1)}, bf16[128,2048]{1,0:T(8,128)(2,1)S(1)}, u32[]{:S(2)}, u32[]{:S(2)}) %collective-permute-start.16) | collective-permute-done | bytes 524320 | tf_op jit(solution)/shard_map/sum_parts/ppermute | solution.py:20
  191.7 5.1 %collective-permute-done.15 = bf16[128,2048]{1,0:T(8,128)(2,1)S(1)} collective-permute-done((bf16[128,2048]{1,0:T(8,128)(2,1)S(1)}, bf16[128,2048]{1,0:T(8,128)(2,1)S(1)}, u32[]{:S(2)}, u32[]{:S(2)}) %collective-permute-start.15) | collective-permute-done | bytes 524320 | tf_op jit(solution)/shard_map/sum_parts/ppermute | solution.py:20
  196.9 9.0 %collective-permute-done.13 = bf16[128,2048]{1,0:T(8,128)(2,1)S(1)} collective-permute-done((bf16[128,2048]{1,0:T(8,128)(2,1)}, bf16[128,2048]{1,0:T(8,128)(2,1)S(1)}, u32[]{:S(2)}, u32[]{:S(2)}) %collective-permute-start.13) | collective-permute-done | bytes 524320 | tf_op jit(solution)/shard_map/sum_parts/ppermute | solution.py:20
  206.1 1.3 fusion
  (60 shorter events, 14.1 us)
Async XLA Ops:
  6.5 10.2 %copy-start = (bf16[256,4096]{1,0:T(8,128)(2,1)S(1)}, bf16[256,4096]{1,0:T(8,128)(2,1)}, u32[]{:S(2)}) copy-start(bf16[256,4096]{1,0:T(8,128)(2,1)} %param.15) | copy-start | bytes 6291460
  6.5 99.7 %all-gather.5.cloned.1.call-start = ((), (), s32[]{:S(2)}) async-start(), calls=%async_computation | async-start | bytes 25952256 | tf_op jit(solution)/shard_map/gather_in_weights/all_gather | solution.py:413
  8.8 149.4 %all-gather.7.cloned.1.call-start = ((), (), s32[]{:S(2)}) async-start(), calls=%async_computation.1 | async-start | bytes 9437184 | tf_op jit(solution)/shard_map/gather_out_weights/all_gather | solution.py:432
  9.8 2.7 %collective-permute-start = (bf16[16,4096]{1,0:T(8,128)(2,1)S(1)}, bf16[16,4096]{1,0:T(8,128)(2,1)S(1)}, u32[]{:S(2)}, u32[]{:S(2)}) collective-permute-start(bf16[16,4096]{1,0:T(8,128)(2,1)S(1)} %slice_bitcast_fusion), channel_id=1, source_target_pairs={{0,1},{1,2},{2,3},{3,4},{4,5},{5,6},{6,7},{8,9},{9,10},{10,11},{11... | collective-permute-start | bytes 393224 | tf_op jit(solution)/shard_map/norm/ppermute | solution.py:417
  12.5 0.7 copy-start.8
  16.7 1.6 copy-start.2
  18.4 30.5 %collective-permute-start.1 = (bf16[144,4096]{1,0:T(8,128)(2,1)S(1)}, bf16[144,4096]{1,0:T(8,128)(2,1)S(1)}, u32[]{:S(2)}, u32[]{:S(2)}) collective-permute-start(bf16[144,4096]{1,0:T(8,128)(2,1)S(1)} %copy-done.2), channel_id=1, source_target_pairs={{0,96},{32,0},{64,32},{96,64},{1,97},{33,1},{65,33},{97,65},{2,98}... | collective-permute-start | bytes 3538952 | tf_op jit(solution)/shard_map/gather_tokens/ppermute | solution.py:20
  19.2 29.7 %collective-permute-start.2 = (bf16[144,4096]{1,0:T(8,128)(2,1)S(1)}, bf16[144,4096]{1,0:T(8,128)(2,1)}, u32[]{:S(2)}, u32[]{:S(2)}) collective-permute-start(bf16[144,4096]{1,0:T(8,128)(2,1)S(1)} %copy-done.2), channel_id=1, source_target_pairs={{0,32},{32,64},{64,96},{96,0},{1,33},{33,65},{65,97},{97,1},{2,34}... | collective-permute-start | bytes 3538952 | tf_op jit(solution)/shard_map/gather_tokens/ppermute | solution.py:20
  21.6 48.0 %collective-permute-start.3 = (bf16[144,4096]{1,0:T(8,128)(2,1)S(1)}, bf16[144,4096]{1,0:T(8,128)(2,1)}, u32[]{:S(2)}, u32[]{:S(2)}) collective-permute-start(bf16[144,4096]{1,0:T(8,128)(2,1)S(1)} %copy-done.2), channel_id=1, source_target_pairs={{0,64},{32,96},{64,0},{96,32},{1,65},{33,97},{65,1},{97,33},{2,66}... | collective-permute-start | bytes 3538952 | tf_op jit(solution)/shard_map/gather_tokens/ppermute | solution.py:20
  23.2 6.5 %collective-permute-start.4 = (f32[48,256]{1,0:T(8,128)}, f32[48,256]{1,0:T(8,128)S(1)}, u32[]{:S(2)}, u32[]{:S(2)}) collective-permute-start(f32[48,256]{1,0:T(8,128)} %pack.1.p0), channel_id=1, source_target_pairs={{0,24},{8,0},{16,8},{24,16},{1,25},{9,1},{17,9},{25,17},{2,26},{10... | collective-permute-start | bytes 147464 | tf_op jit(solution)/shard_map/coefficients/ppermute | solution.py:20
  27.2 6.8 %collective-permute-start.5 = (f32[48,256]{1,0:T(8,128)}, f32[48,256]{1,0:T(8,128)S(1)}, u32[]{:S(2)}, u32[]{:S(2)}) collective-permute-start(f32[48,256]{1,0:T(8,128)} %pack.1.p0), channel_id=1, source_target_pairs={{0,8},{8,16},{16,24},{24,0},{1,9},{9,17},{17,25},{25,1},{2,10},{10... | collective-permute-start | bytes 147464 | tf_op jit(solution)/shard_map/coefficients/ppermute | solution.py:20
  29.7 7.2 %copy-start.10 = (f32[48,256]{1,0:T(8,128)}, f32[48,256]{1,0:T(8,128)S(1)}, u32[]{:S(2)}) copy-start(f32[48,256]{1,0:T(8,128)S(1)} %collective-permute-done.4.p1) | copy-start | bytes 147460
  29.7 7.2 %collective-permute-start.6 = (f32[48,256]{1,0:T(8,128)}, f32[48,256]{1,0:T(8,128)S(1)}, u32[]{:S(2)}, u32[]{:S(2)}) collective-permute-start(f32[48,256]{1,0:T(8,128)} %pack.1.p0), channel_id=1, source_target_pairs={{0,16},{8,24},{16,0},{24,8},{1,17},{9,25},{17,1},{25,9},{2,18},{10... | collective-permute-start | bytes 147464 | tf_op jit(solution)/shard_map/coefficients/ppermute | solution.py:20
  34.0 2.8 %copy-start.11 = (f32[48,256]{1,0:T(8,128)}, f32[48,256]{1,0:T(8,128)S(1)}, u32[]{:S(2)}) copy-start(f32[48,256]{1,0:T(8,128)S(1)} %collective-permute-done.5.p2) | copy-start | bytes 147460
  36.9 0.6 copy-start.12
  48.9 20.8 %copy-start.3 = (bf16[144,4096]{1,0:T(8,128)(2,1)}, bf16[144,4096]{1,0:T(8,128)(2,1)S(1)}, u32[]{:S(2)}) copy-start(bf16[144,4096]{1,0:T(8,128)(2,1)S(1)} %collective-permute-done.1.refs_1_) | copy-start | bytes 3538948
  106.2 21.4 %copy-start.9 = (f32[1,2,4,16,128]{4,3,2,1,0:T(8,128)S(1)}, f32[1,2,4,16,128]{4,3,2,1,0:T(8,128)}, u32[]{:S(2)}) copy-start(f32[1,2,4,16,128]{4,3,2,1,0:T(8,128)} %get-tuple-element.46) | copy-start | bytes 196612
  106.2 22.9 %copy-start.5 = (f32[4,2,16,128]{3,2,1,0:T(8,128)S(1)}, f32[4,2,16,128]{3,2,1,0:T(8,128)}, u32[]{:S(2)}) copy-start(f32[4,2,16,128]{3,2,1,0:T(8,128)} %get-tuple-element.45) | copy-start | bytes 196612
  127.7 1.5 collective-permute-start.7
  129.2 19.7 %collective-permute-start.10 = (bf16[4,2,4,16,128]{4,3,2,1,0:T(8,128)(2,1)S(1)}, bf16[4,2,4,16,128]{4,3,2,1,0:T(8,128)(2,1)S(1)}, u32[]{:S(2)}, u32[]{:S(2)}) collective-permute-start(bf16[4,2,4,16,128]{4,3,2,1,0:T(8,128)(2,1)S(1)} %fusion.2), channel_id=1, source_target_pairs={{0,6},{1,7},{8,14},{9,15},{16,22},{17,23},{24,30},{25,31},{32,38},... | collective-permute-start | bytes 393224 | tf_op jit(solution)/shard_map/states/ppermute | solution.py:25
  133.8 15.0 %collective-permute-start.9 = (bf16[4,2,4,16,128]{4,3,2,1,0:T(8,128)(2,1)S(1)}, bf16[4,2,4,16,128]{4,3,2,1,0:T(8,128)(2,1)S(1)}, u32[]{:S(2)}, u32[]{:S(2)}) collective-permute-start(bf16[4,2,4,16,128]{4,3,2,1,0:T(8,128)(2,1)S(1)} %fusion.2), channel_id=1, source_target_pairs={{0,4},{2,6},{1,5},{3,7},{8,12},{10,14},{9,13},{11,15},{16,20},{18,... | collective-permute-start | bytes 393224 | tf_op jit(solution)/shard_map/states/ppermute | solution.py:25
  135.2 13.7 %collective-permute-start.8 = (bf16[4,2,4,16,128]{4,3,2,1,0:T(8,128)(2,1)S(1)}, bf16[4,2,4,16,128]{4,3,2,1,0:T(8,128)(2,1)S(1)}, u32[]{:S(2)}, u32[]{:S(2)}) collective-permute-start(bf16[4,2,4,16,128]{4,3,2,1,0:T(8,128)(2,1)S(1)} %fusion.2), channel_id=1, source_target_pairs={{0,2},{2,4},{4,6},{1,3},{3,5},{5,7},{8,10},{10,12},{12,14},{9,11},... | collective-permute-start | bytes 393224 | tf_op jit(solution)/shard_map/states/ppermute | solution.py:25
  164.4 15.1 %collective-permute-start.14 = (bf16[128,2048]{1,0:T(8,128)(2,1)}, bf16[128,2048]{1,0:T(8,128)(2,1)S(1)}, u32[]{:S(2)}, u32[]{:S(2)}) collective-permute-start(bf16[128,2048]{1,0:T(8,128)(2,1)} %get-tuple-element.63), channel_id=1, source_target_pairs={{0,96},{32,0},{64,32},{96,64},{1,97},{33,1},{65,33},{97,65},{2,98}... | collective-permute-start | bytes 1572872 | tf_op jit(solution)/shard_map/sum_parts/ppermute | solution.py:20
  165.3 15.6 %collective-permute-start.11 = (bf16[128,2048]{1,0:T(8,128)(2,1)}, bf16[128,2048]{1,0:T(8,128)(2,1)S(1)}, u32[]{:S(2)}, u32[]{:S(2)}) collective-permute-start(bf16[128,2048]{1,0:T(8,128)(2,1)} %get-tuple-element.60), channel_id=1, source_target_pairs={{0,32},{32,64},{64,96},{96,0},{1,33},{33,65},{65,97},{97,1},{2,34}... | collective-permute-start | bytes 1572872 | tf_op jit(solution)/shard_map/sum_parts/ppermute | solution.py:20
  176.6 15.1 %collective-permute-start.16 = (bf16[128,2048]{1,0:T(8,128)(2,1)}, bf16[128,2048]{1,0:T(8,128)(2,1)S(1)}, u32[]{:S(2)}, u32[]{:S(2)}) collective-permute-start(bf16[128,2048]{1,0:T(8,128)(2,1)} %get-tuple-element.64), channel_id=1, source_target_pairs={{0,32},{32,64},{64,96},{96,0},{1,33},{33,65},{65,97},{97,1},{2,34}... | collective-permute-start | bytes 1572872 | tf_op jit(solution)/shard_map/sum_parts/ppermute | solution.py:20
  180.6 16.1 %collective-permute-start.15 = (bf16[128,2048]{1,0:T(8,128)(2,1)S(1)}, bf16[128,2048]{1,0:T(8,128)(2,1)S(1)}, u32[]{:S(2)}, u32[]{:S(2)}) collective-permute-start(bf16[128,2048]{1,0:T(8,128)(2,1)S(1)} %add_convert_fusion), channel_id=1, source_target_pairs={{0,96},{32,0},{64,32},{96,64},{1,97},{33,1},{65,33},{97,65},{2,98}... | collective-permute-start | bytes 1572872 | tf_op jit(solution)/shard_map/sum_parts/ppermute | solution.py:20
  180.7 25.2 %collective-permute-start.13 = (bf16[128,2048]{1,0:T(8,128)(2,1)}, bf16[128,2048]{1,0:T(8,128)(2,1)S(1)}, u32[]{:S(2)}, u32[]{:S(2)}) collective-permute-start(bf16[128,2048]{1,0:T(8,128)(2,1)} %get-tuple-element.61), channel_id=1, source_target_pairs={{0,96},{32,0},{64,32},{96,64},{1,97},{33,1},{65,33},{97,65},{2,98}... | collective-permute-start | bytes 1572872 | tf_op jit(solution)/shard_map/sum_parts/ppermute | solution.py:20
  182.1 24.0 %copy-start.4 = (bf16[1,128,4096]{2,1,0:T(8,128)(2,1)S(1)}, bf16[1,128,4096]{2,1,0:T(8,128)(2,1)}, u32[]{:S(2)}) copy-start(bf16[1,128,4096]{2,1,0:T(8,128)(2,1)} %tokens_ref.1) | copy-start | bytes 3145732
  182.1 23.9 %copy-start.6 = (bf16[128,2048]{1,0:T(8,128)(2,1)S(1)}, bf16[128,2048]{1,0:T(8,128)(2,1)}, u32[]{:S(2)}) copy-start(bf16[128,2048]{1,0:T(8,128)(2,1)} %get-tuple-element.57) | copy-start | bytes 1572868
  182.1 23.9 %copy-start.7 = (bf16[128,2048]{1,0:T(8,128)(2,1)S(1)}, bf16[128,2048]{1,0:T(8,128)(2,1)}, u32[]{:S(2)}) copy-start(bf16[128,2048]{1,0:T(8,128)(2,1)} %get-tuple-element.58) | copy-start | bytes 1572868
  182.1 23.8 %collective-permute-start.12 = (bf16[128,2048]{1,0:T(8,128)(2,1)S(1)}, bf16[128,2048]{1,0:T(8,128)(2,1)S(1)}, u32[]{:S(2)}, u32[]{:S(2)}) collective-permute-start(bf16[128,2048]{1,0:T(8,128)(2,1)S(1)} %add_convert_fusion.1), channel_id=1, source_target_pairs={{0,32},{32,64},{64,96},{96,0},{1,33},{33,65},{65,97},{97,1},{2,34}... | collective-permute-start | bytes 1572872 | tf_op jit(solution)/shard_map/sum_parts/ppermute | solution.py:20
  206.0 2.0 copy-start.1
Sparse Core Ops, SparseCore 0:
  9.6 96.5 all-gather.4
  107.9 49.2 all-gather.6

commit v5 on v4

--- a/solution.py
+++ b/solution.py
@@ -104,12 +104,13 @@
     return jnp.dot(a, b, preferred_element_type=F32)
 
 
-def project(x, w, scratch):
+def project(x, w, *scratches):
     total = dot(x[...], w[...]).astype(BF16).astype(F32)
-    lanes, seqs = scratch.shape[:2]
+    lanes, seqs = scratches[0].shape[:2]
     first_row = lax.broadcasted_iota(jnp.int32, (8, 128), 0) == 0
-    for lane in range(lanes):
-        cols = slice(lane * 128, (lane + 1) * 128)
+    for column in range(lanes * len(scratches)):
+        scratch, lane = scratches[column // lanes], column % lanes
+        cols = slice(column * 128, (column + 1) * 128)
         for s in range(seqs):
             first = s * (HEAD + 8 * CHUNK) + HEAD
             edge = total[first - 8 : first, cols]
@@ -148,7 +149,7 @@
     blocks = w.shape[0]
     for block in range(blocks):
         for i, stream in enumerate((KEY, VALUE)):
-            start_weights(order, w_ref, stream, block + first, w.at[block, i], w_sems.at[block])
+            start_weights(order, w_ref, stream, block + first, w.at[block, :, pl.ds(i * 256, 256)], w_sems.at[block])
         if block == 0:
             start_rows(row_refs, x, row_sem)
     first_row = lax.broadcasted_iota(jnp.int32, (8, 128), 0)
@@ -156,8 +157,7 @@
 
     def each_block(block, carry):
         wait_for(w.at[block], w_sems.at[block])
-        project(x, w.at[block, 0], fk)
-        project(x, w.at[block, 1], fv)
+        project(x, w.at[block], fk, fv)
         c = block + first
 
         def unit(lane, s):
@@ -317,7 +317,7 @@
         out_specs=[IN_PLACE, IN_PLACE, IN_VMEM],
         scratch_shapes=[
             pltpu.VMEM((seqs * high, width), BF16),
-            pltpu.VMEM((blocks, 2, width, lanes * 128), BF16),
+            pltpu.VMEM((blocks, width, 2 * lanes * 128), BF16),
             features,
             features,
             pltpu.VMEM(by_chunk, BF16),
@@ -378,7 +378,7 @@
 def project_out(order, seqs, own, others, w, name):
     length, channels = own.shape[2:]
     blocks, half = w.shape[0], w.shape[2] // 2
-    cols = 4 * channels
+    cols = 8 * channels
     tiles = w.shape[2] // cols
     return pl.pallas_call(
         functools.partial(out_kernel, seqs),
@@ -476,11 +476,9 @@
         added = (near.astype(F32) + passing.astype(F32)).astype(BF16)
         added_b = (back_b.astype(F32) + passing_b.astype(F32)).astype(BF16)
         added, added_b = from_ahead(added, "x", -1), from_ahead(added_b, "x", 1)
-        others = jnp.concatenate(
-            [added.astype(F32) + direct.astype(F32), added_b.astype(F32) + direct_b.astype(F32)], axis=1
-        )
-        own = jnp.concatenate([own, own_b], axis=1)
-        return (tokens[0].astype(F32) + own.astype(F32) + others).astype(BF16)[None]
+        base = tokens[0].astype(F32) + jnp.concatenate([own, own_b], axis=1).astype(F32)
+        base = lax.optimization_barrier(base + jnp.concatenate([direct, direct_b], axis=1).astype(F32))
+        return (base + jnp.concatenate([added, added_b], axis=1).astype(F32)).astype(BF16)[None]
 
 
 def solution(mesh):

time: 216 us -> 213 us (0.986); the launches traced: 215 us -> 210 us
  waiting for transfers between devices: 81.1 us -> 75.8 us
    ppermute x13, waiting for transfers between devices: 60.6 us -> 55.3 us  [from_ahead(): lax.ppermute(value, axis, [(i, (i - steps) % count) for i in range(count)])]
where the time goes in v5:
time: 213 us; the launch traced here: 210 us
  Pallas kernels  77.7 us (36%)
  waiting for transfers between devices  75.8 us (36%)
  starting transfers between devices  30 us (14%)
  between operations  13.6 us (6%)
  other arithmetic  6.42 us (3%)
  local copies, waits for them, and re-layouts  6.07 us (3%)
    ppermute x13, waiting for transfers between devices, from_ahead(): lax.ppermute(value, axis, [(i, (i - steps) % count) for i in range(count)])  55.3 us
    pallas_call x2, Pallas kernels, keys_values(): pl.pallas_call(functools.partial(kv_kernel, first, seqs), in_specs=[IN_SM...  30.9 us
    all_gather x1, waiting for transfers between devices, shards(): lax.all_gather(share, ('z', 'y', 'c'), axis=0)  19.5 us
    ppermute x13, starting transfers between devices, from_ahead(): lax.ppermute(value, axis, [(i, (i - steps) % count) for i in range(count)])  19.4 us
    pallas_call x2, Pallas kernels, queries(): pl.pallas_call(functools.partial(q_kernel, first, seqs), in_specs=[IN_SME...  17.4 us
    pallas_call x2, Pallas kernels, project_out(): pl.pallas_call(functools.partial(out_kernel, seqs), in_specs=[IN_SMEM] +...  13.8 us
    ppermute x3, starting transfers between devices, from_behind(): lax.ppermute(value, axis, [(i, i + steps) for i in range(count - steps)])  8.87 us
    pallas_call x2, Pallas kernels, gate(): pl.pallas_call(gate_kernel, grid=(blocks, lanes), in_specs=[at(a, 0) for...  8.49 us
  transfers between devices with their start and end apart: 19, of which 12 were waited for; matrix products, arithmetic and copies ran while one was open for 3% of the time, Pallas kernels for 34%

profile of v5, /device:TPU:6, one launch (start us, length us, event | category | flops | bytes accessed | tf_op | source)
XLA Modules:
  0.0 209.7 jit_solution(5044354319532617466)
XLA Ops:
  6.5 2.2 %dynamic-slice_bitcast_fusion = bf16[3,512,256]{2,1,0:T(8,128)(2,1)} fusion(bf16[4096,3,256]{2,0,1:T(8,128)(2,1)} %param.10, s32[]{:T(128)S(6)} %select_n.45), kind=kLoop, calls=%fused_computation.6 | loop fusion | bytes 1572868 | tf_op jit(solution)/shard_map/gather_in_weights/dynamic_slice | solution.py:412
  9.8 1.7 collective-permute-start
  13.1 3.6 %norm.1.refs_0_ = bf16[144,4096]{1,0:T(8,128)(2,1)} custom-call(bf16[16,4096]{1,0:T(8,128)(2,1)} %copy-done.8, bf16[1,128,4096]{2,1,0:T(8,128)(2,1)} %tokens_ref.1, f32[1,4096]{1,0:T(1,128)} %bitcast.24), custom_call_target="tpu_custom_call" | custom-call | tf_op jit(solution)/shard_map/norm/norm/pallas_call | solution.py:418
  19.2 2.4 %collective-permute-start.2 = (bf16[144,4096]{1,0:T(8,128)(2,1)S(1)}, bf16[144,4096]{1,0:T(8,128)(2,1)}, u32[]{:S(2)}, u32[]{:S(2)}) collective-permute-start(bf16[144,4096]{1,0:T(8,128)(2,1)S(1)} %copy-done.2), channel_id=1, source_target_pairs={{0,32},{32,64},{64,96},{96,0},{1,33},{33,65},{65,97},{97,1},{2,34}... | collective-permute-start | bytes 3538952 | tf_op jit(solution)/shard_map/gather_tokens/ppermute | solution.py:20
  21.8 1.4 pack.1.p0
  23.2 4.0 %collective-permute-start.4 = (f32[48,256]{1,0:T(8,128)}, f32[48,256]{1,0:T(8,128)S(1)}, u32[]{:S(2)}, u32[]{:S(2)}) collective-permute-start(f32[48,256]{1,0:T(8,128)} %pack.1.p0), channel_id=1, source_target_pairs={{0,24},{8,0},{16,8},{24,16},{1,25},{9,1},{17,9},{25,17},{2,26},{10... | collective-permute-start | bytes 147464 | tf_op jit(solution)/shard_map/coefficients/ppermute | solution.py:20
  27.2 2.5 %collective-permute-done.4.p1 = f32[48,256]{1,0:T(8,128)S(1)} collective-permute-done((f32[48,256]{1,0:T(8,128)}, f32[48,256]{1,0:T(8,128)S(1)}, u32[]{:S(2)}, u32[]{:S(2)}) %collective-permute-start.4) | collective-permute-done | bytes 49184 | tf_op jit(solution)/shard_map/coefficients/ppermute | solution.py:20
  29.7 2.8 %collective-permute-start.6 = (f32[48,256]{1,0:T(8,128)}, f32[48,256]{1,0:T(8,128)S(1)}, u32[]{:S(2)}, u32[]{:S(2)}) collective-permute-start(f32[48,256]{1,0:T(8,128)} %pack.1.p0), channel_id=1, source_target_pairs={{0,16},{8,24},{16,0},{24,8},{1,17},{9,25},{17,1},{25,9},{2,18},{10... | collective-permute-start | bytes 147464 | tf_op jit(solution)/shard_map/coefficients/ppermute | solution.py:20
  34.0 2.8 %collective-permute-done.6.p3 = f32[48,256]{1,0:T(8,128)S(1)} collective-permute-done((f32[48,256]{1,0:T(8,128)}, f32[48,256]{1,0:T(8,128)S(1)}, u32[]{:S(2)}, u32[]{:S(2)}) %collective-permute-start.6) | collective-permute-done | bytes 49184 | tf_op jit(solution)/shard_map/coefficients/ppermute | solution.py:20
  37.5 2.2 %coefficients.1 = (f32[4,2,16,128]{3,2,1,0:T(8,128)}, f32[4,2,16,128]{3,2,1,0:T(8,128)}, f32[4,2,16,128]{3,2,1,0:T(8,128)}, f32[4,2,3,16,128]{4,3,2,1,0:T(8,128)...) custom-call(f32[48,256]{1,0:T(8,128)} %pack.1.p0, f32[48,256]{1,0:T(8,128)} %copy-done.10, ...), custom_call_target="tpu_custom_call" | custom-call | tf_op jit(solution)/shard_map/coefficients/coefficients/pallas_call | solution.py:439
  39.7 9.2 %collective-permute-done.1.refs_1_ = bf16[144,4096]{1,0:T(8,128)(2,1)S(1)} collective-permute-done((bf16[144,4096]{1,0:T(8,128)(2,1)S(1)}, bf16[144,4096]{1,0:T(8,128)(2,1)S(1)}, u32[]{:S(2)}, u32[]{:S(2)}) %collective-permute-start.1) | collective-permute-done | bytes 1179680 | tf_op jit(solution)/shard_map/gather_tokens/ppermute | solution.py:20
  48.9 20.8 %collective-permute-done.3.refs_3_ = bf16[144,4096]{1,0:T(8,128)(2,1)} collective-permute-done((bf16[144,4096]{1,0:T(8,128)(2,1)S(1)}, bf16[144,4096]{1,0:T(8,128)(2,1)}, u32[]{:S(2)}, u32[]{:S(2)}) %collective-permute-start.3) | collective-permute-done | bytes 1179680 | tf_op jit(solution)/shard_map/gather_tokens/ppermute | solution.py:20
  69.6 6.6 %own_queries.1.q_ref = bf16[1,2,4,8,16,128]{5,4,3,2,1,0:T(8,128)(2,1)} custom-call(s32[4]{0:T(128)} %pad_add_fusion.order, bf16[3,4096,256]{2,1,0:T(8,128)(2,1)} %bitcast.22, bf16[144,4096]{1,0:T(8,128)(2,1)} %norm.1.refs_0_, bf16[144,4096]{1,0:T(8,128)(2,1)} %copy-done.3, bf16[144,4096]{1,0:T(8,128)(2,1)} %collective-permute-done.2.refs_2_, ...), custom_call_target="tpu_custom_call" | custom-call | tf_op jit(solution)/shard_map/own_queries/pallas_call | solution.py:343
  76.2 10.4 %own_keys_values.1 = (bf16[1,2,4,8,16,128]{5,4,3,2,1,0:T(8,128)(2,1)}, bf16[1,2,4,8,16,128]{5,4,3,2,1,0:T(8,128)(2,1)}, f32[1,2,4,16,128]{4,3,2,1,0:T(8,128)}) custom-call(s32[4]{0:T(128)} %pad_add_fusion.order, bf16[3,4096,256]{2,1,0:T(8,128)(2,1)} %bitcast.23, bf16[144,4096]{1,0:T(8,128)(2,1)} %norm.1.refs_0_, bf16[144,4096]{1,0:T(8,128)(2,1)} %copy-done.3, ...), custom_call_target="tpu_custom_call" | custom-call | tf_op jit(solution)/shard_map/own_keys_values/pallas_call | solution.py:314
  86.7 19.5 %all-gather.5.cloned.1.call-done = bf16[96,512,256]{2,1,0:T(8,128)(2,1)} async-done(((bf16[3,512,256]{2,1,0:T(8,128)(2,1)}), bf16[96,512,256]{2,1,0:T(8,128)(2,1)}) %all-gather.5.cloned.1.call-update) | async-done | bytes 25165840 | tf_op jit(solution)/shard_map/gather_in_weights/all_gather | solution.py:413
  106.2 20.4 %keys_values.1 = (bf16[3,2,4,8,16,128]{5,4,3,2,1,0:T(8,128)(2,1)}, bf16[3,2,4,8,16,128]{5,4,3,2,1,0:T(8,128)(2,1)}, f32[3,2,4,16,128]{4,3,2,1,0:T(8,128)}) custom-call(s32[4]{0:T(128)} %pad_add_fusion.order, bf16[4,8,3,512,256]{4,3,2,1,0:T(8,128)(2,1)} %bitcast.18, bf16[144,4096]{1,0:T(8,128)(2,1)} %norm.1.refs_0_, bf16[144,4096]{1,0:T(8,128)(2,1)} %copy-done.3, ...), custom_call_target="tpu_custom_call" | custom-call | tf_op jit(solution)/shard_map/keys_values/pallas_call | solution.py:314
  129.2 4.6 %collective-permute-start.10 = (bf16[4,2,4,16,128]{4,3,2,1,0:T(8,128)(2,1)S(1)}, bf16[4,2,4,16,128]{4,3,2,1,0:T(8,128)(2,1)S(1)}, u32[]{:S(2)}, u32[]{:S(2)}) collective-permute-start(bf16[4,2,4,16,128]{4,3,2,1,0:T(8,128)(2,1)S(1)} %fusion.3), channel_id=1, source_target_pairs={{0,6},{1,7},{8,14},{9,15},{16,22},{17,23},{24,30},{25,31},{32,38},... | collective-permute-start | bytes 393224 | tf_op jit(solution)/shard_map/states/ppermute | solution.py:25
  133.8 1.3 collective-permute-start.9
  135.1 2.9 %collective-permute-start.8 = (bf16[4,2,4,16,128]{4,3,2,1,0:T(8,128)(2,1)S(1)}, bf16[4,2,4,16,128]{4,3,2,1,0:T(8,128)(2,1)S(1)}, u32[]{:S(2)}, u32[]{:S(2)}) collective-permute-start(bf16[4,2,4,16,128]{4,3,2,1,0:T(8,128)(2,1)S(1)} %fusion.3), channel_id=1, source_target_pairs={{0,2},{2,4},{4,6},{1,3},{3,5},{5,7},{8,10},{10,12},{12,14},{9,11},... | collective-permute-start | bytes 393224 | tf_op jit(solution)/shard_map/states/ppermute | solution.py:25
  138.1 10.7 %queries.1.q_ref = bf16[3,2,4,8,16,128]{5,4,3,2,1,0:T(8,128)(2,1)} custom-call(s32[4]{0:T(128)} %pad_add_fusion.order, bf16[4,8,3,512,256]{4,3,2,1,0:T(8,128)(2,1)} %bitcast.19, bf16[144,4096]{1,0:T(8,128)(2,1)} %norm.1.refs_0_, bf16[144,4096]{1,0:T(8,128)(2,1)} %copy-done.3, bf16[144,4096]{1,0:T(8,128)(2,1)} %collective-permute-done.2.refs_2_, ...), custom_call_target="tpu_custom_call" | custom-call | tf_op jit(solution)/shard_map/queries/pallas_call | solution.py:343
  149.7 2.6 %own_gate.1.own_ref = bf16[1,4,128,256]{3,2,1,0:T(8,128)(2,1)} custom-call(bf16[1,2,4,8,16,128]{5,4,3,2,1,0:T(8,128)(2,1)} %get-tuple-element.42.y_ref, bf16[1,2,4,8,16,128]{5,4,3,2,1,0:T(8,128)(2,1)} %get-tuple-element.43.e_ref, bf16[1,2,4,8,16,128]{5,4,3,2,1,0:T(8,128)(2,1)} %own_queries.1.q_ref, f32[4,2,4,16,128]{4,3,2,1,0:T(8,128)} %add_select_fusion.in_ref, ...), custom_call_target="tpu_custom_call" | custom-call | tf_op jit(solution)/shard_map/own_gate/pallas_call | solution.py:366
  152.3 5.9 %gate.1.others_ref = bf16[3,4,128,256]{3,2,1,0:T(8,128)(2,1)} custom-call(bf16[3,2,4,8,16,128]{5,4,3,2,1,0:T(8,128)(2,1)} %get-tuple-element.51.y_ref, bf16[3,2,4,8,16,128]{5,4,3,2,1,0:T(8,128)(2,1)} %get-tuple-element.52.e_ref, bf16[3,2,4,8,16,128]{5,4,3,2,1,0:T(8,128)(2,1)} %queries.1.q_ref, f32[4,2,4,16,128]{4,3,2,1,0:T(8,128)} %add_select_fusion.in_ref, ...), custom_call_target="tpu_custom_call" | custom-call | tf_op jit(solution)/shard_map/gate/pallas_call | solution.py:366
  158.2 5.8 %project_far.1 = (bf16[128,2048]{1,0:T(8,128)(2,1)}, bf16[128,2048]{1,0:T(8,128)(2,1)}) custom-call(s32[4]{0:T(128)} %pad_add_fusion.order, bf16[1,4,128,256]{3,2,1,0:T(8,128)(2,1)} %own_gate.1.own_ref, bf16[3,4,128,256]{3,2,1,0:T(8,128)(2,1)} %gate.1.others_ref, bf16[4,256,4096]{2,1,0:T(8,128)(2,1)} %bitcast.20), custom_call_target="tpu_custom_call" | custom-call | tf_op jit(solution)/shard_map/project_far/pallas_call | solution.py:383
  165.0 2.4 %collective-permute-start.13 = (bf16[128,2048]{1,0:T(8,128)(2,1)}, bf16[128,2048]{1,0:T(8,128)(2,1)S(1)}, u32[]{:S(2)}, u32[]{:S(2)}) collective-permute-start(bf16[128,2048]{1,0:T(8,128)(2,1)} %get-tuple-element.62), channel_id=1, source_target_pairs={{0,32},{32,64},{64,96},{96,0},{1,33},{33,65},{65,97},{97,1},{2,34}... | collective-permute-start | bytes 1572872 | tf_op jit(solution)/shard_map/sum_parts/ppermute | solution.py:20
  167.4 8.0 %project_out.1 = (bf16[128,2048]{1,0:T(8,128)(2,1)}, bf16[128,2048]{1,0:T(8,128)(2,1)}, bf16[128,2048]{1,0:T(8,128)(2,1)}, bf16[128,2048]{1,0:T(8,128)(2,1)}, bf...) custom-call(s32[4]{0:T(128)} %pad_add_fusion.order, bf16[1,4,128,256]{3,2,1,0:T(8,128)(2,1)} %own_gate.1.own_ref, ...), custom_call_target="tpu_custom_call" | custom-call | tf_op jit(solution)/shard_map/project_out/pallas_call | solution.py:383
  175.5 2.0 collective-permute-start.11
  177.5 1.9 collective-permute-done.15
  180.7 1.2 add_convert_fusion.2
  181.9 3.3 %collective-permute-start.14 = (bf16[128,2048]{1,0:T(8,128)(2,1)S(1)}, bf16[128,2048]{1,0:T(8,128)(2,1)S(1)}, u32[]{:S(2)}, u32[]{:S(2)}) collective-permute-start(bf16[128,2048]{1,0:T(8,128)(2,1)S(1)} %add_convert_fusion.2), channel_id=1, source_target_pairs={{0,32},{32,64},{64,96},{96,0},{1,33},{33,65},{65,97},{97,1},{2,34}... | collective-permute-start | bytes 1572872 | tf_op jit(solution)/shard_map/sum_parts/ppermute | solution.py:20
  185.2 6.1 %collective-permute-done.12 = bf16[128,2048]{1,0:T(8,128)(2,1)S(1)} collective-permute-done((bf16[128,2048]{1,0:T(8,128)(2,1)}, bf16[128,2048]{1,0:T(8,128)(2,1)S(1)}, u32[]{:S(2)}, u32[]{:S(2)}) %collective-permute-start.12) | collective-permute-done | bytes 524320 | tf_op jit(solution)/shard_map/sum_parts/ppermute | solution.py:20
  192.3 9.3 %collective-permute-done.16 = bf16[128,2048]{1,0:T(8,128)(2,1)S(1)} collective-permute-done((bf16[128,2048]{1,0:T(8,128)(2,1)S(1)}, bf16[128,2048]{1,0:T(8,128)(2,1)S(1)}, u32[]{:S(2)}, u32[]{:S(2)}) %collective-permute-start.16) | collective-permute-done | bytes 524320 | tf_op jit(solution)/shard_map/sum_parts/ppermute | solution.py:20
  201.6 1.2 fusion.1
  (59 shorter events, 14.0 us)
Async XLA Ops:
  6.5 10.2 %copy-start = (bf16[256,4096]{1,0:T(8,128)(2,1)S(1)}, bf16[256,4096]{1,0:T(8,128)(2,1)}, u32[]{:S(2)}) copy-start(bf16[256,4096]{1,0:T(8,128)(2,1)} %param.15) | copy-start | bytes 6291460
  6.5 99.7 %all-gather.5.cloned.1.call-start = ((), (), s32[]{:S(2)}) async-start(), calls=%async_computation | async-start | bytes 25952256 | tf_op jit(solution)/shard_map/gather_in_weights/all_gather | solution.py:413
  8.8 149.4 %all-gather.7.cloned.1.call-start = ((), (), s32[]{:S(2)}) async-start(), calls=%async_computation.1 | async-start | bytes 9437184 | tf_op jit(solution)/shard_map/gather_out_weights/all_gather | solution.py:432
  9.8 2.7 %collective-permute-start = (bf16[16,4096]{1,0:T(8,128)(2,1)S(1)}, bf16[16,4096]{1,0:T(8,128)(2,1)S(1)}, u32[]{:S(2)}, u32[]{:S(2)}) collective-permute-start(bf16[16,4096]{1,0:T(8,128)(2,1)S(1)} %slice_bitcast_fusion), channel_id=1, source_target_pairs={{0,1},{1,2},{2,3},{3,4},{4,5},{5,6},{6,7},{8,9},{9,10},{10,11},{11... | collective-permute-start | bytes 393224 | tf_op jit(solution)/shard_map/norm/ppermute | solution.py:417
  12.5 0.7 copy-start.8
  16.7 1.6 copy-start.2
  18.4 30.5 %collective-permute-start.1 = (bf16[144,4096]{1,0:T(8,128)(2,1)S(1)}, bf16[144,4096]{1,0:T(8,128)(2,1)S(1)}, u32[]{:S(2)}, u32[]{:S(2)}) collective-permute-start(bf16[144,4096]{1,0:T(8,128)(2,1)S(1)} %copy-done.2), channel_id=1, source_target_pairs={{0,96},{32,0},{64,32},{96,64},{1,97},{33,1},{65,33},{97,65},{2,98}... | collective-permute-start | bytes 3538952 | tf_op jit(solution)/shard_map/gather_tokens/ppermute | solution.py:20
  19.2 29.7 %collective-permute-start.2 = (bf16[144,4096]{1,0:T(8,128)(2,1)S(1)}, bf16[144,4096]{1,0:T(8,128)(2,1)}, u32[]{:S(2)}, u32[]{:S(2)}) collective-permute-start(bf16[144,4096]{1,0:T(8,128)(2,1)S(1)} %copy-done.2), channel_id=1, source_target_pairs={{0,32},{32,64},{64,96},{96,0},{1,33},{33,65},{65,97},{97,1},{2,34}... | collective-permute-start | bytes 3538952 | tf_op jit(solution)/shard_map/gather_tokens/ppermute | solution.py:20
  21.6 48.0 %collective-permute-start.3 = (bf16[144,4096]{1,0:T(8,128)(2,1)S(1)}, bf16[144,4096]{1,0:T(8,128)(2,1)}, u32[]{:S(2)}, u32[]{:S(2)}) collective-permute-start(bf16[144,4096]{1,0:T(8,128)(2,1)S(1)} %copy-done.2), channel_id=1, source_target_pairs={{0,64},{32,96},{64,0},{96,32},{1,65},{33,97},{65,1},{97,33},{2,66}... | collective-permute-start | bytes 3538952 | tf_op jit(solution)/shard_map/gather_tokens/ppermute | solution.py:20
  23.2 6.5 %collective-permute-start.4 = (f32[48,256]{1,0:T(8,128)}, f32[48,256]{1,0:T(8,128)S(1)}, u32[]{:S(2)}, u32[]{:S(2)}) collective-permute-start(f32[48,256]{1,0:T(8,128)} %pack.1.p0), channel_id=1, source_target_pairs={{0,24},{8,0},{16,8},{24,16},{1,25},{9,1},{17,9},{25,17},{2,26},{10... | collective-permute-start | bytes 147464 | tf_op jit(solution)/shard_map/coefficients/ppermute | solution.py:20
  27.2 6.8 %collective-permute-start.5 = (f32[48,256]{1,0:T(8,128)}, f32[48,256]{1,0:T(8,128)S(1)}, u32[]{:S(2)}, u32[]{:S(2)}) collective-permute-start(f32[48,256]{1,0:T(8,128)} %pack.1.p0), channel_id=1, source_target_pairs={{0,8},{8,16},{16,24},{24,0},{1,9},{9,17},{17,25},{25,1},{2,10},{10... | collective-permute-start | bytes 147464 | tf_op jit(solution)/shard_map/coefficients/ppermute | solution.py:20
  29.7 7.2 %copy-start.10 = (f32[48,256]{1,0:T(8,128)}, f32[48,256]{1,0:T(8,128)S(1)}, u32[]{:S(2)}) copy-start(f32[48,256]{1,0:T(8,128)S(1)} %collective-permute-done.4.p1) | copy-start | bytes 147460
  29.7 7.2 %collective-permute-start.6 = (f32[48,256]{1,0:T(8,128)}, f32[48,256]{1,0:T(8,128)S(1)}, u32[]{:S(2)}, u32[]{:S(2)}) collective-permute-start(f32[48,256]{1,0:T(8,128)} %pack.1.p0), channel_id=1, source_target_pairs={{0,16},{8,24},{16,0},{24,8},{1,17},{9,25},{17,1},{25,9},{2,18},{10... | collective-permute-start | bytes 147464 | tf_op jit(solution)/shard_map/coefficients/ppermute | solution.py:20
  34.0 2.8 %copy-start.11 = (f32[48,256]{1,0:T(8,128)}, f32[48,256]{1,0:T(8,128)S(1)}, u32[]{:S(2)}) copy-start(f32[48,256]{1,0:T(8,128)S(1)} %collective-permute-done.5.p2) | copy-start | bytes 147460
  36.9 0.6 copy-start.12
  48.9 20.8 %copy-start.3 = (bf16[144,4096]{1,0:T(8,128)(2,1)}, bf16[144,4096]{1,0:T(8,128)(2,1)S(1)}, u32[]{:S(2)}) copy-start(bf16[144,4096]{1,0:T(8,128)(2,1)S(1)} %collective-permute-done.1.refs_1_) | copy-start | bytes 3538948
  106.2 21.4 %copy-start.9 = (f32[1,2,4,16,128]{4,3,2,1,0:T(8,128)S(1)}, f32[1,2,4,16,128]{4,3,2,1,0:T(8,128)}, u32[]{:S(2)}) copy-start(f32[1,2,4,16,128]{4,3,2,1,0:T(8,128)} %get-tuple-element.46) | copy-start | bytes 196612
  106.2 22.9 %copy-start.5 = (f32[4,2,16,128]{3,2,1,0:T(8,128)S(1)}, f32[4,2,16,128]{3,2,1,0:T(8,128)}, u32[]{:S(2)}) copy-start(f32[4,2,16,128]{3,2,1,0:T(8,128)} %get-tuple-element.45) | copy-start | bytes 196612
  127.7 1.5 collective-permute-start.7
  129.2 19.7 %collective-permute-start.10 = (bf16[4,2,4,16,128]{4,3,2,1,0:T(8,128)(2,1)S(1)}, bf16[4,2,4,16,128]{4,3,2,1,0:T(8,128)(2,1)S(1)}, u32[]{:S(2)}, u32[]{:S(2)}) collective-permute-start(bf16[4,2,4,16,128]{4,3,2,1,0:T(8,128)(2,1)S(1)} %fusion.3), channel_id=1, source_target_pairs={{0,6},{1,7},{8,14},{9,15},{16,22},{17,23},{24,30},{25,31},{32,38},... | collective-permute-start | bytes 393224 | tf_op jit(solution)/shard_map/states/ppermute | solution.py:25
  133.8 15.0 %collective-permute-start.9 = (bf16[4,2,4,16,128]{4,3,2,1,0:T(8,128)(2,1)S(1)}, bf16[4,2,4,16,128]{4,3,2,1,0:T(8,128)(2,1)S(1)}, u32[]{:S(2)}, u32[]{:S(2)}) collective-permute-start(bf16[4,2,4,16,128]{4,3,2,1,0:T(8,128)(2,1)S(1)} %fusion.3), channel_id=1, source_target_pairs={{0,4},{2,6},{1,5},{3,7},{8,12},{10,14},{9,13},{11,15},{16,20},{18,... | collective-permute-start | bytes 393224 | tf_op jit(solution)/shard_map/states/ppermute | solution.py:25
  135.1 13.7 %collective-permute-start.8 = (bf16[4,2,4,16,128]{4,3,2,1,0:T(8,128)(2,1)S(1)}, bf16[4,2,4,16,128]{4,3,2,1,0:T(8,128)(2,1)S(1)}, u32[]{:S(2)}, u32[]{:S(2)}) collective-permute-start(bf16[4,2,4,16,128]{4,3,2,1,0:T(8,128)(2,1)S(1)} %fusion.3), channel_id=1, source_target_pairs={{0,2},{2,4},{4,6},{1,3},{3,5},{5,7},{8,10},{10,12},{12,14},{9,11},... | collective-permute-start | bytes 393224 | tf_op jit(solution)/shard_map/states/ppermute | solution.py:25
  164.0 15.4 %collective-permute-start.15 = (bf16[128,2048]{1,0:T(8,128)(2,1)}, bf16[128,2048]{1,0:T(8,128)(2,1)S(1)}, u32[]{:S(2)}, u32[]{:S(2)}) collective-permute-start(bf16[128,2048]{1,0:T(8,128)(2,1)} %get-tuple-element.64), channel_id=1, source_target_pairs={{0,96},{32,0},{64,32},{96,64},{1,97},{33,1},{65,33},{97,65},{2,98}... | collective-permute-start | bytes 1572872 | tf_op jit(solution)/shard_map/sum_parts/ppermute | solution.py:20
  165.0 15.7 %collective-permute-start.13 = (bf16[128,2048]{1,0:T(8,128)(2,1)}, bf16[128,2048]{1,0:T(8,128)(2,1)S(1)}, u32[]{:S(2)}, u32[]{:S(2)}) collective-permute-start(bf16[128,2048]{1,0:T(8,128)(2,1)} %get-tuple-element.62), channel_id=1, source_target_pairs={{0,32},{32,64},{64,96},{96,0},{1,33},{33,65},{65,97},{97,1},{2,34}... | collective-permute-start | bytes 1572872 | tf_op jit(solution)/shard_map/sum_parts/ppermute | solution.py:20
  175.4 16.5 %copy-start.4 = (bf16[1,128,4096]{2,1,0:T(8,128)(2,1)S(1)}, bf16[1,128,4096]{2,1,0:T(8,128)(2,1)}, u32[]{:S(2)}) copy-start(bf16[1,128,4096]{2,1,0:T(8,128)(2,1)} %tokens_ref.1) | copy-start | bytes 3145732
  175.4 16.5 %copy-start.6 = (bf16[128,2048]{1,0:T(8,128)(2,1)S(1)}, bf16[128,2048]{1,0:T(8,128)(2,1)}, u32[]{:S(2)}) copy-start(bf16[128,2048]{1,0:T(8,128)(2,1)} %get-tuple-element.57) | copy-start | bytes 1572868
  175.4 16.5 %copy-start.7 = (bf16[128,2048]{1,0:T(8,128)(2,1)S(1)}, bf16[128,2048]{1,0:T(8,128)(2,1)}, u32[]{:S(2)}) copy-start(bf16[128,2048]{1,0:T(8,128)(2,1)} %get-tuple-element.58) | copy-start | bytes 1572868
  175.4 15.9 %collective-permute-start.12 = (bf16[128,2048]{1,0:T(8,128)(2,1)}, bf16[128,2048]{1,0:T(8,128)(2,1)S(1)}, u32[]{:S(2)}, u32[]{:S(2)}) collective-permute-start(bf16[128,2048]{1,0:T(8,128)(2,1)} %get-tuple-element.60), channel_id=1, source_target_pairs={{0,32},{32,64},{64,96},{96,0},{1,33},{33,65},{65,97},{97,1},{2,34}... | collective-permute-start | bytes 1572872 | tf_op jit(solution)/shard_map/sum_parts/ppermute | solution.py:20
  175.5 16.4 %collective-permute-start.11 = (bf16[128,2048]{1,0:T(8,128)(2,1)}, bf16[128,2048]{1,0:T(8,128)(2,1)S(1)}, u32[]{:S(2)}, u32[]{:S(2)}) collective-permute-start(bf16[128,2048]{1,0:T(8,128)(2,1)} %get-tuple-element.59), channel_id=1, source_target_pairs={{0,96},{32,0},{64,32},{96,64},{1,97},{33,1},{65,33},{97,65},{2,98}... | collective-permute-start | bytes 1572872 | tf_op jit(solution)/shard_map/sum_parts/ppermute | solution.py:20
  180.6 21.0 %collective-permute-start.16 = (bf16[128,2048]{1,0:T(8,128)(2,1)S(1)}, bf16[128,2048]{1,0:T(8,128)(2,1)S(1)}, u32[]{:S(2)}, u32[]{:S(2)}) collective-permute-start(bf16[128,2048]{1,0:T(8,128)(2,1)S(1)} %add_convert_fusion.1), channel_id=1, source_target_pairs={{0,96},{32,0},{64,32},{96,64},{1,97},{33,1},{65,33},{97,65},{2,98}... | collective-permute-start | bytes 1572872 | tf_op jit(solution)/shard_map/sum_parts/ppermute | solution.py:20
  181.9 19.7 %collective-permute-start.14 = (bf16[128,2048]{1,0:T(8,128)(2,1)S(1)}, bf16[128,2048]{1,0:T(8,128)(2,1)S(1)}, u32[]{:S(2)}, u32[]{:S(2)}) collective-permute-start(bf16[128,2048]{1,0:T(8,128)(2,1)S(1)} %add_convert_fusion.2), channel_id=1, source_target_pairs={{0,32},{32,64},{64,96},{96,0},{1,33},{33,65},{65,97},{97,1},{2,34}... | collective-permute-start | bytes 1572872 | tf_op jit(solution)/shard_map/sum_parts/ppermute | solution.py:20
  191.9 11.0 %copy-start.1 = (bf16[256,4096]{1,0:T(8,128)(2,1)S(1)}, bf16[256,4096]{1,0:T(8,128)(2,1)}, u32[]{:S(2)}) copy-start(bf16[256,4096]{1,0:T(8,128)(2,1)} %param.15) | copy-start | bytes 6291460
Sparse Core Ops, SparseCore 0:
  9.6 96.5 all-gather.4
  107.9 49.2 all-gather.6

commit v6 on v5

--- a/solution.py
+++ b/solution.py
@@ -257,30 +257,23 @@
 
 
 def out_kernel(seqs, order, own_ref, others_ref, w_ref, *refs):
-    outs, (w, rows, sums, row_sem, w_sems, out_sems) = refs[: 2 * len(seqs)], refs[2 * len(seqs) :]
+    outs, (w, rows, sums, row_sem, w_sem, out_sems) = refs[: 2 * len(seqs)], refs[2 * len(seqs) :]
     length, channels = own_ref.shape[2:]
-    tiles, _, _, cols = w.shape
+    half_width = w.shape[2] // 2
     for r in range(4):
         block = pl.ds(pl.multiple_of(order[r] * channels, channels), channels)
         for i, s in enumerate(seqs):
             source = own_ref.at[0, s] if r == 0 else others_ref.at[r - 1, s]
             copy(source, rows.at[pl.ds(i * length, length), block], row_sem)
-    for t in range(tiles):
-        copy(w_ref.at[:, :, pl.ds(t * cols, cols)], w.at[t], w_sems.at[t])
+    for r in range(4):
+        copy(w_ref.at[r], w.at[r], w_sem)
     wait_for(rows, row_sem)
+    wait_for(w, w_sem)
     for half in range(2):
-
-        def each_tile(i, carry, half=half):
-            t = half * (tiles // 2) + i
-            wait_for(w.at[t], w_sems.at[t])
-            total = dot(rows[...], w[t].reshape(rows.shape[1], cols)).astype(BF16)
-            for s in range(len(seqs)):
-                there = pl.ds(pl.multiple_of(i * cols, cols), cols)
-                sums[half, s, :, there] = total[s * length : (s + 1) * length]
-            return carry
-
-        lax.fori_loop(0, tiles // 2, each_tile, 0)
+        there = pl.ds(half * half_width, half_width)
+        total = dot(rows[...], w[:, :, there].reshape(rows.shape[1], half_width)).astype(BF16)
         for s in range(len(seqs)):
+            sums[half, s] = total[s * length : (s + 1) * length]
             copy(sums.at[half, s], outs[2 * s + half], out_sems.at[half])
     for half in range(2):
         wait_for(sums.at[half], out_sems.at[half])
@@ -378,18 +371,16 @@
 def project_out(order, seqs, own, others, w, name):
     length, channels = own.shape[2:]
     blocks, half = w.shape[0], w.shape[2] // 2
-    cols = 8 * channels
-    tiles = w.shape[2] // cols
     return pl.pallas_call(
         functools.partial(out_kernel, seqs),
         in_specs=[IN_SMEM] + [IN_PLACE] * 3,
         out_specs=[IN_PLACE] * (2 * len(seqs)),
         scratch_shapes=[
-            pltpu.VMEM((tiles, blocks, channels, cols), BF16),
+            pltpu.VMEM(w.shape, BF16),
             pltpu.VMEM((len(seqs) * length, blocks * channels), BF16),
             pltpu.VMEM((2, len(seqs), length, half), BF16),
             DMA,
-            DMA((tiles,)),
+            DMA,
             DMA((2,)),
         ],
         out_shape=[jax.ShapeDtypeStruct((length, half), BF16)] * (2 * len(seqs)),

time: 213 us -> 214 us (level)
  transfers between devices with their start and end apart: 19 -> 19, of which waited for: 12 -> 12; matrix products, arithmetic and copies ran while one was open for 3% -> 3% of each run, Pallas kernels for 34% -> 35%
where the time goes in v6:
time: 214 us; the launch traced here: 211 us
  Pallas kernels  79.3 us (37%)
  waiting for transfers between devices  75.4 us (35%)
  starting transfers between devices  30 us (14%)
  between operations  13.6 us (6%)
  other arithmetic  6.42 us (3%)
  local copies, waits for them, and re-layouts  6.07 us (3%)
    ppermute x13, waiting for transfers between devices, from_ahead(): lax.ppermute(value, axis, [(i, (i - steps) % count) for i in range(count)])  54.9 us
    pallas_call x2, Pallas kernels, keys_values(): pl.pallas_call(functools.partial(kv_kernel, first, seqs), in_specs=[IN_SM...  30.9 us
    all_gather x1, waiting for transfers between devices, shards(): lax.all_gather(share, ('z', 'y', 'c'), axis=0)  19.5 us
    ppermute x13, starting transfers between devices, from_ahead(): lax.ppermute(value, axis, [(i, (i - steps) % count) for i in range(count)])  19.4 us
    pallas_call x2, Pallas kernels, queries(): pl.pallas_call(functools.partial(q_kernel, first, seqs), in_specs=[IN_SME...  17.4 us
    pallas_call x2, Pallas kernels, project_out(): pl.pallas_call(functools.partial(out_kernel, seqs), in_specs=[IN_SMEM] +...  15.5 us
    ppermute x3, starting transfers between devices, from_behind(): lax.ppermute(value, axis, [(i, i + steps) for i in range(count - steps)])  8.87 us
    pallas_call x2, Pallas kernels, gate(): pl.pallas_call(gate_kernel, grid=(blocks, lanes), in_specs=[at(a, 0) for...  8.49 us
  transfers between devices with their start and end apart: 19, of which 12 were waited for; matrix products, arithmetic and copies ran while one was open for 3% of the time, Pallas kernels for 35%

profile of v6, /device:TPU:6, one launch (start us, length us, event | category | flops | bytes accessed | tf_op | source)
XLA Modules:
  0.0 210.9 jit_solution(17314124898025583383)
XLA Ops:
  6.5 2.2 %dynamic-slice_bitcast_fusion = bf16[3,512,256]{2,1,0:T(8,128)(2,1)} fusion(bf16[4096,3,256]{2,0,1:T(8,128)(2,1)} %param.10, s32[]{:T(128)S(6)} %select_n.45), kind=kLoop, calls=%fused_computation.6 | loop fusion | bytes 1572868 | tf_op jit(solution)/shard_map/gather_in_weights/dynamic_slice | solution.py:403
  9.8 1.7 collective-permute-start
  13.1 3.6 %norm.1.refs_0_ = bf16[144,4096]{1,0:T(8,128)(2,1)} custom-call(bf16[16,4096]{1,0:T(8,128)(2,1)} %copy-done.8, bf16[1,128,4096]{2,1,0:T(8,128)(2,1)} %tokens_ref.1, f32[1,4096]{1,0:T(1,128)} %bitcast.24), custom_call_target="tpu_custom_call" | custom-call | tf_op jit(solution)/shard_map/norm/norm/pallas_call | solution.py:409
  19.2 2.4 %collective-permute-start.2 = (bf16[144,4096]{1,0:T(8,128)(2,1)S(1)}, bf16[144,4096]{1,0:T(8,128)(2,1)}, u32[]{:S(2)}, u32[]{:S(2)}) collective-permute-start(bf16[144,4096]{1,0:T(8,128)(2,1)S(1)} %copy-done.2), channel_id=1, source_target_pairs={{0,32},{32,64},{64,96},{96,0},{1,33},{33,65},{65,97},{97,1},{2,34}... | collective-permute-start | bytes 3538952 | tf_op jit(solution)/shard_map/gather_tokens/ppermute | solution.py:20
  21.8 1.4 pack.1.p0
  23.2 4.0 %collective-permute-start.4 = (f32[48,256]{1,0:T(8,128)}, f32[48,256]{1,0:T(8,128)S(1)}, u32[]{:S(2)}, u32[]{:S(2)}) collective-permute-start(f32[48,256]{1,0:T(8,128)} %pack.1.p0), channel_id=1, source_target_pairs={{0,24},{8,0},{16,8},{24,16},{1,25},{9,1},{17,9},{25,17},{2,26},{10... | collective-permute-start | bytes 147464 | tf_op jit(solution)/shard_map/coefficients/ppermute | solution.py:20
  27.2 2.5 %collective-permute-done.4.p1 = f32[48,256]{1,0:T(8,128)S(1)} collective-permute-done((f32[48,256]{1,0:T(8,128)}, f32[48,256]{1,0:T(8,128)S(1)}, u32[]{:S(2)}, u32[]{:S(2)}) %collective-permute-start.4) | collective-permute-done | bytes 49184 | tf_op jit(solution)/shard_map/coefficients/ppermute | solution.py:20
  29.7 2.8 %collective-permute-start.6 = (f32[48,256]{1,0:T(8,128)}, f32[48,256]{1,0:T(8,128)S(1)}, u32[]{:S(2)}, u32[]{:S(2)}) collective-permute-start(f32[48,256]{1,0:T(8,128)} %pack.1.p0), channel_id=1, source_target_pairs={{0,16},{8,24},{16,0},{24,8},{1,17},{9,25},{17,1},{25,9},{2,18},{10... | collective-permute-start | bytes 147464 | tf_op jit(solution)/shard_map/coefficients/ppermute | solution.py:20
  34.0 2.8 %collective-permute-done.6.p3 = f32[48,256]{1,0:T(8,128)S(1)} collective-permute-done((f32[48,256]{1,0:T(8,128)}, f32[48,256]{1,0:T(8,128)S(1)}, u32[]{:S(2)}, u32[]{:S(2)}) %collective-permute-start.6) | collective-permute-done | bytes 49184 | tf_op jit(solution)/shard_map/coefficients/ppermute | solution.py:20
  37.5 2.2 %coefficients.1 = (f32[4,2,16,128]{3,2,1,0:T(8,128)}, f32[4,2,16,128]{3,2,1,0:T(8,128)}, f32[4,2,16,128]{3,2,1,0:T(8,128)}, f32[4,2,3,16,128]{4,3,2,1,0:T(8,128)...) custom-call(f32[48,256]{1,0:T(8,128)} %pack.1.p0, f32[48,256]{1,0:T(8,128)} %copy-done.10, ...), custom_call_target="tpu_custom_call" | custom-call | tf_op jit(solution)/shard_map/coefficients/coefficients/pallas_call | solution.py:430
  39.7 9.2 %collective-permute-done.1.refs_1_ = bf16[144,4096]{1,0:T(8,128)(2,1)S(1)} collective-permute-done((bf16[144,4096]{1,0:T(8,128)(2,1)S(1)}, bf16[144,4096]{1,0:T(8,128)(2,1)S(1)}, u32[]{:S(2)}, u32[]{:S(2)}) %collective-permute-start.1) | collective-permute-done | bytes 1179680 | tf_op jit(solution)/shard_map/gather_tokens/ppermute | solution.py:20
  48.9 20.8 %collective-permute-done.3.refs_3_ = bf16[144,4096]{1,0:T(8,128)(2,1)} collective-permute-done((bf16[144,4096]{1,0:T(8,128)(2,1)S(1)}, bf16[144,4096]{1,0:T(8,128)(2,1)}, u32[]{:S(2)}, u32[]{:S(2)}) %collective-permute-start.3) | collective-permute-done | bytes 1179680 | tf_op jit(solution)/shard_map/gather_tokens/ppermute | solution.py:20
  69.6 6.6 %own_queries.1.q_ref = bf16[1,2,4,8,16,128]{5,4,3,2,1,0:T(8,128)(2,1)} custom-call(s32[4]{0:T(128)} %pad_add_fusion.order, bf16[3,4096,256]{2,1,0:T(8,128)(2,1)} %bitcast.22, bf16[144,4096]{1,0:T(8,128)(2,1)} %norm.1.refs_0_, bf16[144,4096]{1,0:T(8,128)(2,1)} %copy-done.3, bf16[144,4096]{1,0:T(8,128)(2,1)} %collective-permute-done.2.refs_2_, ...), custom_call_target="tpu_custom_call" | custom-call | tf_op jit(solution)/shard_map/own_queries/pallas_call | solution.py:336
  76.2 10.4 %own_keys_values.1 = (bf16[1,2,4,8,16,128]{5,4,3,2,1,0:T(8,128)(2,1)}, bf16[1,2,4,8,16,128]{5,4,3,2,1,0:T(8,128)(2,1)}, f32[1,2,4,16,128]{4,3,2,1,0:T(8,128)}) custom-call(s32[4]{0:T(128)} %pad_add_fusion.order, bf16[3,4096,256]{2,1,0:T(8,128)(2,1)} %bitcast.23, bf16[144,4096]{1,0:T(8,128)(2,1)} %norm.1.refs_0_, bf16[144,4096]{1,0:T(8,128)(2,1)} %copy-done.3, ...), custom_call_target="tpu_custom_call" | custom-call | tf_op jit(solution)/shard_map/own_keys_values/pallas_call | solution.py:307
  86.7 19.5 %all-gather.5.cloned.1.call-done = bf16[96,512,256]{2,1,0:T(8,128)(2,1)} async-done(((bf16[3,512,256]{2,1,0:T(8,128)(2,1)}), bf16[96,512,256]{2,1,0:T(8,128)(2,1)}) %all-gather.5.cloned.1.call-update) | async-done | bytes 25165840 | tf_op jit(solution)/shard_map/gather_in_weights/all_gather | solution.py:404
  106.2 20.4 %keys_values.1 = (bf16[3,2,4,8,16,128]{5,4,3,2,1,0:T(8,128)(2,1)}, bf16[3,2,4,8,16,128]{5,4,3,2,1,0:T(8,128)(2,1)}, f32[3,2,4,16,128]{4,3,2,1,0:T(8,128)}) custom-call(s32[4]{0:T(128)} %pad_add_fusion.order, bf16[4,8,3,512,256]{4,3,2,1,0:T(8,128)(2,1)} %bitcast.18, bf16[144,4096]{1,0:T(8,128)(2,1)} %norm.1.refs_0_, bf16[144,4096]{1,0:T(8,128)(2,1)} %copy-done.3, ...), custom_call_target="tpu_custom_call" | custom-call | tf_op jit(solution)/shard_map/keys_values/pallas_call | solution.py:307
  129.2 4.6 %collective-permute-start.10 = (bf16[4,2,4,16,128]{4,3,2,1,0:T(8,128)(2,1)S(1)}, bf16[4,2,4,16,128]{4,3,2,1,0:T(8,128)(2,1)S(1)}, u32[]{:S(2)}, u32[]{:S(2)}) collective-permute-start(bf16[4,2,4,16,128]{4,3,2,1,0:T(8,128)(2,1)S(1)} %fusion.3), channel_id=1, source_target_pairs={{0,6},{1,7},{8,14},{9,15},{16,22},{17,23},{24,30},{25,31},{32,38},... | collective-permute-start | bytes 393224 | tf_op jit(solution)/shard_map/states/ppermute | solution.py:25
  133.8 1.3 collective-permute-start.9
  135.1 2.9 %collective-permute-start.8 = (bf16[4,2,4,16,128]{4,3,2,1,0:T(8,128)(2,1)S(1)}, bf16[4,2,4,16,128]{4,3,2,1,0:T(8,128)(2,1)S(1)}, u32[]{:S(2)}, u32[]{:S(2)}) collective-permute-start(bf16[4,2,4,16,128]{4,3,2,1,0:T(8,128)(2,1)S(1)} %fusion.3), channel_id=1, source_target_pairs={{0,2},{2,4},{4,6},{1,3},{3,5},{5,7},{8,10},{10,12},{12,14},{9,11},... | collective-permute-start | bytes 393224 | tf_op jit(solution)/shard_map/states/ppermute | solution.py:25
  138.1 10.7 %queries.1.q_ref = bf16[3,2,4,8,16,128]{5,4,3,2,1,0:T(8,128)(2,1)} custom-call(s32[4]{0:T(128)} %pad_add_fusion.order, bf16[4,8,3,512,256]{4,3,2,1,0:T(8,128)(2,1)} %bitcast.19, bf16[144,4096]{1,0:T(8,128)(2,1)} %norm.1.refs_0_, bf16[144,4096]{1,0:T(8,128)(2,1)} %copy-done.3, bf16[144,4096]{1,0:T(8,128)(2,1)} %collective-permute-done.2.refs_2_, ...), custom_call_target="tpu_custom_call" | custom-call | tf_op jit(solution)/shard_map/queries/pallas_call | solution.py:336
  149.7 2.6 %own_gate.1.own_ref = bf16[1,4,128,256]{3,2,1,0:T(8,128)(2,1)} custom-call(bf16[1,2,4,8,16,128]{5,4,3,2,1,0:T(8,128)(2,1)} %get-tuple-element.42.y_ref, bf16[1,2,4,8,16,128]{5,4,3,2,1,0:T(8,128)(2,1)} %get-tuple-element.43.e_ref, bf16[1,2,4,8,16,128]{5,4,3,2,1,0:T(8,128)(2,1)} %own_queries.1.q_ref, f32[4,2,4,16,128]{4,3,2,1,0:T(8,128)} %add_select_fusion.in_ref, ...), custom_call_target="tpu_custom_call" | custom-call | tf_op jit(solution)/shard_map/own_gate/pallas_call | solution.py:359
  152.3 5.9 %gate.1.others_ref = bf16[3,4,128,256]{3,2,1,0:T(8,128)(2,1)} custom-call(bf16[3,2,4,8,16,128]{5,4,3,2,1,0:T(8,128)(2,1)} %get-tuple-element.51.y_ref, bf16[3,2,4,8,16,128]{5,4,3,2,1,0:T(8,128)(2,1)} %get-tuple-element.52.e_ref, bf16[3,2,4,8,16,128]{5,4,3,2,1,0:T(8,128)(2,1)} %queries.1.q_ref, f32[4,2,4,16,128]{4,3,2,1,0:T(8,128)} %add_select_fusion.in_ref, ...), custom_call_target="tpu_custom_call" | custom-call | tf_op jit(solution)/shard_map/gate/pallas_call | solution.py:359
  158.2 6.3 %project_far.1 = (bf16[128,2048]{1,0:T(8,128)(2,1)}, bf16[128,2048]{1,0:T(8,128)(2,1)}) custom-call(s32[4]{0:T(128)} %pad_add_fusion.order, bf16[1,4,128,256]{3,2,1,0:T(8,128)(2,1)} %own_gate.1.own_ref, bf16[3,4,128,256]{3,2,1,0:T(8,128)(2,1)} %gate.1.others_ref, bf16[4,256,4096]{2,1,0:T(8,128)(2,1)} %bitcast.20), custom_call_target="tpu_custom_call" | custom-call | tf_op jit(solution)/shard_map/project_far/pallas_call | solution.py:374
  165.5 2.4 %collective-permute-start.13 = (bf16[128,2048]{1,0:T(8,128)(2,1)}, bf16[128,2048]{1,0:T(8,128)(2,1)S(1)}, u32[]{:S(2)}, u32[]{:S(2)}) collective-permute-start(bf16[128,2048]{1,0:T(8,128)(2,1)} %get-tuple-element.62), channel_id=1, source_target_pairs={{0,32},{32,64},{64,96},{96,0},{1,33},{33,65},{65,97},{97,1},{2,34}... | collective-permute-start | bytes 1572872 | tf_op jit(solution)/shard_map/sum_parts/ppermute | solution.py:20
  167.8 9.1 %project_out.1 = (bf16[128,2048]{1,0:T(8,128)(2,1)}, bf16[128,2048]{1,0:T(8,128)(2,1)}, bf16[128,2048]{1,0:T(8,128)(2,1)}, bf16[128,2048]{1,0:T(8,128)(2,1)}, bf...) custom-call(s32[4]{0:T(128)} %pad_add_fusion.order, bf16[1,4,128,256]{3,2,1,0:T(8,128)(2,1)} %own_gate.1.own_ref, ...), custom_call_target="tpu_custom_call" | custom-call | tf_op jit(solution)/shard_map/project_out/pallas_call | solution.py:374
  177.1 2.0 collective-permute-start.11
  180.9 1.2 add_convert_fusion.2
  182.1 3.3 %collective-permute-start.14 = (bf16[128,2048]{1,0:T(8,128)(2,1)S(1)}, bf16[128,2048]{1,0:T(8,128)(2,1)S(1)}, u32[]{:S(2)}, u32[]{:S(2)}) collective-permute-start(bf16[128,2048]{1,0:T(8,128)(2,1)S(1)} %add_convert_fusion.2), channel_id=1, source_target_pairs={{0,32},{32,64},{64,96},{96,0},{1,33},{33,65},{65,97},{97,1},{2,34}... | collective-permute-start | bytes 1572872 | tf_op jit(solution)/shard_map/sum_parts/ppermute | solution.py:20
  185.4 6.8 %collective-permute-done.12 = bf16[128,2048]{1,0:T(8,128)(2,1)S(1)} collective-permute-done((bf16[128,2048]{1,0:T(8,128)(2,1)}, bf16[128,2048]{1,0:T(8,128)(2,1)S(1)}, u32[]{:S(2)}, u32[]{:S(2)}) %collective-permute-start.12) | collective-permute-done | bytes 524320 | tf_op jit(solution)/shard_map/sum_parts/ppermute | solution.py:20
  192.2 1.3 collective-permute-done.11
  193.9 9.0 %collective-permute-done.16 = bf16[128,2048]{1,0:T(8,128)(2,1)S(1)} collective-permute-done((bf16[128,2048]{1,0:T(8,128)(2,1)S(1)}, bf16[128,2048]{1,0:T(8,128)(2,1)S(1)}, u32[]{:S(2)}, u32[]{:S(2)}) %collective-permute-start.16) | collective-permute-done | bytes 524320 | tf_op jit(solution)/shard_map/sum_parts/ppermute | solution.py:20
  202.9 1.2 fusion.1
  (59 shorter events, 14.0 us)
Async XLA Ops:
  6.5 10.2 %copy-start = (bf16[256,4096]{1,0:T(8,128)(2,1)S(1)}, bf16[256,4096]{1,0:T(8,128)(2,1)}, u32[]{:S(2)}) copy-start(bf16[256,4096]{1,0:T(8,128)(2,1)} %param.15) | copy-start | bytes 6291460
  6.5 99.7 %all-gather.5.cloned.1.call-start = ((), (), s32[]{:S(2)}) async-start(), calls=%async_computation | async-start | bytes 25952256 | tf_op jit(solution)/shard_map/gather_in_weights/all_gather | solution.py:404
  8.8 149.4 %all-gather.7.cloned.1.call-start = ((), (), s32[]{:S(2)}) async-start(), calls=%async_computation.1 | async-start | bytes 9437184 | tf_op jit(solution)/shard_map/gather_out_weights/all_gather | solution.py:423
  9.8 2.7 %collective-permute-start = (bf16[16,4096]{1,0:T(8,128)(2,1)S(1)}, bf16[16,4096]{1,0:T(8,128)(2,1)S(1)}, u32[]{:S(2)}, u32[]{:S(2)}) collective-permute-start(bf16[16,4096]{1,0:T(8,128)(2,1)S(1)} %slice_bitcast_fusion), channel_id=1, source_target_pairs={{0,1},{1,2},{2,3},{3,4},{4,5},{5,6},{6,7},{8,9},{9,10},{10,11},{11... | collective-permute-start | bytes 393224 | tf_op jit(solution)/shard_map/norm/ppermute | solution.py:408
  12.5 0.7 copy-start.8
  16.7 1.6 copy-start.2
  18.4 30.5 %collective-permute-start.1 = (bf16[144,4096]{1,0:T(8,128)(2,1)S(1)}, bf16[144,4096]{1,0:T(8,128)(2,1)S(1)}, u32[]{:S(2)}, u32[]{:S(2)}) collective-permute-start(bf16[144,4096]{1,0:T(8,128)(2,1)S(1)} %copy-done.2), channel_id=1, source_target_pairs={{0,96},{32,0},{64,32},{96,64},{1,97},{33,1},{65,33},{97,65},{2,98}... | collective-permute-start | bytes 3538952 | tf_op jit(solution)/shard_map/gather_tokens/ppermute | solution.py:20
  19.2 29.7 %collective-permute-start.2 = (bf16[144,4096]{1,0:T(8,128)(2,1)S(1)}, bf16[144,4096]{1,0:T(8,128)(2,1)}, u32[]{:S(2)}, u32[]{:S(2)}) collective-permute-start(bf16[144,4096]{1,0:T(8,128)(2,1)S(1)} %copy-done.2), channel_id=1, source_target_pairs={{0,32},{32,64},{64,96},{96,0},{1,33},{33,65},{65,97},{97,1},{2,34}... | collective-permute-start | bytes 3538952 | tf_op jit(solution)/shard_map/gather_tokens/ppermute | solution.py:20
  21.6 48.0 %collective-permute-start.3 = (bf16[144,4096]{1,0:T(8,128)(2,1)S(1)}, bf16[144,4096]{1,0:T(8,128)(2,1)}, u32[]{:S(2)}, u32[]{:S(2)}) collective-permute-start(bf16[144,4096]{1,0:T(8,128)(2,1)S(1)} %copy-done.2), channel_id=1, source_target_pairs={{0,64},{32,96},{64,0},{96,32},{1,65},{33,97},{65,1},{97,33},{2,66}... | collective-permute-start | bytes 3538952 | tf_op jit(solution)/shard_map/gather_tokens/ppermute | solution.py:20
  23.2 6.5 %collective-permute-start.4 = (f32[48,256]{1,0:T(8,128)}, f32[48,256]{1,0:T(8,128)S(1)}, u32[]{:S(2)}, u32[]{:S(2)}) collective-permute-start(f32[48,256]{1,0:T(8,128)} %pack.1.p0), channel_id=1, source_target_pairs={{0,24},{8,0},{16,8},{24,16},{1,25},{9,1},{17,9},{25,17},{2,26},{10... | collective-permute-start | bytes 147464 | tf_op jit(solution)/shard_map/coefficients/ppermute | solution.py:20
  27.2 6.8 %collective-permute-start.5 = (f32[48,256]{1,0:T(8,128)}, f32[48,256]{1,0:T(8,128)S(1)}, u32[]{:S(2)}, u32[]{:S(2)}) collective-permute-start(f32[48,256]{1,0:T(8,128)} %pack.1.p0), channel_id=1, source_target_pairs={{0,8},{8,16},{16,24},{24,0},{1,9},{9,17},{17,25},{25,1},{2,10},{10... | collective-permute-start | bytes 147464 | tf_op jit(solution)/shard_map/coefficients/ppermute | solution.py:20
  29.7 7.2 %copy-start.10 = (f32[48,256]{1,0:T(8,128)}, f32[48,256]{1,0:T(8,128)S(1)}, u32[]{:S(2)}) copy-start(f32[48,256]{1,0:T(8,128)S(1)} %collective-permute-done.4.p1) | copy-start | bytes 147460
  29.7 7.2 %collective-permute-start.6 = (f32[48,256]{1,0:T(8,128)}, f32[48,256]{1,0:T(8,128)S(1)}, u32[]{:S(2)}, u32[]{:S(2)}) collective-permute-start(f32[48,256]{1,0:T(8,128)} %pack.1.p0), channel_id=1, source_target_pairs={{0,16},{8,24},{16,0},{24,8},{1,17},{9,25},{17,1},{25,9},{2,18},{10... | collective-permute-start | bytes 147464 | tf_op jit(solution)/shard_map/coefficients/ppermute | solution.py:20
  34.0 2.8 %copy-start.11 = (f32[48,256]{1,0:T(8,128)}, f32[48,256]{1,0:T(8,128)S(1)}, u32[]{:S(2)}) copy-start(f32[48,256]{1,0:T(8,128)S(1)} %collective-permute-done.5.p2) | copy-start | bytes 147460
  36.9 0.6 copy-start.12
  48.9 20.8 %copy-start.3 = (bf16[144,4096]{1,0:T(8,128)(2,1)}, bf16[144,4096]{1,0:T(8,128)(2,1)S(1)}, u32[]{:S(2)}) copy-start(bf16[144,4096]{1,0:T(8,128)(2,1)S(1)} %collective-permute-done.1.refs_1_) | copy-start | bytes 3538948
  106.2 21.4 %copy-start.9 = (f32[1,2,4,16,128]{4,3,2,1,0:T(8,128)S(1)}, f32[1,2,4,16,128]{4,3,2,1,0:T(8,128)}, u32[]{:S(2)}) copy-start(f32[1,2,4,16,128]{4,3,2,1,0:T(8,128)} %get-tuple-element.46) | copy-start | bytes 196612
  106.2 22.9 %copy-start.5 = (f32[4,2,16,128]{3,2,1,0:T(8,128)S(1)}, f32[4,2,16,128]{3,2,1,0:T(8,128)}, u32[]{:S(2)}) copy-start(f32[4,2,16,128]{3,2,1,0:T(8,128)} %get-tuple-element.45) | copy-start | bytes 196612
  127.7 1.5 collective-permute-start.7
  129.2 19.7 %collective-permute-start.10 = (bf16[4,2,4,16,128]{4,3,2,1,0:T(8,128)(2,1)S(1)}, bf16[4,2,4,16,128]{4,3,2,1,0:T(8,128)(2,1)S(1)}, u32[]{:S(2)}, u32[]{:S(2)}) collective-permute-start(bf16[4,2,4,16,128]{4,3,2,1,0:T(8,128)(2,1)S(1)} %fusion.3), channel_id=1, source_target_pairs={{0,6},{1,7},{8,14},{9,15},{16,22},{17,23},{24,30},{25,31},{32,38},... | collective-permute-start | bytes 393224 | tf_op jit(solution)/shard_map/states/ppermute | solution.py:25
  133.8 15.0 %collective-permute-start.9 = (bf16[4,2,4,16,128]{4,3,2,1,0:T(8,128)(2,1)S(1)}, bf16[4,2,4,16,128]{4,3,2,1,0:T(8,128)(2,1)S(1)}, u32[]{:S(2)}, u32[]{:S(2)}) collective-permute-start(bf16[4,2,4,16,128]{4,3,2,1,0:T(8,128)(2,1)S(1)} %fusion.3), channel_id=1, source_target_pairs={{0,4},{2,6},{1,5},{3,7},{8,12},{10,14},{9,13},{11,15},{16,20},{18,... | collective-permute-start | bytes 393224 | tf_op jit(solution)/shard_map/states/ppermute | solution.py:25
  135.1 13.7 %collective-permute-start.8 = (bf16[4,2,4,16,128]{4,3,2,1,0:T(8,128)(2,1)S(1)}, bf16[4,2,4,16,128]{4,3,2,1,0:T(8,128)(2,1)S(1)}, u32[]{:S(2)}, u32[]{:S(2)}) collective-permute-start(bf16[4,2,4,16,128]{4,3,2,1,0:T(8,128)(2,1)S(1)} %fusion.3), channel_id=1, source_target_pairs={{0,2},{2,4},{4,6},{1,3},{3,5},{5,7},{8,10},{10,12},{12,14},{9,11},... | collective-permute-start | bytes 393224 | tf_op jit(solution)/shard_map/states/ppermute | solution.py:25
  164.5 15.1 %collective-permute-start.15 = (bf16[128,2048]{1,0:T(8,128)(2,1)}, bf16[128,2048]{1,0:T(8,128)(2,1)S(1)}, u32[]{:S(2)}, u32[]{:S(2)}) collective-permute-start(bf16[128,2048]{1,0:T(8,128)(2,1)} %get-tuple-element.64), channel_id=1, source_target_pairs={{0,96},{32,0},{64,32},{96,64},{1,97},{33,1},{65,33},{97,65},{2,98}... | collective-permute-start | bytes 1572872 | tf_op jit(solution)/shard_map/sum_parts/ppermute | solution.py:20
  165.5 15.4 %collective-permute-start.13 = (bf16[128,2048]{1,0:T(8,128)(2,1)}, bf16[128,2048]{1,0:T(8,128)(2,1)S(1)}, u32[]{:S(2)}, u32[]{:S(2)}) collective-permute-start(bf16[128,2048]{1,0:T(8,128)(2,1)} %get-tuple-element.62), channel_id=1, source_target_pairs={{0,32},{32,64},{64,96},{96,0},{1,33},{33,65},{65,97},{97,1},{2,34}... | collective-permute-start | bytes 1572872 | tf_op jit(solution)/shard_map/sum_parts/ppermute | solution.py:20
  177.0 16.5 %copy-start.4 = (bf16[1,128,4096]{2,1,0:T(8,128)(2,1)S(1)}, bf16[1,128,4096]{2,1,0:T(8,128)(2,1)}, u32[]{:S(2)}) copy-start(bf16[1,128,4096]{2,1,0:T(8,128)(2,1)} %tokens_ref.1) | copy-start | bytes 3145732
  177.0 16.5 %copy-start.6 = (bf16[128,2048]{1,0:T(8,128)(2,1)S(1)}, bf16[128,2048]{1,0:T(8,128)(2,1)}, u32[]{:S(2)}) copy-start(bf16[128,2048]{1,0:T(8,128)(2,1)} %get-tuple-element.57) | copy-start | bytes 1572868
  177.0 16.5 %copy-start.7 = (bf16[128,2048]{1,0:T(8,128)(2,1)S(1)}, bf16[128,2048]{1,0:T(8,128)(2,1)}, u32[]{:S(2)}) copy-start(bf16[128,2048]{1,0:T(8,128)(2,1)} %get-tuple-element.58) | copy-start | bytes 1572868
  177.0 15.1 %collective-permute-start.12 = (bf16[128,2048]{1,0:T(8,128)(2,1)}, bf16[128,2048]{1,0:T(8,128)(2,1)S(1)}, u32[]{:S(2)}, u32[]{:S(2)}) collective-permute-start(bf16[128,2048]{1,0:T(8,128)(2,1)} %get-tuple-element.60), channel_id=1, source_target_pairs={{0,32},{32,64},{64,96},{96,0},{1,33},{33,65},{65,97},{97,1},{2,34}... | collective-permute-start | bytes 1572872 | tf_op jit(solution)/shard_map/sum_parts/ppermute | solution.py:20
  177.1 16.4 %collective-permute-start.11 = (bf16[128,2048]{1,0:T(8,128)(2,1)}, bf16[128,2048]{1,0:T(8,128)(2,1)S(1)}, u32[]{:S(2)}, u32[]{:S(2)}) collective-permute-start(bf16[128,2048]{1,0:T(8,128)(2,1)} %get-tuple-element.59), channel_id=1, source_target_pairs={{0,96},{32,0},{64,32},{96,64},{1,97},{33,1},{65,33},{97,65},{2,98}... | collective-permute-start | bytes 1572872 | tf_op jit(solution)/shard_map/sum_parts/ppermute | solution.py:20
  180.8 22.1 %collective-permute-start.16 = (bf16[128,2048]{1,0:T(8,128)(2,1)S(1)}, bf16[128,2048]{1,0:T(8,128)(2,1)S(1)}, u32[]{:S(2)}, u32[]{:S(2)}) collective-permute-start(bf16[128,2048]{1,0:T(8,128)(2,1)S(1)} %add_convert_fusion.1), channel_id=1, source_target_pairs={{0,96},{32,0},{64,32},{96,64},{1,97},{33,1},{65,33},{97,65},{2,98}... | collective-permute-start | bytes 1572872 | tf_op jit(solution)/shard_map/sum_parts/ppermute | solution.py:20
  182.1 20.8 %collective-permute-start.14 = (bf16[128,2048]{1,0:T(8,128)(2,1)S(1)}, bf16[128,2048]{1,0:T(8,128)(2,1)S(1)}, u32[]{:S(2)}, u32[]{:S(2)}) collective-permute-start(bf16[128,2048]{1,0:T(8,128)(2,1)S(1)} %add_convert_fusion.2), channel_id=1, source_target_pairs={{0,32},{32,64},{64,96},{96,0},{1,33},{33,65},{65,97},{97,1},{2,34}... | collective-permute-start | bytes 1572872 | tf_op jit(solution)/shard_map/sum_parts/ppermute | solution.py:20
  193.5 10.6 %copy-start.1 = (bf16[256,4096]{1,0:T(8,128)(2,1)S(1)}, bf16[256,4096]{1,0:T(8,128)(2,1)}, u32[]{:S(2)}) copy-start(bf16[256,4096]{1,0:T(8,128)(2,1)} %param.15) | copy-start | bytes 6291460
Sparse Core Ops, SparseCore 0:
  9.6 96.5 all-gather.4
  107.9 49.2 all-gather.6
